TPU v7x, 32 devices: a whole 2x2x4 slice. The times are simulated.
32 devices in a mesh: dp: 4 (over z), gx: 2 (over x), gy: 4 (over y, core).
Axes of the slice: x: 2, y: 2, z: 4, core: 2. Of those that a mesh axis runs over, the one named last changes fastest.
Arguments:
- fields: bfloat16 [4, 20, 32, 16384], P('dp', None, None, ('gx', 'gy')), may hold values from -6 to 6
- cotangent: bfloat16 [4, 20, 32, 16384], P('dp', None, None, ('gx', 'gy')), may hold values from -6 to 6
- mix_weight: bfloat16 [20, 20], replicated, may hold values from -1.25 to 1.25
- spectral_weight: bfloat16 [288, 2, 20, 20], P(('gx', 'gy')), may hold values from -1 to 1
Outputs:
- output: bfloat16 [4, 20, 32, 16384], P('dp', None, None, ('gx', 'gy'))
- spectral_grad: float32 [288, 2, 20, 20], P(('gx', 'gy'))
- mixing_grad: float32 [20, 20], replicated
All inputs are finite; a program needn't handle non-finite values.
Results may differ from a plain program's by a relative error of at most 0.0031.
Values may be sent and summed in bfloat16 or wider, within the bound.
No kernel may reach another device: no remote copies, remote signals or barrier semaphores. Data moves between devices by JAX's collectives and lax.ppermute only.
A program may use at most 128 MiB of HBM per device.

v0:
```python
import math

import jax
import jax.numpy as jnp
from jax import lax
from jax.sharding import PartitionSpec as P

NX = 128
NY = 128
KX = 24
KY = 12
P_SIZE = 32
MODES = 288


HI = lax.Precision.HIGHEST


def gelu_value(h):
    k = math.sqrt(2.0 / math.pi)
    t = jnp.tanh(k * (h + 0.044715 * h * h * h))
    return 0.5 * h * (1.0 + t)


def gelu_slope(h):
    k = math.sqrt(2.0 / math.pi)
    t = jnp.tanh(k * (h + 0.044715 * h * h * h))
    return 0.5 * (1.0 + t) + 0.5 * h * (1.0 - t * t) * k * (1.0 + 3.0 * 0.044715 * h * h)


def axis_table(waves, n):
    cells = jnp.arange(n, dtype=jnp.int32)
    angle = 2.0 * math.pi / n * (waves[:, None] * cells[None, :] % n).astype(jnp.float32)
    return (jnp.cos(angle), jnp.sin(angle))


def tables():
    index = jnp.arange(KX, dtype=jnp.int32)
    waves_x = jnp.where(index < KX // 2, index, NX - KX + index)
    cos_x, sin_x = axis_table(waves_x, NX)
    cos_y, sin_y = axis_table(jnp.arange(KY, dtype=jnp.int32), NY)
    return (cos_x, sin_x, cos_y, sin_y)


def forward_dft(data, scale):
    cos_x, sin_x, cos_y, sin_y = tables()
    a_re = jnp.einsum("cpxy,ky->cpxk", data, cos_y, precision=HI)
    a_im = -jnp.einsum("cpxy,ky->cpxk", data, sin_y, precision=HI)
    s_re = jnp.einsum("cpxk,jx->jkcp", a_re, cos_x, precision=HI) + jnp.einsum(
        "cpxk,jx->jkcp", a_im, sin_x, precision=HI
    )
    s_im = jnp.einsum("cpxk,jx->jkcp", a_im, cos_x, precision=HI) - jnp.einsum(
        "cpxk,jx->jkcp", a_re, sin_x, precision=HI
    )
    chans, planes = (data.shape[0], data.shape[1])
    return scale * jnp.stack(
        [s_re.reshape(MODES, chans, planes), s_im.reshape(MODES, chans, planes)], axis=1
    )


def inverse_dft(vals, scale):
    cos_x, sin_x, cos_y, sin_y = tables()
    chans, planes = (vals.shape[2], vals.shape[3])
    v_re = vals[:, 0].reshape(KX, KY, chans, planes)
    v_im = vals[:, 1].reshape(KX, KY, chans, planes)
    b_re = jnp.einsum("jkdp,jx->dpxk", v_re, cos_x, precision=HI) - jnp.einsum(
        "jkdp,jx->dpxk", v_im, sin_x, precision=HI
    )
    b_im = jnp.einsum("jkdp,jx->dpxk", v_re, sin_x, precision=HI) + jnp.einsum(
        "jkdp,jx->dpxk", v_im, cos_x, precision=HI
    )
    return scale * (
        jnp.einsum("dpxk,ky->dpxy", b_re, cos_y, precision=HI)
        - jnp.einsum("dpxk,ky->dpxy", b_im, sin_y, precision=HI)
    )


def spectral_mix(spec, weight):
    w = weight.astype(jnp.float32)
    v_re = jnp.einsum("mcp,mcd->mdp", spec[:, 0], w[:, 0], precision=HI) - jnp.einsum(
        "mcp,mcd->mdp", spec[:, 1], w[:, 1], precision=HI
    )
    v_im = jnp.einsum("mcp,mcd->mdp", spec[:, 0], w[:, 1], precision=HI) + jnp.einsum(
        "mcp,mcd->mdp", spec[:, 1], w[:, 0], precision=HI
    )
    return jnp.stack([v_re, v_im], axis=1)


def grads_of(spec, gspec):
    g_re = jnp.einsum("mcp,mdp->mcd", spec[:, 0], gspec[:, 0], precision=HI) + jnp.einsum(
        "mcp,mdp->mcd", spec[:, 1], gspec[:, 1], precision=HI
    )
    g_im = jnp.einsum("mcp,mdp->mcd", spec[:, 0], gspec[:, 1], precision=HI) - jnp.einsum(
        "mcp,mdp->mcd", spec[:, 1], gspec[:, 0], precision=HI
    )
    return jnp.stack([g_re, g_im], axis=1)


def to_planes(block):
    chans, planes, rows_x, full_y = block.shape
    size_x = lax.axis_size("gx")
    size_y = lax.axis_size("gy")
    moved = lax.all_to_all(
        lax.all_to_all(block, "gx", split_axis=1, concat_axis=2, tiled=True),
        "gy",
        split_axis=1,
        concat_axis=2,
        tiled=True,
    )
    own = moved.shape[1]
    moved = moved.reshape(chans, own, size_y, size_x, rows_x, full_y)
    moved = jnp.transpose(moved, (0, 1, 3, 2, 4, 5))
    return moved.reshape(chans, own, size_x * size_y * rows_x, full_y)


def to_cells(plane_block):
    chans, own, full_x, full_y = plane_block.shape
    size_x = lax.axis_size("gx")
    size_y = lax.axis_size("gy")
    rows_x = full_x // (size_x * size_y)
    moved = lax.all_to_all(
        lax.all_to_all(plane_block, "gx", split_axis=2, concat_axis=1, tiled=True),
        "gy",
        split_axis=2,
        concat_axis=1,
        tiled=True,
    )
    moved = moved.reshape(chans, size_y, size_x, own, rows_x, full_y)
    moved = jnp.transpose(moved, (0, 2, 1, 3, 4, 5))
    return moved.reshape(chans, size_x * size_y * own, rows_x, full_y)


def local(fields, cotangent, mix_weight, spectral_weight):
    flat = fields[0]
    grad_out = cotangent[0].astype(jnp.float32)
    chans, planes, cells = flat.shape
    rows_x = cells // NY
    norm_in = 1.0 / math.sqrt(NX * NY)
    norm_out = 1.0 / math.sqrt(MODES)
    samples = lax.axis_size("dp")
    mixed = jnp.einsum("cpq,cd->dpq", flat, mix_weight, preferred_element_type=jnp.float32)
    plane_field = to_planes(flat.reshape(chans, planes, rows_x, NY)).astype(jnp.float32)
    spec = forward_dft(plane_field, norm_in)
    full_weight = lax.all_gather(spectral_weight, ("gx", "gy"), axis=0, tiled=True)
    vals = spectral_mix(spec, full_weight)
    branch = to_cells(inverse_dft(vals, norm_out)).reshape(chans, planes, cells)
    pre = branch + mixed
    output = gelu_value(pre).astype(jnp.bfloat16).reshape(1, chans, planes, cells)
    back = (grad_out * gelu_slope(pre)).astype(jnp.bfloat16)
    local_mix = jnp.einsum("cpq,dpq->cd", flat, back, preferred_element_type=jnp.float32)
    mix_scale = 1.0 / math.sqrt(samples * P_SIZE * NX * NY)
    spec_scale = 1.0 / math.sqrt(samples * P_SIZE)
    plane_back = to_planes(back.reshape(chans, planes, rows_x, NY)).astype(jnp.float32)
    gspec = forward_dft(plane_back, norm_out)
    local_spec = grads_of(spec, gspec)
    share = lax.psum_scatter(local_spec, ("gx", "gy"), scatter_dimension=0, tiled=True)
    spectral_grad = lax.psum(share, "dp") * spec_scale
    mixing_grad = lax.psum(local_mix, ("dp", "gx", "gy")) * mix_scale
    return (output, spectral_grad, mixing_grad)


def solution(mesh):
    return jax.shard_map(
        local,
        mesh=mesh,
        in_specs=(
            P("dp", None, None, ("gx", "gy")),
            P("dp", None, None, ("gx", "gy")),
            P(),
            P(("gx", "gy"), None, None, None),
        ),
        out_specs=(P("dp", None, None, ("gx", "gy")), P(("gx", "gy"), None, None, None), P()),
        check_vma=False,
    )
```

profile of v0, /device:TPU:0, one launch (start us, length us, event | category | flops | bytes accessed | tf_op | source)
XLA Modules:
  0.0 625.7 jit_solution(5017690169541826358)
XLA Ops:
  10.5 34.5 %all_to_all.99 = bf16[20,32,16,128]{3,2,0,1:T(8,128)(2,1)S(1)} all-to-all(bf16[20,32,16,128]{3,2,0,1:T(8,128)(2,1)S(1)} %copy.190), channel_id=1, replica_groups=mesh['dp'=4,'gx'=2,'gy'=4] {'gx'}, dimensions={1} | all-to-all | bytes 5242880 | tf_op jit(solution)/shard_map/all_to_all | solution.py:104
  47.9 4.7 all-to-all-start.1
  53.9 46.4 %all_gather.3 = bf16[288,2,20,20]{3,2,0,1:T(8,128)(2,1)S(1)} all-gather(bf16[36,2,20,20]{3,2,0,1:T(8,128)(2,1)} %copy.204), channel_id=1, replica_groups=mesh['dp'=4,'gx'=2,'gy'=4] {'gx','gy'}, dimensions={0}, use_global_device_ids=true | all-gather | bytes 518400 | tf_op jit(solution)/shard_map/all_gather | solution.py:144
  113.4 3.9 fusion.23
  117.3 3.9 fusion.22
  152.6 3.8 fusion.19
  161.4 8.3 %fusion.66 = f32[20,4,128,128]{3,2,1,0:T(8,128)S(1)} fusion(f32[20,4,128,12]{2,3,1,0:T(8,128)S(1)} %fusion.16), kind=kOutput, calls=%fused_computation.98 | convolution fusion | flops 188765184 | bytes 5734400 | tf_op jit(solution)/shard_map/dpxk,ky->dpxy/dot_general | solution.py:73
  169.7 8.7 %subtract_multiply_fusion = f32[20,4,128,128]{3,2,1,0:T(8,128)S(1)} fusion(f32[20,4,128,128]{3,2,1,0:T(8,128)S(1)} %fusion.66, f32[20,4,128,12]{2,3,1,0:T(8,128)S(1)} %fusion.15), kind=kOutput, calls=%fused_computation.11 | convolution fusion | flops 191386624 | bytes 10977280 | tf_op jit(solution)/shard_map/dpxk,ky->dpxy/dot_general | solution.py:74
  181.8 62.2 %all_to_all.100 = f32[20,4,128,128]{3,1,0,2:T(4,128)S(1)} all-to-all(f32[20,4,128,128]{3,1,0,2:T(4,128)S(1)} %copy.209), channel_id=1, replica_groups=mesh['dp'=4,'gx'=2,'gy'=4] {'gx'}, dimensions={2} | all-to-all | bytes 10485760 | tf_op jit(solution)/shard_map/all_to_all | solution.py:122
  249.6 62.4 %all_to_all.101 = f32[20,8,64,128]{3,1,0,2:T(8,128)S(1)} all-to-all(f32[20,8,64,128]{3,1,0,2:T(8,128)S(1)} %copy.212), channel_id=1, replica_groups=mesh['dp'=4,'gx'=2,'gy'=4] {'gy'}, dimensions={2} | all-to-all | bytes 10485760 | tf_op jit(solution)/shard_map/all_to_all | solution.py:121
  318.0 7.0 %reshape.54 = f32[20,32,2048]{2,0,1:T(8,128)} reshape(f32[20,2,4,4,16,128]{5,4,0,3,2,1:T(8,128)} %copy.249) | data formatting | bytes 10485760 | tf_op jit(solution)/shard_map/reshape;reshape | solution.py:146
  325.0 13.1 %fusion.6 = (bf16[20,32,2048]{2,0,1:T(8,128)(2,1)}, bf16[1,20,32,2048]{3,1,2,0:T(8,128)(2,1)}) fusion(bf16[1,20,32,2048]{3,2,1,0:T(8,128)(2,1)} %param.5, f32[20,32,2048]{2,0,1:T(8,128)} %reshape.54, bf16[20,32,2048]{2,1,0:T(8,128)(2,1)S(1)} %bitcast.209, bf16[20,20]{1,0:T(8,128)(2,1)S(1)} %copy-done), kind=kOutput, calls=%fused_computation.9 | convolution fusion | flops 82575360 | bytes 15729440 | tf_op jit(solution)/shard_map/cpq,cd->dpq/dot_general | solution.py:141
  338.1 4.3 reshape.55
  342.4 33.0 %all_to_all.102 = bf16[20,32,16,128]{3,2,0,1:T(8,128)(2,1)S(1)} all-to-all(bf16[20,32,16,128]{3,2,0,1:T(8,128)(2,1)S(1)} %reshape.55), channel_id=1, replica_groups=mesh['dp'=4,'gx'=2,'gy'=4] {'gx'}, dimensions={1} | all-to-all | bytes 5242880 | tf_op jit(solution)/shard_map/all_to_all | solution.py:104
  376.8 33.8 %all_to_all.103 = bf16[20,16,32,128]{3,2,0,1:T(8,128)(2,1)S(1)} all-to-all(bf16[20,16,32,128]{3,2,0,1:T(8,128)(2,1)S(1)} %copy.224), channel_id=1, replica_groups=mesh['dp'=4,'gx'=2,'gy'=4] {'gy'}, dimensions={1} | all-to-all | bytes 5242880 | tf_op jit(solution)/shard_map/all_to_all | solution.py:103
  432.1 5.9 fusion.40
  437.9 6.3 %fusion.39 = f32[288,20,20]{2,1,0:T(8,128)S(1)} fusion(f32[288,2,20,4]{2,3,0,1:T(4,128)S(1)} %broadcast_multiply_fusion, f32[288,2,20,4]{2,3,0,1:T(4,128)S(1)} %copy-done.3), kind=kOutput, calls=%fused_computation.62 | convolution fusion | flops 5529600 | bytes 1640448 | tf_op jit(solution)/shard_map/mcp,mdp->mcd/dot_general | solution.py:90
  444.3 6.0 subtract_bitcast_fusion
  450.2 6.1 add_bitcast_fusion
  459.8 10.1 %copy.235 = f32[288,2,20,20]{3,1,2,0:T(2,128)} copy(f32[288,2,20,20]{3,2,0,1:T(8,128)} %pad_maximum_fusion) | data formatting | bytes 1843200 | tf_op jit(solution)/shard_map/stack | solution.py:96
  471.8 5.0 copy.237
  480.4 40.8 %psum.15 = f32[20,20]{0,1:T(8,128)S(1)} all-reduce(f32[20,20]{0,1:T(8,128)S(1)} %fusion.24), channel_id=1, replica_groups=mesh['dp'=4,'gx'=2,'gy'=4] {'dp','gx','gy'}, use_global_device_ids=true, to_apply=%region_2.3 | all-reduce | flops 400 | bytes 3200 | tf_op jit(solution)/shard_map/psum | solution.py:158
  521.3 49.5 %all-reduce.6.cloned.1.call-done = f32[288,2,20,20]{3,1,2,0:T(2,128)} async-done(((f32[288,2,20,20]{3,1,2,0:T(2,128)}), f32[288,2,20,20]{3,1,2,0:T(2,128)}) %all-reduce.6.cloned.1.call-update) | async-done | bytes 921616
  573.5 42.4 %all-reduce.4.cloned.1.call-done = f32[36,2,20,20]{3,1,2,0:T(2,128)} async-done(((f32[36,2,20,20]{3,1,2,0:T(2,128)}), f32[36,2,20,20]{3,1,2,0:T(2,128)}) %all-reduce.4.cloned.1.call-update) | async-done | bytes 115216 | tf_op jit(solution)/shard_map/psum | solution.py:157
  (82 shorter events, 108.4 us)
Async XLA Ops:
  7.2 317.8 %copy-start = (bf16[20,20]{1,0:T(8,128)(2,1)S(1)}, bf16[20,20]{1,0:T(8,128)(2,1)}, u32[]{:S(2)}) copy-start(bf16[20,20]{1,0:T(8,128)(2,1)} %param.6) | copy-start | bytes 2404
  47.9 4.7 copy-start.8
  47.9 52.4 %all-to-all-start.1 = ((bf16[20,16,32,128]{3,2,0,1:T(8,128)(2,1)}), bf16[20,16,32,128]{3,2,0,1:T(8,128)(2,1)}, u32[]{:S(2)}, u32[]{:S(2)}) async-start(bf16[20,16,32,128]{3,2,0,1:T(8,128)(2,1)} %copy.193), calls=%async_computation.1 | async-start | bytes 5242880 | tf_op jit(solution)/shard_map/all_to_all | solution.py:103
  52.6 518.2 %all-reduce.6.cloned.1.call-start = ((), (), s32[]{:S(2)}) async-start(), calls=%async_computation.7 | async-start | bytes 11796480
  137.5 7.0 %copy-start.2 = (f32[288,2,20,4]{2,3,0,1:T(4,128)}, f32[288,2,20,4]{2,3,0,1:T(4,128)S(1)}, u32[]{:S(2)}) copy-start(f32[288,2,20,4]{2,3,0,1:T(4,128)S(1)} %broadcast_multiply_fusion.1) | copy-start | bytes 552964
  156.4 3.8 copy-start.7
  318.0 7.0 %copy-start.5 = (bf16[1,20,32,2048]{3,2,1,0:T(8,128)(2,1)S(1)}, bf16[1,20,32,2048]{3,2,1,0:T(8,128)(2,1)}, u32[]{:S(2)}) copy-start(bf16[1,20,32,2048]{3,2,1,0:T(8,128)(2,1)} %param.4) | copy-start | bytes 7864324
  429.6 2.5 copy-start.3
  469.9 0.7 copy-start.9
  469.9 6.8 %copy-start.4 = (bf16[20,32,2048]{2,0,1:T(8,128)(2,1)S(1)}, bf16[20,32,2048]{2,0,1:T(8,128)(2,1)}, u32[]{:S(2)}) copy-start(bf16[20,32,2048]{2,0,1:T(8,128)(2,1)} %get-tuple-element.21) | copy-start | bytes 7864324
  469.9 146.0 %all-reduce.4.cloned.1.call-start = ((), (), s32[]{:S(2)}) async-start(), calls=%async_computation.6 | async-start | bytes 1474560 | tf_op jit(solution)/shard_map/psum | solution.py:157
  471.8 5.0 copy-start.6
  476.8 141.9 %copy-start.1 = (bf16[20,20]{1,0:T(8,128)(2,1)S(1)}, bf16[20,20]{1,0:T(8,128)(2,1)}, u32[]{:S(2)}) copy-start(bf16[20,20]{1,0:T(8,128)(2,1)} %param.6) | copy-start | bytes 2404
Sparse Core Ops, SparseCore 0:
  470.0 100.7 all-reduce.5
  573.3 42.6 all-reduce.3
where the time goes:
time: 630 us; the launch traced here: 626 us
  blocking collectives  313 us (50%)
  matrix products  113 us (18%)
  waiting for transfers between devices  92 us (15%)
  local copies, waits for them, and re-layouts  79.4 us (13%)
  between operations  15.2 us (2%)
  other arithmetic  8.58 us (1%)
    all_to_all x2, blocking collectives, to_planes(): lax.all_to_all(block, 'gx', split_axis=1, concat_axis=2, tiled=True)  67.5 us
    all_to_all x1, blocking collectives, to_cells(): lax.all_to_all(lax.all_to_all(plane_block, 'gx', split_axis=2, concat_axi...  62.4 us
    all_to_all x1, blocking collectives, to_cells(): lax.all_to_all(plane_block, 'gx', split_axis=2, concat_axis=1, tiled=True)  62.2 us
    unnamed x3, waiting for transfers between devices  49.6 us
    all_gather x1, blocking collectives, local(): lax.all_gather(spectral_weight, ('gx', 'gy'), axis=0, tiled=True)  46.4 us
    psum x1, waiting for transfers between devices, local(): spectral_grad = lax.psum(share, 'dp') * spec_scale  42.4 us
    psum x1, blocking collectives, local(): mixing_grad = lax.psum(local_mix, ('dp', 'gx', 'gy')) * mix_scale  40.8 us
    all_to_all x1, blocking collectives, to_planes(): lax.all_to_all(lax.all_to_all(block, 'gx', split_axis=1, concat_axis=2, t...  33.8 us
  transfers between devices with their start and end apart: 3, of which 2 were waited for; matrix products, arithmetic and copies ran while one was open for 2% of the time, Pallas kernels for 0%

commit v1 on v0

v1 whole, which is shorter than its diff:
```python
import functools
import math

import jax
import jax.numpy as jnp
import ml_dtypes
import numpy as np
from jax import lax
from jax.experimental import pallas as pl
from jax.experimental.pallas import tpu as pltpu
from jax.sharding import PartitionSpec as P

NX = 128
NY = 128
KX = 24
KY = 12
MODES = 288
C = 20
PL = 32
CP = C * PL
CR = 24
SCALE = 1.6656925
GROUP = ("gx", "gy")
BF = jnp.bfloat16
F32 = jnp.float32


def round_up(n, k):
    return -(-n // k) * k


def table(groups):
    per = MODES // groups
    rows = round_up(2 * per, 8)
    index = np.arange(KX)
    waves_x = np.where(index < KX // 2, index, NX - KX + index)
    kx = np.repeat(waves_x, KY)
    ky = np.tile(np.arange(KY), KX)
    x = np.arange(NX * NY) // NY
    y = np.arange(NX * NY) % NY
    turn = (kx[:, None] * x[None] + ky[:, None] * y[None]) % 128
    wheel = 2.0 * np.pi * np.arange(128) / 128
    both = np.stack([(SCALE * np.cos(wheel))[turn], (-SCALE * np.sin(wheel))[turn]], 0)
    both = both.reshape(2, groups, per, -1).transpose(1, 0, 2, 3).reshape(groups, 2 * per, -1)
    full = np.zeros((groups, rows, NX * NY), np.float32)
    full[:, : 2 * per] = both
    full = full.reshape(groups * rows, groups, -1).transpose(1, 0, 2)
    return full.astype(ml_dtypes.bfloat16)


def selectors(groups):
    per = MODES // groups
    rows = round_up(2 * per, 8)
    re, im = np.arange(per), per + np.arange(per)
    spread = np.zeros((rows, 256), np.float32)
    spread[re, re] = 1
    spread[im, im] = 1
    spread[im, 128 + re] = -1
    spread[re, 128 + im] = 1
    weights = np.zeros((per, 128), np.float32)
    weights[re, re] = 1
    weights[re, im] = 1
    collect = np.zeros((rows, 128), np.float32)
    collect[re, re] = 1
    collect[im, im] = 1
    fold = np.zeros((rows, 256), np.float32)
    fold[re, re] = 1
    fold[re, im] = 1
    fold[im, 128 + re] = 1
    fold[im, 128 + im] = 1
    cast = lambda a: a.astype(ml_dtypes.bfloat16)
    return (
        cast(np.concatenate([spread, spread], 0)),
        cast(weights),
        cast(np.concatenate([collect, collect], 1)),
        cast(np.concatenate([fold, fold], 1)),
    )


def expander():
    e = np.zeros((CP, 128), np.float32)
    e[np.arange(CP), np.arange(CP) // PL] = 1
    return e.astype(ml_dtypes.bfloat16)


def dot(a, b, ca, cb):
    return lax.dot_general(a, b, (((ca,), (cb,)), ((), ())), preferred_element_type=F32)


def encode(v):
    return ((v * jnp.abs(v)) * (v * v)).astype(BF)


def decode(y):
    y = y.astype(F32)
    z = lax.rsqrt(jnp.maximum(jnp.abs(y), 1e-36))
    return ((y * z) * z) * lax.rsqrt(z)


def split(v):
    hi = v.astype(BF)
    return hi, (v - hi.astype(F32)).astype(BF)


def first_kernel(groups, rows, steps, gid_ref, f_ref, t_ref, o_ref, acc_ref):
    step = pl.program_id(0)
    part = dot(t_ref[0], f_ref[...], 1, 1)

    @pl.when(step == 0)
    def _():
        acc_ref[...] = part

    @pl.when(step > 0)
    def _():
        acc_ref[...] += part

    @pl.when(step == steps - 1)
    def _():
        for g in range(groups):
            o_ref[g] = encode(acc_ref[g * rows : (g + 1) * rows, :])


def mix_kernel(groups, rows, r_ref, w_ref, spread_ref, wsel_ref, collect_ref, v_ref, s_ref, wa_ref, wb_ref, vals_ref):
    total = decode(r_ref[0])
    for g in range(1, groups):
        total = total + decode(r_ref[g])
    total = total * (1.0 / (SCALE * math.sqrt(NX * NY)))
    hi, lo = split(total)
    both = jnp.concatenate([hi.astype(F32), lo.astype(F32)], 0).astype(BF)
    s_ref[0, 0:CP, :] = dot(both, spread_ref[:, 0:128], 0, 0)
    s_ref[1, 0:CP, :] = dot(both, spread_ref[:, 128:256], 0, 0)
    s_ref[:, CP:, :] = jnp.zeros((2, CR * PL - CP, 128), F32)
    w = w_ref[...]
    wa_ref[...] = dot(w[:, : C * C], wsel_ref[...], 0, 0)
    wb_ref[...] = dot(w[:, C * C :], wsel_ref[...], 0, 0)

    def some(block, _):
        base = block * 4
        acc = [None] * 4
        for c in range(C):
            s = s_ref[0, c * PL : (c + 1) * PL, :]
            t = s_ref[1, c * PL : (c + 1) * PL, :]
            for k in range(4):
                row = c * C + base + k
                term = s * wa_ref[pl.ds(row, 1), :] + t * wb_ref[pl.ds(row, 1), :]
                acc[k] = term if acc[k] is None else acc[k] + term
        for k in range(4):
            vals_ref[pl.ds(pl.multiple_of((base + k) * PL, PL), PL), :] = acc[k]
        return 0

    lax.fori_loop(0, C // 4, some, 0)
    vals = vals_ref[...] * (1.0 / (SCALE * math.sqrt(MODES)))
    hi, lo = split(vals)
    v_ref[...] = dot(collect_ref[...], jnp.concatenate([hi, lo], 1), 1, 1).astype(BF)


def gelu_both(h):
    k = math.sqrt(2.0 / math.pi)
    h2 = h * h
    t = jnp.tanh(h * (k + (k * 0.044715) * h2))
    half = 0.5 + 0.5 * t
    slope = half + (h * (half * (1.0 - t))) * (k + (3.0 * 0.044715 * k) * h2)
    return h * half, slope


def same_plane(n):
    i = lax.broadcasted_iota(jnp.int32, (n, n), 0)
    j = lax.broadcasted_iota(jnp.int32, (n, n), 1)
    return lax.rem(i, PL) == lax.rem(j, PL)


def main_kernel(
    groups, rows, steps, gid_ref, f_ref, cot_ref, t_ref, v_ref, mix_ref, e_ref,
    out_ref, o_ref, a_ref, m_ref, acc_ref, accm_ref,
):
    step = pl.program_id(0)

    @pl.when(step == 0)
    def _():
        a_ref[...] = jnp.transpose(v_ref[...].astype(F32)).astype(BF)
        e = e_ref[:, 0:C]
        u = dot(e, mix_ref[...], 1, 1).astype(BF)
        m = dot(u, e, 1, 1)
        m_ref[...] = jnp.where(same_plane(CP), m, 0.0).astype(BF)

    t = t_ref[0]
    f = f_ref[...]
    pre = dot(a_ref[...], t, 1, 0) + dot(m_ref[...], f, 1, 0)
    value, slope = gelu_both(pre)
    out_ref[...] = value.astype(BF)
    back = (cot_ref[...].astype(F32) * slope).astype(BF)
    part = dot(t, back, 1, 1)
    partm = dot(f, back, 1, 1)

    @pl.when(step == 0)
    def _():
        acc_ref[...] = part
        accm_ref[...] = partm

    @pl.when(step > 0)
    def _():
        acc_ref[...] += part
        accm_ref[...] += partm

    @pl.when(step == steps - 1)
    def _():
        kept = jnp.where(same_plane(CP), accm_ref[...], 0.0)
        kept = jnp.sum(kept.reshape(C, PL, CP), axis=1)
        kept = jnp.concatenate([kept, jnp.zeros((CR - C, CP), F32)], 0)
        hi, lo = split(kept)
        y = dot(hi, e_ref[...], 1, 0) + dot(lo, e_ref[...], 1, 0)
        yh = y.astype(BF).astype(F32)
        y = yh + pltpu.roll(y - yh, 64, 1)
        extra = jnp.concatenate([y[0:8], y[8:16], y[16:24], jnp.zeros((8, CP - 384), F32)], 1).astype(BF)
        extra = extra.astype(F32)
        for g in range(groups):
            v = acc_ref[g * rows : (g + 1) * rows, :]
            coded = (v * jnp.abs(v)) * (v * v)
            o_ref[g] = jnp.concatenate([coded, extra], 0).astype(BF)


def grad_kernel(groups, rows, r_ref, s_ref, spread_ref, fold_ref, o_ref, g_ref, p_ref):
    total = None
    extra = None
    for g in range(groups):
        block = r_ref[g].astype(F32)
        y = block[0:rows]
        z = lax.rsqrt(jnp.maximum(jnp.abs(y), 1e-36))
        y = ((y * z) * z) * lax.rsqrt(z)
        total = y if total is None else total + y
        x = block[rows : rows + 8]
        extra = x if extra is None else extra + x
    total = total * (1.0 / (SCALE * math.sqrt(MODES)))
    hi, lo = split(total)
    both = jnp.concatenate([hi.astype(F32), lo.astype(F32)], 0).astype(BF)
    g_ref[...] = dot(both, spread_ref[:, 0:128], 0, 0)

    def some(block, _):
        base = block * 4
        one = [jnp.zeros((CR, 128), F32)] * 4
        two = [jnp.zeros((CR, 128), F32)] * 4
        for p in range(PL):
            s = s_ref[0, pl.ds(p, CR, stride=PL), :]
            t = s_ref[1, pl.ds(p, CR, stride=PL), :]
            for k in range(4):
                g = g_ref[pl.ds((base + k) * PL + p, 1), :]
                one[k] = one[k] + s * g
                two[k] = two[k] + t * g
        for k in range(4):
            at = pl.multiple_of((base + k) * CR, CR)
            p_ref[pl.ds(at, CR), 0:128] = one[k]
            p_ref[pl.ds(at, CR), 128:256] = two[k]
        return 0

    lax.fori_loop(0, C // 4, some, 0)
    hi, lo = split(p_ref[...])
    grads = dot(fold_ref[...], jnp.concatenate([hi, lo], 1), 1, 1)
    grads = jnp.concatenate([grads, jnp.zeros((rows, 512 - C * CR), F32)], 1)
    extra = extra[:, 0:512]
    extra = extra + pltpu.roll(extra, 512 - 64, 1)
    all_rows = jnp.concatenate([grads, extra], 0)
    o_ref[...] = (all_rows * jnp.abs(all_rows)) * (all_rows * all_rows)


def compiler_params(mib):
    return pltpu.CompilerParams(vmem_limit_bytes=mib * 2**20)


def local(tables, consts, fields, cotangent, mix_weight, spectral_weight):
    spread, wsel, collect, fold = consts
    cells = fields.shape[3]
    groups = lax.axis_size("gx") * lax.axis_size("gy")
    samples = lax.axis_size("dp")
    per = MODES // groups
    rows = round_up(2 * per, 8)
    flat = fields.reshape(CP, cells)
    cot = cotangent.reshape(CP, cells)
    gid = (lax.axis_index("gx") * lax.axis_size("gy") + lax.axis_index("gy")).astype(jnp.int32).reshape(1)
    width = min(512, cells)
    steps = cells // width
    whole = lambda shape: pl.BlockSpec(shape, lambda *_: (0,) * len(shape))
    cells_spec = pl.BlockSpec((CP, width), lambda i, gid: (0, i))
    table_spec = pl.BlockSpec((1, groups * rows, width), lambda i, gid: (gid[0], 0, i))

    sent = pl.pallas_call(
        functools.partial(first_kernel, groups, rows, steps),
        grid_spec=pltpu.PrefetchScalarGridSpec(
            num_scalar_prefetch=1,
            grid=(steps,),
            in_specs=[cells_spec, table_spec],
            out_specs=whole((groups, rows, CP)),
            scratch_shapes=[pltpu.VMEM((groups * rows, CP), F32)],
        ),
        out_shape=jax.ShapeDtypeStruct((groups, rows, CP), BF),
        compiler_params=compiler_params(32),
        name="spectrum_parts",
    )(gid, flat, tables)
    got = lax.all_to_all(sent, GROUP, 0, 0, tiled=True)

    weights = spectral_weight.reshape(per, 2 * C * C)
    vals, spec = pl.pallas_call(
        functools.partial(mix_kernel, groups, rows),
        out_shape=(jax.ShapeDtypeStruct((rows, CP), BF), jax.ShapeDtypeStruct((2, CR * PL, 128), F32)),
        scratch_shapes=[pltpu.VMEM((C * C, 128), F32), pltpu.VMEM((C * C, 128), F32), pltpu.VMEM((CP, 128), F32)],
        compiler_params=compiler_params(32),
        name="mode_mixing",
    )(got, weights, spread, wsel, collect)
    all_vals = lax.all_gather(vals, GROUP, axis=0, tiled=True)

    output, sent = pl.pallas_call(
        functools.partial(main_kernel, groups, rows, steps),
        grid_spec=pltpu.PrefetchScalarGridSpec(
            num_scalar_prefetch=1,
            grid=(steps,),
            in_specs=[
                cells_spec,
                cells_spec,
                table_spec,
                whole((groups * rows, CP)),
                whole((C, C)),
                whole((CP, 128)),
            ],
            out_specs=[cells_spec, whole((groups, rows + 8, CP))],
            scratch_shapes=[
                pltpu.VMEM((CP, groups * rows), BF),
                pltpu.VMEM((CP, CP), BF),
                pltpu.VMEM((groups * rows, CP), F32),
                pltpu.VMEM((CP, CP), F32),
            ],
        ),
        out_shape=(
            jax.ShapeDtypeStruct((CP, cells), BF),
            jax.ShapeDtypeStruct((groups, rows + 8, CP), BF),
        ),
        compiler_params=compiler_params(48),
        name="cells",
    )(gid, flat, cot, tables, all_vals, mix_weight, expander())
    got = lax.all_to_all(sent, GROUP, 0, 0, tiled=True)

    coded = pl.pallas_call(
        functools.partial(grad_kernel, groups, rows),
        out_shape=jax.ShapeDtypeStruct((rows + 8, 512), F32),
        scratch_shapes=[pltpu.VMEM((CP, 128), F32), pltpu.VMEM((C * CR, 256), F32)],
        compiler_params=compiler_params(32),
        name="mode_grads",
    )(got, spec, spread, fold)
    coded = coded.astype(BF)
    total = decode(coded)
    for k in range(1, samples):
        total = total + decode(lax.ppermute(coded, "dp", [(i, (i + k) % samples) for i in range(samples)]))

    grads = total[: 2 * per, : C * CR].reshape(2, per, C, CR)[..., :C]
    spectral_grad = jnp.transpose(grads, (1, 0, 3, 2)) * (1.0 / math.sqrt(samples * PL))
    extra = total[rows:, :384].reshape(8, 3, 128)[:, :, :C]
    mixing = jnp.transpose(extra, (1, 0, 2)).reshape(24, C)[:C]
    mixing_grad = mixing * (1.0 / math.sqrt(samples * PL * NX * NY))
    return (output.reshape(1, C, PL, cells), spectral_grad, mixing_grad)


def solution(mesh):
    groups = mesh.shape["gx"] * mesh.shape["gy"]
    body = functools.partial(local, table(groups), selectors(groups))
    return jax.shard_map(
        body,
        mesh=mesh,
        in_specs=(
            P("dp", None, None, GROUP),
            P("dp", None, None, GROUP),
            P(),
            P(GROUP, None, None, None),
        ),
        out_specs=(P("dp", None, None, GROUP), P(GROUP, None, None, None), P()),
        check_vma=False,
    )
```

time: 630 us -> 92.3 us (0.15)
  blocking collectives: 313 us -> 25.8 us
  matrix products: 113 us -> 0 us
  waiting for transfers between devices: 92 us -> 11.2 us
  local copies, waits for them, and re-layouts: 79.4 us -> 15.5 us
  Pallas kernels: 0 us -> 25.6 us
  between operations: 15.2 us -> 0.76 us
  other arithmetic: 8.58 us -> 1.02 us
  starting transfers between devices: 4.77 us -> 11.9 us
    all_to_all x5 -> x1, blocking collectives: 226 us -> 15.5 us  [local(): got = lax.all_to_all(sent, GROUP, 0, 0, tiled=True)]
    dot_general x28 -> x0, matrix products: 113 us -> none  [the longest x1 13.1 us: local(): jnp.einsum('cpq,cd->dpq', flat, mix_weight, preferred_element_type=jnp.fl...]
    unnamed x3 -> x0, waiting for transfers between devices: 49.6 us -> none
    psum x1 -> x0, waiting for transfers between devices: 42.4 us -> none  [local(): spectral_grad = lax.psum(share, 'dp') * spec_scale]
    psum x1 -> x0, blocking collectives: 40.8 us -> none  [local(): mixing_grad = lax.psum(local_mix, ('dp', 'gx', 'gy')) * mix_scale]
    all_gather x1, blocking collectives: 46.4 us -> 10.3 us  [local(): all_vals = lax.all_gather(vals, GROUP, axis=0, tiled=True)]
    another operation x12 -> x0, local copies, waits for them, and re-layouts: 33.3 us -> none  [the longest x1 10.1 us: grads_of(): return jnp.stack([g_re, g_im], axis=1)]
    pallas_call x0 -> x4, Pallas kernels: none -> 25.6 us  [the longest x1 15.4 us: local(): pl.pallas_call(functools.partial(main_kernel, groups, rows, steps), grid_...]
  transfers between devices with their start and end apart: 3 -> 4, of which waited for: 2 -> 4; matrix products, arithmetic and copies ran while one was open for 2% -> 4% of each run, Pallas kernels for 0% -> 0%
where the time goes in v1:
time: 92.3 us; the launch traced here: 91.8 us
  blocking collectives  25.8 us (28%)
  Pallas kernels  25.6 us (28%)
  local copies, waits for them, and re-layouts  15.5 us (17%)
  starting transfers between devices  11.9 us (13%)
  waiting for transfers between devices  11.2 us (12%)
  other arithmetic  1.02 us (1%)
    all_to_all x1, blocking collectives, local(): got = lax.all_to_all(sent, GROUP, 0, 0, tiled=True)  15.5 us
    pallas_call x1, Pallas kernels, local(): pl.pallas_call(functools.partial(main_kernel, groups, rows, steps), grid_...  15.4 us
    unnamed x21, local copies, waits for them, and re-layouts  11.5 us
    all_gather x1, blocking collectives, local(): all_vals = lax.all_gather(vals, GROUP, axis=0, tiled=True)  10.3 us
    all_to_all x1, waiting for transfers between devices, local(): got = lax.all_to_all(sent, GROUP, 0, 0, tiled=True)  7.55 us
    ppermute x3, starting transfers between devices, local(): lax.ppermute(coded, 'dp', [(i, (i + k) % samples) for i in range(samples)])  6.48 us
    all_to_all x1, starting transfers between devices, local(): got = lax.all_to_all(sent, GROUP, 0, 0, tiled=True)  5.43 us
    pallas_call x1, Pallas kernels, local(): pl.pallas_call(functools.partial(grad_kernel, groups, rows), out_shape=ja...  4.01 us
  transfers between devices with their start and end apart: 4, of which 4 were waited for; matrix products, arithmetic and copies ran while one was open for 4% of the time, Pallas kernels for 0%

profile of v1, /device:TPU:0, one launch (start us, length us, event | category | flops | bytes accessed | tf_op | source)
XLA Modules:
  0.0 91.8 jit_solution(13771508416008937036)
XLA Ops:
  0.6 6.4 %copy-done = bf16[8,576,2048]{2,1,0:T(8,128)(2,1)S(1)} copy-done((bf16[8,576,2048]{2,1,0:T(8,128)(2,1)S(1)}, bf16[8,576,2048]{2,1,0:T(8,128)(2,1)}, u32[]{:S(2)}) %copy-start) | copy-done | bytes 18874392
  7.0 1.7 %copy-done.1 = bf16[1,20,32,2048]{3,2,1,0:T(8,128)(2,1)S(1)} copy-done((bf16[1,20,32,2048]{3,2,1,0:T(8,128)(2,1)S(1)}, bf16[1,20,32,2048]{3,2,1,0:T(8,128)(2,1)}, u32[]{:S(2)}) %copy-start.1) | copy-done | bytes 2621464
  8.8 3.8 %spectrum_parts.1 = bf16[8,72,640]{2,1,0:T(8,128)(2,1)S(1)} custom-call(s32[1]{0:T(128)} %bitcast.gid_ref, bf16[640,2048]{1,0:T(8,128)(2,1)S(1)} %bitcast.14, bf16[8,576,2048]{2,1,0:T(8,128)(2,1)S(1)} %copy-done), custom_call_target="tpu_custom_call" | custom-call | tf_op jit(solution)/shard_map/spectrum_parts/pallas_call | solution.py:285
  12.6 0.9 copy-done.3
  13.4 5.4 %all-to-all-start = ((bf16[8,72,640]{2,1,0:T(8,128)(2,1)}), bf16[8,72,640]{2,1,0:T(8,128)(2,1)S(1)}, u32[]{:S(2)}, u32[]{:S(2)}) async-start(bf16[8,72,640]{2,1,0:T(8,128)(2,1)} %copy-done.3), calls=%async_computation | async-start | bytes 1474560 | tf_op jit(solution)/shard_map/all_to_all | solution.py:298
  18.9 2.2 %copy.19 = bf16[36,2,20,20]{3,2,1,0:T(8,128)(2,1)} copy(bf16[36,2,20,20]{0,1,3,2:T(2,128)(2,1)} %param.13) | data formatting | bytes 115200 | tf_op jit(solution)/shard_map/reshape | solution.py:300
  21.1 1.4 %reshape.38.w_ref = bf16[36,800]{1,0:T(8,128)(2,1)S(1)} reshape(bf16[36,2,20,20]{3,2,1,0:T(8,128)(2,1)} %copy.19) | data formatting | bytes 115200 | tf_op jit(solution)/shard_map/reshape | solution.py:300
  22.4 7.5 %all-to-all-done.r_ref = bf16[8,72,640]{2,1,0:T(8,128)(2,1)S(1)} async-done(((bf16[8,72,640]{2,1,0:T(8,128)(2,1)}), bf16[8,72,640]{2,1,0:T(8,128)(2,1)S(1)}, u32[]{:S(2)}, u32[]{:S(2)}) %all-to-all-start) | async-done | bytes 737312 | tf_op jit(solution)/shard_map/all_to_all | solution.py:298
  30.0 2.4 %mode_mixing.1 = (bf16[72,640]{1,0:T(8,128)(2,1)S(1)}, f32[2,768,128]{2,1,0:T(8,128)S(1)}) custom-call(bf16[8,72,640]{2,1,0:T(8,128)(2,1)S(1)} %all-to-all-done.r_ref, bf16[36,800]{1,0:T(8,128)(2,1)S(1)} %reshape.38.w_ref, bf16[144,256]{1,0:T(8,128)(2,1)S(1)} %copy-done.4, bf16[36,128]{1,0:T(8,128)(2,1)S(1)} %copy-done.8, bf16[72,256]{1,0:T(8,128)(2,1)S(1)} %copy-done.7), custom_call_target="tpu_custom_call" | custom-call | tf_op jit(solution)/shard_map/mode_mixing/pallas_call | solution.py:301
  32.4 10.3 %all_gather.3.v_ref = bf16[576,640]{1,0:T(8,128)(2,1)S(1)} all-gather(bf16[72,640]{1,0:T(8,128)(2,1)S(1)} %get-tuple-element.7), channel_id=1, replica_groups=mesh['dp'=4,'gx'=2,'gy'=4] {'gx','gy'}, dimensions={0}, use_global_device_ids=true | all-gather | bytes 829440 | tf_op jit(solution)/shard_map/all_gather | solution.py:308
  42.7 0.9 copy-done.5
  43.6 0.7 copy-done.9
  44.3 15.4 %cells.1 = (bf16[640,2048]{1,0:T(8,128)(2,1)}, bf16[8,80,640]{2,1,0:T(8,128)(2,1)S(1)}) custom-call(s32[1]{0:T(128)} %bitcast.gid_ref, bf16[640,2048]{1,0:T(8,128)(2,1)S(1)} %bitcast.15, bf16[640,2048]{1,0:T(8,128)(2,1)} %bitcast.16, bf16[8,576,2048]{2,1,0:T(8,128)(2,1)} %constant.29.clone.t_ref, bf16[576,640]{1,0:T(8,128)(2,1)S(1)} %all_gather.3.v_ref, ...), custom_call_target="tpu_custom_call" | custom-call | tf_op jit(solution)/shard_map/cells/pallas_call | solution.py:310
  59.7 15.5 %all_to_all.10.r_ref = bf16[8,80,640]{2,1,0:T(8,128)(2,1)S(1)} all-to-all(bf16[8,80,640]{2,1,0:T(8,128)(2,1)S(1)} %get-tuple-element.9), channel_id=1, replica_groups=mesh['dp'=4,'gx'=2,'gy'=4] {'gx','gy'}, dimensions={0} | all-to-all | bytes 1638400 | tf_op jit(solution)/shard_map/all_to_all | solution.py:338
  75.3 4.0 %mode_grads.1 = f32[80,512]{1,0:T(8,128)S(1)} custom-call(bf16[8,80,640]{2,1,0:T(8,128)(2,1)S(1)} %all_to_all.10.r_ref, f32[2,768,128]{2,1,0:T(8,128)S(1)} %get-tuple-element.10.s_ref, bf16[144,256]{1,0:T(8,128)(2,1)S(1)} %copy-done.4, bf16[72,512]{1,0:T(8,128)(2,1)S(1)} %copy-done.6), custom_call_target="tpu_custom_call" | custom-call | tf_op jit(solution)/shard_map/mode_grads/pallas_call | solution.py:340
  79.3 2.7 %collective-permute-start.1 = (bf16[80,512]{1,0:T(8,128)(2,1)S(1)}, bf16[80,512]{1,0:T(8,128)(2,1)S(1)}, u32[]{:S(2)}, u32[]{:S(2)}) collective-permute-start(bf16[80,512]{1,0:T(8,128)(2,1)S(1)} %convert_element_type.15), channel_id=1, source_target_pairs={{0,16},{8,24},{16,0},{24,8},{1,17},{9,25},{17,1},{25,9},{2,18},{10... | collective-permute-start | bytes 245768 | tf_op jit(solution)/shard_map/ppermute | solution.py:350
  82.0 1.6 %collective-permute-start = (bf16[80,512]{1,0:T(8,128)(2,1)S(1)}, bf16[80,512]{1,0:T(8,128)(2,1)S(1)}, u32[]{:S(2)}, u32[]{:S(2)}) collective-permute-start(bf16[80,512]{1,0:T(8,128)(2,1)S(1)} %convert_element_type.15), channel_id=1, source_target_pairs={{0,8},{8,16},{16,24},{24,0},{1,9},{9,17},{17,25},{25,1},{2,10},{10... | collective-permute-start | bytes 245768 | tf_op jit(solution)/shard_map/ppermute | solution.py:350
  83.5 2.3 %collective-permute-start.2 = (bf16[80,512]{1,0:T(8,128)(2,1)S(1)}, bf16[80,512]{1,0:T(8,128)(2,1)S(1)}, u32[]{:S(2)}, u32[]{:S(2)}) collective-permute-start(bf16[80,512]{1,0:T(8,128)(2,1)S(1)} %convert_element_type.15), channel_id=1, source_target_pairs={{0,24},{8,0},{16,8},{24,16},{1,25},{9,1},{17,9},{25,17},{2,26},{10... | collective-permute-start | bytes 245768 | tf_op jit(solution)/shard_map/ppermute | solution.py:350
  85.8 2.1 %collective-permute-done.1 = bf16[80,512]{1,0:T(8,128)(2,1)S(1)} collective-permute-done((bf16[80,512]{1,0:T(8,128)(2,1)S(1)}, bf16[80,512]{1,0:T(8,128)(2,1)S(1)}, u32[]{:S(2)}, u32[]{:S(2)}) %collective-permute-start.1) | collective-permute-done | bytes 81952 | tf_op jit(solution)/shard_map/ppermute | solution.py:350
  87.9 0.7 collective-permute-done
  88.6 0.8 collective-permute-done.2
  89.6 0.6 slice_multiply_fusion.1
  90.4 0.3 reshape.35
  90.9 0.9 copy.18
  (22 shorter events, 0.6 us)
Async XLA Ops:
  0.6 6.4 %copy-start = (bf16[8,576,2048]{2,1,0:T(8,128)(2,1)S(1)}, bf16[8,576,2048]{2,1,0:T(8,128)(2,1)}, u32[]{:S(2)}) copy-start(bf16[8,576,2048]{2,1,0:T(8,128)(2,1)} %constant.29.clone.t_ref) | copy-start | bytes 56623108
  7.0 1.7 %copy-start.1 = (bf16[1,20,32,2048]{3,2,1,0:T(8,128)(2,1)S(1)}, bf16[1,20,32,2048]{3,2,1,0:T(8,128)(2,1)}, u32[]{:S(2)}) copy-start(bf16[1,20,32,2048]{3,2,1,0:T(8,128)(2,1)} %param.10) | copy-start | bytes 7864324
  8.7 21.3 %copy-start.4 = (bf16[144,256]{1,0:T(8,128)(2,1)S(1)}, bf16[144,256]{1,0:T(8,128)(2,1)}, u32[]{:S(2)}) copy-start(bf16[144,256]{1,0:T(8,128)(2,1)} %constant.30.clone.spread_ref) | copy-start | bytes 221188
  8.7 21.3 %copy-start.7 = (bf16[72,256]{1,0:T(8,128)(2,1)S(1)}, bf16[72,256]{1,0:T(8,128)(2,1)}, u32[]{:S(2)}) copy-start(bf16[72,256]{1,0:T(8,128)(2,1)} %constant.32.clone.collect_ref) | copy-start | bytes 110596
  12.6 0.9 copy-start.3
  13.4 16.6 %copy-start.8 = (bf16[36,128]{1,0:T(8,128)(2,1)S(1)}, bf16[36,128]{1,0:T(8,128)(2,1)}, u32[]{:S(2)}) copy-start(bf16[36,128]{1,0:T(8,128)(2,1)} %constant.31.clone.wsel_ref) | copy-start | bytes 27652
  13.4 29.3 %copy-start.2 = (bf16[1,20,32,2048]{3,2,1,0:T(8,128)(2,1)S(1)}, bf16[1,20,32,2048]{3,2,1,0:T(8,128)(2,1)}, u32[]{:S(2)}) copy-start(bf16[1,20,32,2048]{3,2,1,0:T(8,128)(2,1)} %param.10) | copy-start | bytes 7864324
  13.4 16.6 %all-to-all-start = ((bf16[8,72,640]{2,1,0:T(8,128)(2,1)}), bf16[8,72,640]{2,1,0:T(8,128)(2,1)S(1)}, u32[]{:S(2)}, u32[]{:S(2)}) async-start(bf16[8,72,640]{2,1,0:T(8,128)(2,1)} %copy-done.3), calls=%async_computation | async-start | bytes 1474560 | tf_op jit(solution)/shard_map/all_to_all | solution.py:298
  42.7 0.9 copy-start.5
  43.6 0.7 copy-start.9
  44.3 30.9 %copy-start.6 = (bf16[72,512]{1,0:T(8,128)(2,1)S(1)}, bf16[72,512]{1,0:T(8,128)(2,1)}, u32[]{:S(2)}) copy-start(bf16[72,512]{1,0:T(8,128)(2,1)} %constant.34.clone.fold_ref) | copy-start | bytes 221188
  79.3 8.6 %collective-permute-start.1 = (bf16[80,512]{1,0:T(8,128)(2,1)S(1)}, bf16[80,512]{1,0:T(8,128)(2,1)S(1)}, u32[]{:S(2)}, u32[]{:S(2)}) collective-permute-start(bf16[80,512]{1,0:T(8,128)(2,1)S(1)} %convert_element_type.15), channel_id=1, source_target_pairs={{0,16},{8,24},{16,0},{24,8},{1,17},{9,25},{17,1},{25,9},{2,18},{10... | collective-permute-start | bytes 245768 | tf_op jit(solution)/shard_map/ppermute | solution.py:350
  82.0 6.7 %collective-permute-start = (bf16[80,512]{1,0:T(8,128)(2,1)S(1)}, bf16[80,512]{1,0:T(8,128)(2,1)S(1)}, u32[]{:S(2)}, u32[]{:S(2)}) collective-permute-start(bf16[80,512]{1,0:T(8,128)(2,1)S(1)} %convert_element_type.15), channel_id=1, source_target_pairs={{0,8},{8,16},{16,24},{24,0},{1,9},{9,17},{17,25},{25,1},{2,10},{10... | collective-permute-start | bytes 245768 | tf_op jit(solution)/shard_map/ppermute | solution.py:350
  83.5 5.9 %collective-permute-start.2 = (bf16[80,512]{1,0:T(8,128)(2,1)S(1)}, bf16[80,512]{1,0:T(8,128)(2,1)S(1)}, u32[]{:S(2)}, u32[]{:S(2)}) collective-permute-start(bf16[80,512]{1,0:T(8,128)(2,1)S(1)} %convert_element_type.15), channel_id=1, source_target_pairs={{0,24},{8,0},{16,8},{24,16},{1,25},{9,1},{17,9},{25,17},{2,26},{10... | collective-permute-start | bytes 245768 | tf_op jit(solution)/shard_map/ppermute | solution.py:350

commit v2 on v1

--- a/solution.py
+++ b/solution.py
@@ -18,6 +18,8 @@
 C = 20
 PL = 32
 CP = C * PL
+HP = 16
+HALF = C * HP
 CR = 24
 SCALE = 1.6656925
 GROUP = ("gx", "gy")
@@ -77,12 +79,6 @@
     )
 
 
-def expander():
-    e = np.zeros((CP, 128), np.float32)
-    e[np.arange(CP), np.arange(CP) // PL] = 1
-    return e.astype(ml_dtypes.bfloat16)
-
-
 def dot(a, b, ca, cb):
     return lax.dot_general(a, b, (((ca,), (cb,)), ((), ())), preferred_element_type=F32)
 
@@ -102,22 +98,83 @@
     return hi, (v - hi.astype(F32)).astype(BF)
 
 
-def first_kernel(groups, rows, steps, gid_ref, f_ref, t_ref, o_ref, acc_ref):
-    step = pl.program_id(0)
-    part = dot(t_ref[0], f_ref[...], 1, 1)
-
-    @pl.when(step == 0)
-    def _():
-        acc_ref[...] = part
-
-    @pl.when(step > 0)
-    def _():
-        acc_ref[...] += part
-
-    @pl.when(step == steps - 1)
-    def _():
-        for g in range(groups):
-            o_ref[g] = encode(acc_ref[g * rows : (g + 1) * rows, :])
+def chunk_copies(pairs, parts, sem):
+    copies = []
+    for j in range(parts):
+        copies.append([])
+        for k, (source, target) in enumerate(pairs):
+            width = target.shape[-1] // parts
+            index = (slice(None),) * (len(target.shape) - 1) + (pl.ds(j * width, width),)
+            copies[j].append(pltpu.make_async_copy(source.at[index], target.at[index], sem.at[k, j]))
+    return copies
+
+
+def start_chunk(copies, j):
+    if j < len(copies):
+        for copy in copies[j]:
+            copy.start()
+
+
+def first_kernel(groups, rows, parts, gid_ref, f_hbm, t_hbm, o_hbm, f_ref, t_ref, acc_ref, o_ref, sem, o_sem):
+    gid = gid_ref[0]
+    width = f_ref.shape[1] // parts
+    copies = chunk_copies([(f_hbm, f_ref), (t_hbm.at[gid], t_ref)], parts, sem)
+    for j in range(parts):
+        start_chunk(copies, j)
+    for j in range(parts):
+        at = slice(j * width, (j + 1) * width)
+        for copy in copies[j]:
+            copy.wait()
+        part = dot(t_ref[:, at], f_ref[:, at], 1, 1)
+        if j == 0:
+            acc_ref[...] = part
+        elif j < parts - 1:
+            acc_ref[...] += part
+    sent = acc_ref[...] + part if parts > 1 else part
+    out = []
+    for g in range(groups):
+        o_ref[g] = encode(sent[g * rows : (g + 1) * rows, :])
+        out.append(pltpu.make_async_copy(o_ref.at[g], o_hbm.at[g], o_sem.at[g]))
+        out[g].start()
+    for copy in out:
+        copy.wait()
+
+
+def same_plane(n):
+    i = lax.broadcasted_iota(jnp.int32, (n, n), 0)
+    j = lax.broadcasted_iota(jnp.int32, (n, n), 1)
+    return lax.rem(i, HP) == lax.rem(j, HP)
+
+
+def channel_of(lanes):
+    i = lax.broadcasted_iota(jnp.int32, (HALF, lanes), 0)
+    j = lax.broadcasted_iota(jnp.int32, (HALF, lanes), 1)
+    return jnp.where(lax.div(i, HP) == j, 1.0, 0.0).astype(BF)
+
+
+def half(x, h):
+    return x.reshape(C, PL // HP, HP, x.shape[1])[:, h].reshape(HALF, x.shape[1])
+
+
+def cell_mix_kernel(parts, f_hbm, mix_ref, o_hbm, f_ref, o_ref, sem, o_sem):
+    width = f_ref.shape[1] // parts
+    copies = chunk_copies([(f_hbm, f_ref)], parts, sem)
+    start_chunk(copies, 0)
+    e = channel_of(C)
+    u = dot(e, mix_ref[...], 1, 1).astype(BF)
+    m = jnp.where(same_plane(HALF), dot(u, e, 1, 1), 0.0).astype(BF)
+    out = []
+    for j in range(parts):
+        at = slice(j * width, (j + 1) * width)
+        copies[j][0].wait()
+        start_chunk(copies, j + 1)
+        f = f_ref[:, at]
+        for h in range(PL // HP):
+            o_ref[:, h, :, at] = dot(m, half(f, h), 1, 0).reshape(C, HP, width)
+        out.append(pltpu.make_async_copy(o_ref.at[:, :, :, at], o_hbm.at[:, :, :, at], o_sem.at[j]))
+        out[j].start()
+    for copy in out:
+        copy.wait()
 
 
 def mix_kernel(groups, rows, r_ref, w_ref, spread_ref, wsel_ref, collect_ref, v_ref, s_ref, wa_ref, wb_ref, vals_ref):
@@ -163,60 +220,61 @@
     return h * half, slope
 
 
-def same_plane(n):
-    i = lax.broadcasted_iota(jnp.int32, (n, n), 0)
-    j = lax.broadcasted_iota(jnp.int32, (n, n), 1)
-    return lax.rem(i, PL) == lax.rem(j, PL)
-
-
 def main_kernel(
-    groups, rows, steps, gid_ref, f_ref, cot_ref, t_ref, v_ref, mix_ref, e_ref,
-    out_ref, o_ref, a_ref, m_ref, acc_ref, accm_ref,
+    groups, rows, parts, gid_ref, t_hbm, mixed_hbm, cot_hbm, f_hbm, v_ref, out_hbm, o_ref,
+    t_ref, mixed_ref, cot_ref, f_ref, out_ref, a_ref, acc_ref, product_ref, t_sem, sem, out_sem,
 ):
-    step = pl.program_id(0)
-
-    @pl.when(step == 0)
-    def _():
-        a_ref[...] = jnp.transpose(v_ref[...].astype(F32)).astype(BF)
-        e = e_ref[:, 0:C]
-        u = dot(e, mix_ref[...], 1, 1).astype(BF)
-        m = dot(u, e, 1, 1)
-        m_ref[...] = jnp.where(same_plane(CP), m, 0.0).astype(BF)
-
-    t = t_ref[0]
-    f = f_ref[...]
-    pre = dot(a_ref[...], t, 1, 0) + dot(m_ref[...], f, 1, 0)
-    value, slope = gelu_both(pre)
-    out_ref[...] = value.astype(BF)
-    back = (cot_ref[...].astype(F32) * slope).astype(BF)
-    part = dot(t, back, 1, 1)
-    partm = dot(f, back, 1, 1)
-
-    @pl.when(step == 0)
-    def _():
-        acc_ref[...] = part
-        accm_ref[...] = partm
-
-    @pl.when(step > 0)
-    def _():
-        acc_ref[...] += part
-        accm_ref[...] += partm
-
-    @pl.when(step == steps - 1)
-    def _():
-        kept = jnp.where(same_plane(CP), accm_ref[...], 0.0)
-        kept = jnp.sum(kept.reshape(C, PL, CP), axis=1)
-        kept = jnp.concatenate([kept, jnp.zeros((CR - C, CP), F32)], 0)
-        hi, lo = split(kept)
-        y = dot(hi, e_ref[...], 1, 0) + dot(lo, e_ref[...], 1, 0)
-        yh = y.astype(BF).astype(F32)
-        y = yh + pltpu.roll(y - yh, 64, 1)
-        extra = jnp.concatenate([y[0:8], y[8:16], y[16:24], jnp.zeros((8, CP - 384), F32)], 1).astype(BF)
-        extra = extra.astype(F32)
-        for g in range(groups):
-            v = acc_ref[g * rows : (g + 1) * rows, :]
-            coded = (v * jnp.abs(v)) * (v * v)
-            o_ref[g] = jnp.concatenate([coded, extra], 0).astype(BF)
+    gid = gid_ref[0]
+    width = f_ref.shape[1] // parts
+    table_copy = pltpu.make_async_copy(t_hbm.at[gid], t_ref, t_sem.at[0])
+    table_copy.start()
+    copies = chunk_copies([(mixed_hbm, mixed_ref), (cot_hbm, cot_ref), (f_hbm, f_ref)], parts, sem)
+    for j in range(parts):
+        start_chunk(copies, j)
+    a_ref[...] = jnp.transpose(v_ref[...].astype(F32)).astype(BF)
+    table_copy.wait()
+    out = []
+    for j in range(parts):
+        at = slice(j * width, (j + 1) * width)
+        t = t_ref[:, at]
+        pre = dot(a_ref[...], t, 1, 0)
+        for copy in copies[j]:
+            copy.wait()
+        pre = pre + mixed_ref[:, :, :, at].reshape(CP, width)
+        value, slope = gelu_both(pre)
+        out_ref[:, at] = value.astype(BF)
+        out.append(pltpu.make_async_copy(out_ref.at[:, at], out_hbm.at[:, at], out_sem.at[j]))
+        out[j].start()
+        back = (cot_ref[:, at].astype(F32) * slope).astype(BF)
+        part = dot(t, back, 1, 1)
+        f = f_ref[:, at]
+        product = dot(half(f, 0), half(back, 0), 1, 1)
+        for h in range(1, PL // HP):
+            product = product + dot(half(f, h), half(back, h), 1, 1)
+        if j == 0:
+            acc_ref[...] = part
+            product_ref[...] = product
+        else:
+            acc_ref[...] += part
+            product_ref[...] += product
+    spectrum = acc_ref[...]
+    product = product_ref[...]
+
+    kept = jnp.where(same_plane(HALF), product, 0.0)
+    kept = jnp.sum(kept.reshape(C, HP, HALF), axis=1)
+    kept = jnp.concatenate([kept, jnp.zeros((CR - C, HALF), F32)], 0)
+    hi, lo = split(kept)
+    e = channel_of(128)
+    y = dot(hi, e, 1, 0) + dot(lo, e, 1, 0)
+    yh = y.astype(BF).astype(F32)
+    y = yh + pltpu.roll(y - yh, 64, 1)
+    extra = jnp.concatenate([y[0:8], y[8:16], y[16:24], jnp.zeros((8, CP - 384), F32)], 1)
+    for g in range(groups):
+        v = spectrum[g * rows : (g + 1) * rows, :]
+        coded = (v * jnp.abs(v)) * (v * v)
+        o_ref[g] = jnp.concatenate([coded, extra], 0).astype(BF)
+    for copy in out:
+        copy.wait()
 
 
 def grad_kernel(groups, rows, r_ref, s_ref, spread_ref, fold_ref, o_ref, g_ref, p_ref):
@@ -262,6 +320,20 @@
     o_ref[...] = (all_rows * jnp.abs(all_rows)) * (all_rows * all_rows)
 
 
+def sum_over_dp(coded, samples):
+    if samples & (samples - 1):
+        parts = lax.all_gather(coded, "dp", axis=0)
+        return jnp.sum(decode(parts), axis=0)
+    step = 1
+    while True:
+        other = lax.ppermute(coded, "dp", [(i, i ^ step) for i in range(samples)])
+        total = decode(coded) + decode(other)
+        step *= 2
+        if step >= samples:
+            return total
+        coded = encode(total)
+
+
 def compiler_params(mib):
     return pltpu.CompilerParams(vmem_limit_bytes=mib * 2**20)
 
@@ -276,78 +348,93 @@
     flat = fields.reshape(CP, cells)
     cot = cotangent.reshape(CP, cells)
     gid = (lax.axis_index("gx") * lax.axis_size("gy") + lax.axis_index("gy")).astype(jnp.int32).reshape(1)
-    width = min(512, cells)
-    steps = cells // width
-    whole = lambda shape: pl.BlockSpec(shape, lambda *_: (0,) * len(shape))
-    cells_spec = pl.BlockSpec((CP, width), lambda i, gid: (0, i))
-    table_spec = pl.BlockSpec((1, groups * rows, width), lambda i, gid: (gid[0], 0, i))
+    parts = max(1, cells // 512)
+    halves = max(1, cells // 1024)
+    high = groups * rows
+    vmem = pl.BlockSpec(memory_space=pltpu.VMEM)
+    smem = pl.BlockSpec(memory_space=pltpu.SMEM)
+
+    hbm = pl.BlockSpec(memory_space=pltpu.HBM)
+    mixed_shape = (C, PL // HP, HP, cells)
 
     sent = pl.pallas_call(
-        functools.partial(first_kernel, groups, rows, steps),
-        grid_spec=pltpu.PrefetchScalarGridSpec(
-            num_scalar_prefetch=1,
-            grid=(steps,),
-            in_specs=[cells_spec, table_spec],
-            out_specs=whole((groups, rows, CP)),
-            scratch_shapes=[pltpu.VMEM((groups * rows, CP), F32)],
-        ),
+        functools.partial(first_kernel, groups, rows, halves),
+        in_specs=[smem, hbm, hbm],
+        out_specs=hbm,
         out_shape=jax.ShapeDtypeStruct((groups, rows, CP), BF),
-        compiler_params=compiler_params(32),
+        scratch_shapes=[
+            pltpu.VMEM((CP, cells), BF),
+            pltpu.VMEM((high, cells), BF),
+            pltpu.VMEM((high, CP), F32),
+            pltpu.VMEM((groups, rows, CP), BF),
+            pltpu.SemaphoreType.DMA((2, halves)),
+            pltpu.SemaphoreType.DMA((groups,)),
+        ],
+        compiler_params=compiler_params(60),
         name="spectrum_parts",
     )(gid, flat, tables)
     got = lax.all_to_all(sent, GROUP, 0, 0, tiled=True)
+
+    mixed = pl.pallas_call(
+        functools.partial(cell_mix_kernel, parts),
+        in_specs=[hbm, vmem],
+        out_specs=hbm,
+        out_shape=jax.ShapeDtypeStruct(mixed_shape, F32),
+        scratch_shapes=[
+            pltpu.VMEM((CP, cells), BF),
+            pltpu.VMEM(mixed_shape, F32),
+            pltpu.SemaphoreType.DMA((1, parts)),
+            pltpu.SemaphoreType.DMA((parts,)),
+        ],
+        compiler_params=compiler_params(60),
+        cost_estimate=pl.CostEstimate(flops=2 * 2 * HALF * HALF * cells, bytes_accessed=8 * 2**20, transcendentals=0),
+        name="cell_mixing",
+    )(flat, mix_weight)
 
     weights = spectral_weight.reshape(per, 2 * C * C)
     vals, spec = pl.pallas_call(
         functools.partial(mix_kernel, groups, rows),
         out_shape=(jax.ShapeDtypeStruct((rows, CP), BF), jax.ShapeDtypeStruct((2, CR * PL, 128), F32)),
         scratch_shapes=[pltpu.VMEM((C * C, 128), F32), pltpu.VMEM((C * C, 128), F32), pltpu.VMEM((CP, 128), F32)],
-        compiler_params=compiler_params(32),
+        compiler_params=compiler_params(8),
         name="mode_mixing",
     )(got, weights, spread, wsel, collect)
     all_vals = lax.all_gather(vals, GROUP, axis=0, tiled=True)
 
     output, sent = pl.pallas_call(
-        functools.partial(main_kernel, groups, rows, steps),
-        grid_spec=pltpu.PrefetchScalarGridSpec(
-            num_scalar_prefetch=1,
-            grid=(steps,),
-            in_specs=[
-                cells_spec,
-                cells_spec,
-                table_spec,
-                whole((groups * rows, CP)),
-                whole((C, C)),
-                whole((CP, 128)),
-            ],
-            out_specs=[cells_spec, whole((groups, rows + 8, CP))],
-            scratch_shapes=[
-                pltpu.VMEM((CP, groups * rows), BF),
-                pltpu.VMEM((CP, CP), BF),
-                pltpu.VMEM((groups * rows, CP), F32),
-                pltpu.VMEM((CP, CP), F32),
-            ],
-        ),
+        functools.partial(main_kernel, groups, rows, halves),
+        in_specs=[smem, hbm, hbm, hbm, hbm, vmem],
+        out_specs=(hbm, vmem),
         out_shape=(
             jax.ShapeDtypeStruct((CP, cells), BF),
             jax.ShapeDtypeStruct((groups, rows + 8, CP), BF),
         ),
+        scratch_shapes=[
+            pltpu.VMEM((high, cells), BF),
+            pltpu.VMEM(mixed_shape, F32),
+            pltpu.VMEM((CP, cells), BF),
+            pltpu.VMEM((CP, cells), BF),
+            pltpu.VMEM((CP, cells), BF),
+            pltpu.VMEM((CP, high), BF),
+            pltpu.VMEM((high, CP), F32),
+            pltpu.VMEM((HALF, HALF), F32),
+            pltpu.SemaphoreType.DMA((1,)),
+            pltpu.SemaphoreType.DMA((3, halves)),
+            pltpu.SemaphoreType.DMA((halves,)),
+        ],
         compiler_params=compiler_params(48),
         name="cells",
-    )(gid, flat, cot, tables, all_vals, mix_weight, expander())
+    )(gid, tables, mixed, cot, flat, all_vals)
     got = lax.all_to_all(sent, GROUP, 0, 0, tiled=True)
 
     coded = pl.pallas_call(
         functools.partial(grad_kernel, groups, rows),
         out_shape=jax.ShapeDtypeStruct((rows + 8, 512), F32),
         scratch_shapes=[pltpu.VMEM((CP, 128), F32), pltpu.VMEM((C * CR, 256), F32)],
-        compiler_params=compiler_params(32),
+        compiler_params=compiler_params(8),
         name="mode_grads",
     )(got, spec, spread, fold)
-    coded = coded.astype(BF)
-    total = decode(coded)
-    for k in range(1, samples):
-        total = total + decode(lax.ppermute(coded, "dp", [(i, (i + k) % samples) for i in range(samples)]))
+    total = sum_over_dp(coded.astype(BF), samples)
 
     grads = total[: 2 * per, : C * CR].reshape(2, per, C, CR)[..., :C]
     spectral_grad = jnp.transpose(grads, (1, 0, 3, 2)) * (1.0 / math.sqrt(samples * PL))

time: 92.3 us -> 78 us (0.85)
  local copies, waits for them, and re-layouts: 15.5 us -> 2.28 us
  Pallas kernels: 25.6 us -> 29.2 us
  starting transfers between devices: 11.9 us -> 9.48 us
  waiting for transfers between devices: 11.2 us -> 8.89 us
    unnamed x21 -> x13, local copies, waits for them, and re-layouts: 11.5 us -> 0.93 us
    all_to_all x1, waiting for transfers between devices: 7.55 us -> 3.28 us  [local(): got = lax.all_to_all(sent, GROUP, 0, 0, tiled=True)]
    pallas_call x2 -> x3, Pallas kernels: 19.2 us -> 22.7 us  [the longest x1 10.6 us: local(): pl.pallas_call(functools.partial(main_kernel, groups, rows, halves), in_s...]
    reshape x2, local copies, waits for them, and re-layouts: 3.57 us -> 0.91 us  [local(): weights = spectral_weight.reshape(per, 2 * C * C)]
    ppermute x3 -> x2, starting transfers between devices: 6.48 us -> 4.3 us  [sum_over_dp(): other = lax.ppermute(coded, 'dp', [(i, i ^ step) for i in range(samples)])]
    ppermute x3 -> x2, waiting for transfers between devices: 3.61 us -> 5.61 us  [sum_over_dp(): other = lax.ppermute(coded, 'dp', [(i, i ^ step) for i in range(samples)])]
  transfers between devices with their start and end apart: 4 -> 3, of which waited for: 4 -> 3; matrix products, arithmetic and copies ran while one was open for 4% -> 1% of each run, Pallas kernels for 0% -> 9%
where the time goes in v2:
time: 78 us; the launch traced here: 77.6 us
  Pallas kernels  29.2 us (37%)
  blocking collectives  26 us (33%)
  starting transfers between devices  9.48 us (12%)
  waiting for transfers between devices  8.89 us (11%)
  local copies, waits for them, and re-layouts  2.28 us (3%)
  other arithmetic  1.05 us (1%)
  between operations  0.79 us (1%)
    all_to_all x1, blocking collectives, local(): got = lax.all_to_all(sent, GROUP, 0, 0, tiled=True)  15.5 us
    pallas_call x1, Pallas kernels, local(): pl.pallas_call(functools.partial(main_kernel, groups, rows, halves), in_s...  10.6 us
    all_gather x1, blocking collectives, local(): all_vals = lax.all_gather(vals, GROUP, axis=0, tiled=True)  10.5 us
    pallas_call x1, Pallas kernels, local(): pl.pallas_call(functools.partial(cell_mix_kernel, parts), in_specs=[hbm,...  6.87 us
    ppermute x2, waiting for transfers between devices, sum_over_dp(): other = lax.ppermute(coded, 'dp', [(i, i ^ step) for i in range(samples)])  5.61 us
    pallas_call x1, Pallas kernels, local(): pl.pallas_call(functools.partial(first_kernel, groups, rows, halves), in_...  5.23 us
    all_to_all x1, starting transfers between devices, local(): got = lax.all_to_all(sent, GROUP, 0, 0, tiled=True)  5.18 us
    ppermute x2, starting transfers between devices, sum_over_dp(): other = lax.ppermute(coded, 'dp', [(i, i ^ step) for i in range(samples)])  4.3 us
  transfers between devices with their start and end apart: 3, of which 3 were waited for; matrix products, arithmetic and copies ran while one was open for 1% of the time, Pallas kernels for 9%

profile of v2, /device:TPU:0, one launch (start us, length us, event | category | flops | bytes accessed | tf_op | source)
XLA Modules:
  0.0 77.6 jit_solution(4228607642552110191)
XLA Ops:
  0.6 5.2 %spectrum_parts.1 = bf16[8,72,640]{2,1,0:T(8,128)(2,1)} custom-call(s32[1]{0:T(128)} %bitcast.gid_ref, bf16[640,2048]{1,0:T(8,128)(2,1)} %bitcast.15, bf16[8,576,2048]{2,1,0:T(8,128)(2,1)} %constant.27.clone.t_hbm), custom_call_target="tpu_custom_call" | custom-call | tf_op jit(solution)/shard_map/spectrum_parts/pallas_call | solution.py:360
  5.9 5.2 %all-to-all-start = ((bf16[8,72,640]{2,1,0:T(8,128)(2,1)}), bf16[8,72,640]{2,1,0:T(8,128)(2,1)S(1)}, u32[]{:S(2)}, u32[]{:S(2)}) async-start(bf16[8,72,640]{2,1,0:T(8,128)(2,1)} %spectrum_parts.1), calls=%async_computation | async-start | bytes 1474560 | tf_op jit(solution)/shard_map/all_to_all | solution.py:376
  11.1 0.5 copy.18
  11.6 0.4 reshape.38.w_ref
  12.0 0.0 copy-start.1
  12.0 0.0 copy-start.3
  12.0 6.9 %cell_mixing.1.mixed_hbm = f32[20,2,16,2048]{3,2,1,0:T(8,128)} custom-call(bf16[640,2048]{1,0:T(8,128)(2,1)} %bitcast.16, bf16[20,20]{1,0:T(8,128)(2,1)} %mix_ref.1), custom_call_target="tpu_custom_call" | custom-call | flops 838860800 | bytes 8388608 | tf_op jit(solution)/shard_map/cell_mixing/pallas_call | solution.py:378
  18.9 3.3 %all-to-all-done.r_ref = bf16[8,72,640]{2,1,0:T(8,128)(2,1)S(1)} async-done(((bf16[8,72,640]{2,1,0:T(8,128)(2,1)}), bf16[8,72,640]{2,1,0:T(8,128)(2,1)S(1)}, u32[]{:S(2)}, u32[]{:S(2)}) %all-to-all-start) | async-done | bytes 737312 | tf_op jit(solution)/shard_map/all_to_all | solution.py:376
  22.2 2.4 %mode_mixing.1 = (bf16[72,640]{1,0:T(8,128)(2,1)S(1)}, f32[2,768,128]{2,1,0:T(8,128)S(1)}) custom-call(bf16[8,72,640]{2,1,0:T(8,128)(2,1)S(1)} %all-to-all-done.r_ref, bf16[36,800]{1,0:T(8,128)(2,1)S(1)} %reshape.38.w_ref, bf16[144,256]{1,0:T(8,128)(2,1)S(1)} %copy-done.1, bf16[36,128]{1,0:T(8,128)(2,1)S(1)} %copy-done.4, bf16[72,256]{1,0:T(8,128)(2,1)S(1)} %copy-done.3), custom_call_target="tpu_custom_call" | custom-call | tf_op jit(solution)/shard_map/mode_mixing/pallas_call | solution.py:395
  24.6 10.5 %all_gather.3.v_ref = bf16[576,640]{1,0:T(8,128)(2,1)S(1)} all-gather(bf16[72,640]{1,0:T(8,128)(2,1)S(1)} %get-tuple-element.7), channel_id=1, replica_groups=mesh['dp'=4,'gx'=2,'gy'=4] {'gx','gy'}, dimensions={0}, use_global_device_ids=true | all-gather | bytes 829440 | tf_op jit(solution)/shard_map/all_gather | solution.py:402
  35.1 10.6 %cells.1 = (bf16[640,2048]{1,0:T(8,128)(2,1)}, bf16[8,80,640]{2,1,0:T(8,128)(2,1)S(1)}) custom-call(s32[1]{0:T(128)} %bitcast.gid_ref, bf16[8,576,2048]{2,1,0:T(8,128)(2,1)} %constant.27.clone.t_hbm, f32[20,2,16,2048]{3,2,1,0:T(8,128)} %cell_mixing.1.mixed_hbm, bf16[640,2048]{1,0:T(8,128)(2,1)S(1)} %bitcast.14, bf16[640,2048]{1,0:T(8,128)(2,1)} %bitcast.17, ...), custom_call_target="tpu_custom_call" | custom-call | tf_op jit(solution)/shard_map/cells/pallas_call | solution.py:404
  45.7 15.5 %all_to_all.10.r_ref = bf16[8,80,640]{2,1,0:T(8,128)(2,1)S(1)} all-to-all(bf16[8,80,640]{2,1,0:T(8,128)(2,1)S(1)} %get-tuple-element.9), channel_id=1, replica_groups=mesh['dp'=4,'gx'=2,'gy'=4] {'gx','gy'}, dimensions={0} | all-to-all | bytes 1638400 | tf_op jit(solution)/shard_map/all_to_all | solution.py:428
  61.2 4.0 %mode_grads.1 = f32[80,512]{1,0:T(8,128)S(1)} custom-call(bf16[8,80,640]{2,1,0:T(8,128)(2,1)S(1)} %all_to_all.10.r_ref, f32[2,768,128]{2,1,0:T(8,128)S(1)} %get-tuple-element.10.s_ref, bf16[144,256]{1,0:T(8,128)(2,1)S(1)} %copy-done.1, bf16[72,512]{1,0:T(8,128)(2,1)S(1)} %copy-done.2), custom_call_target="tpu_custom_call" | custom-call | tf_op jit(solution)/shard_map/mode_grads/pallas_call | solution.py:430
  65.3 1.6 %collective-permute-start = (bf16[80,512]{1,0:T(8,128)(2,1)S(1)}, bf16[80,512]{1,0:T(8,128)(2,1)S(1)}, u32[]{:S(2)}, u32[]{:S(2)}) collective-permute-start(bf16[80,512]{1,0:T(8,128)(2,1)S(1)} %convert_element_type.18), channel_id=1, source_target_pairs={{0,8},{8,0},{16,24},{24,16},{1,9},{9,1},{17,25},{25,17},{2,10},{10... | collective-permute-start | bytes 245768 | tf_op jit(solution)/shard_map/ppermute | solution.py:329
  66.9 2.9 %collective-permute-done = bf16[80,512]{1,0:T(8,128)(2,1)S(1)} collective-permute-done((bf16[80,512]{1,0:T(8,128)(2,1)S(1)}, bf16[80,512]{1,0:T(8,128)(2,1)S(1)}, u32[]{:S(2)}, u32[]{:S(2)}) %collective-permute-start) | collective-permute-done | bytes 81952 | tf_op jit(solution)/shard_map/ppermute | solution.py:329
  69.8 0.1 fusion.20
  69.9 2.7 %collective-permute-start.1 = (bf16[80,512]{1,0:T(8,128)(2,1)S(1)}, bf16[80,512]{1,0:T(8,128)(2,1)S(1)}, u32[]{:S(2)}, u32[]{:S(2)}) collective-permute-start(bf16[80,512]{1,0:T(8,128)(2,1)S(1)} %fusion.20), channel_id=1, source_target_pairs={{0,16},{8,24},{16,0},{24,8},{1,17},{9,25},{17,1},{25,9},{2,18},{10... | collective-permute-start | bytes 245768 | tf_op jit(solution)/shard_map/ppermute | solution.py:329
  72.6 2.7 %collective-permute-done.1 = bf16[80,512]{1,0:T(8,128)(2,1)S(1)} collective-permute-done((bf16[80,512]{1,0:T(8,128)(2,1)S(1)}, bf16[80,512]{1,0:T(8,128)(2,1)S(1)}, u32[]{:S(2)}, u32[]{:S(2)}) %collective-permute-start.1) | collective-permute-done | bytes 81952 | tf_op jit(solution)/shard_map/ppermute | solution.py:329
  75.3 0.1 fusion.14
  75.5 0.6 slice_multiply_fusion.1
  76.1 0.1 copy.16
  76.2 0.3 reshape.35
  76.5 0.2 fusion
  76.7 0.9 %copy.17 = f32[36,2,20,20]{0,1,3,2:T(2,128)} copy(f32[36,2,20,20]{0,1,2,3:T(2,128)S(1)} %fusion) | data formatting | bytes 230400
  (14 shorter events, 0.1 us)
Async XLA Ops:
  0.6 10.4 %copy-start.5 = (bf16[36,2,20,20]{0,1,3,2:T(2,128)(2,1)S(1)}, bf16[36,2,20,20]{0,1,3,2:T(2,128)(2,1)}, u32[]{:S(2)}) copy-start(bf16[36,2,20,20]{0,1,3,2:T(2,128)(2,1)} %param.12) | copy-start | bytes 172804
  5.9 16.3 %all-to-all-start = ((bf16[8,72,640]{2,1,0:T(8,128)(2,1)}), bf16[8,72,640]{2,1,0:T(8,128)(2,1)S(1)}, u32[]{:S(2)}, u32[]{:S(2)}) async-start(bf16[8,72,640]{2,1,0:T(8,128)(2,1)} %spectrum_parts.1), calls=%async_computation | async-start | bytes 1474560 | tf_op jit(solution)/shard_map/all_to_all | solution.py:376
  12.0 10.2 %copy-start.1 = (bf16[144,256]{1,0:T(8,128)(2,1)S(1)}, bf16[144,256]{1,0:T(8,128)(2,1)}, u32[]{:S(2)}) copy-start(bf16[144,256]{1,0:T(8,128)(2,1)} %constant.28.clone.spread_ref) | copy-start | bytes 221188
  12.0 10.2 %copy-start.3 = (bf16[72,256]{1,0:T(8,128)(2,1)S(1)}, bf16[72,256]{1,0:T(8,128)(2,1)}, u32[]{:S(2)}) copy-start(bf16[72,256]{1,0:T(8,128)(2,1)} %constant.30.clone.collect_ref) | copy-start | bytes 110596
  12.0 10.2 %copy-start.4 = (bf16[36,128]{1,0:T(8,128)(2,1)S(1)}, bf16[36,128]{1,0:T(8,128)(2,1)}, u32[]{:S(2)}) copy-start(bf16[36,128]{1,0:T(8,128)(2,1)} %constant.29.clone.wsel_ref) | copy-start | bytes 27652
  12.0 23.1 %copy-start = (bf16[1,20,32,2048]{3,2,1,0:T(8,128)(2,1)S(1)}, bf16[1,20,32,2048]{3,2,1,0:T(8,128)(2,1)}, u32[]{:S(2)}) copy-start(bf16[1,20,32,2048]{3,2,1,0:T(8,128)(2,1)} %param.10) | copy-start | bytes 7864324
  35.1 26.1 %copy-start.2 = (bf16[72,512]{1,0:T(8,128)(2,1)S(1)}, bf16[72,512]{1,0:T(8,128)(2,1)}, u32[]{:S(2)}) copy-start(bf16[72,512]{1,0:T(8,128)(2,1)} %constant.31.clone.fold_ref) | copy-start | bytes 221188
  65.3 4.5 %collective-permute-start = (bf16[80,512]{1,0:T(8,128)(2,1)S(1)}, bf16[80,512]{1,0:T(8,128)(2,1)S(1)}, u32[]{:S(2)}, u32[]{:S(2)}) collective-permute-start(bf16[80,512]{1,0:T(8,128)(2,1)S(1)} %convert_element_type.18), channel_id=1, source_target_pairs={{0,8},{8,0},{16,24},{24,16},{1,9},{9,1},{17,25},{25,17},{2,10},{10... | collective-permute-start | bytes 245768 | tf_op jit(solution)/shard_map/ppermute | solution.py:329
  69.9 5.4 %collective-permute-start.1 = (bf16[80,512]{1,0:T(8,128)(2,1)S(1)}, bf16[80,512]{1,0:T(8,128)(2,1)S(1)}, u32[]{:S(2)}, u32[]{:S(2)}) collective-permute-start(bf16[80,512]{1,0:T(8,128)(2,1)S(1)} %fusion.20), channel_id=1, source_target_pairs={{0,16},{8,24},{16,0},{24,8},{1,17},{9,25},{17,1},{25,9},{2,18},{10... | collective-permute-start | bytes 245768 | tf_op jit(solution)/shard_map/ppermute | solution.py:329

commit v3 on v2

--- a/solution.py
+++ b/solution.py
@@ -88,7 +88,10 @@
 
 
 def decode(y):
-    y = y.astype(F32)
+    return root(y.astype(F32))
+
+
+def root(y):
     z = lax.rsqrt(jnp.maximum(jnp.abs(y), 1e-36))
     return ((y * z) * z) * lax.rsqrt(z)
 
@@ -268,70 +271,101 @@
     y = dot(hi, e, 1, 0) + dot(lo, e, 1, 0)
     yh = y.astype(BF).astype(F32)
     y = yh + pltpu.roll(y - yh, 64, 1)
-    extra = jnp.concatenate([y[0:8], y[8:16], y[16:24], jnp.zeros((8, CP - 384), F32)], 1)
+    extra = y[0:8] + pltpu.roll(y[8:16], C, 1) + pltpu.roll(y[16:24], 2 * C, 1)
     for g in range(groups):
         v = spectrum[g * rows : (g + 1) * rows, :]
         coded = (v * jnp.abs(v)) * (v * v)
-        o_ref[g] = jnp.concatenate([coded, extra], 0).astype(BF)
+        tiles = [coded[:, 128 * i : 128 * (i + 1)] for i in range(CP // 128)]
+        o_ref[g] = jnp.concatenate(tiles + [extra], 0).astype(BF)
     for copy in out:
         copy.wait()
 
 
+def payload_rows(rows):
+    return round_up(3 * rows + 16, 16)
+
+
 def grad_kernel(groups, rows, r_ref, s_ref, spread_ref, fold_ref, o_ref, g_ref, p_ref):
+    high = rows * CP // 128
     total = None
     extra = None
     for g in range(groups):
         block = r_ref[g].astype(F32)
-        y = block[0:rows]
-        z = lax.rsqrt(jnp.maximum(jnp.abs(y), 1e-36))
-        y = ((y * z) * z) * lax.rsqrt(z)
+        y = root(block[0:high])
         total = y if total is None else total + y
-        x = block[rows : rows + 8]
+        x = block[high : high + 8]
         extra = x if extra is None else extra + x
     total = total * (1.0 / (SCALE * math.sqrt(MODES)))
+    total = jnp.concatenate([total[i * rows : (i + 1) * rows] for i in range(CP // 128)], 1)
     hi, lo = split(total)
     both = jnp.concatenate([hi.astype(F32), lo.astype(F32)], 0).astype(BF)
-    g_ref[...] = dot(both, spread_ref[:, 0:128], 0, 0)
+    g_ref[0:CP, :] = dot(both, spread_ref[:, 0:128], 0, 0)
+    g_ref[CP:, :] = jnp.zeros((CR * PL - CP, 128), F32)
 
     def some(block, _):
-        base = block * 4
-        one = [jnp.zeros((CR, 128), F32)] * 4
-        two = [jnp.zeros((CR, 128), F32)] * 4
+        base = block * 5
+        one = [jnp.zeros((CR, 128), F32)] * 5
+        two = [jnp.zeros((CR, 128), F32)] * 5
         for p in range(PL):
-            s = s_ref[0, pl.ds(p, CR, stride=PL), :]
-            t = s_ref[1, pl.ds(p, CR, stride=PL), :]
-            for k in range(4):
-                g = g_ref[pl.ds((base + k) * PL + p, 1), :]
-                one[k] = one[k] + s * g
-                two[k] = two[k] + t * g
-        for k in range(4):
+            g = g_ref[pl.ds(p, CR, stride=PL), :]
+            for k in range(5):
+                one[k] = one[k] + s_ref[0, pl.ds((base + k) * PL + p, 1), :] * g
+                two[k] = two[k] + s_ref[1, pl.ds((base + k) * PL + p, 1), :] * g
+        for k in range(5):
             at = pl.multiple_of((base + k) * CR, CR)
             p_ref[pl.ds(at, CR), 0:128] = one[k]
             p_ref[pl.ds(at, CR), 128:256] = two[k]
         return 0
 
-    lax.fori_loop(0, C // 4, some, 0)
-    hi, lo = split(p_ref[...])
+    lax.fori_loop(0, C // 5, some, 0)
+    products = jnp.concatenate([p_ref[c * CR : c * CR + C, :] for c in range(C)], 0)
+    hi, lo = split(products)
     grads = dot(fold_ref[...], jnp.concatenate([hi, lo], 1), 1, 1)
-    grads = jnp.concatenate([grads, jnp.zeros((rows, 512 - C * CR), F32)], 1)
-    extra = extra[:, 0:512]
-    extra = extra + pltpu.roll(extra, 512 - 64, 1)
-    all_rows = jnp.concatenate([grads, extra], 0)
-    o_ref[...] = (all_rows * jnp.abs(all_rows)) * (all_rows * all_rows)
+    tail = jnp.concatenate([grads[:, 384:], jnp.zeros((rows, 512 - C * C), F32)], 1)
+    lane = lax.broadcasted_iota(jnp.int32, (8, 128), 1)
+    extra = extra + pltpu.roll(extra, 64, 1)
+    extra = jnp.where(lane < 3 * C, extra, 0.0)
+    strip = [jnp.zeros((8, 128), F32), pltpu.roll(extra, 64, 1)]
+    for i in range(rows // 8):
+        piece = tail[8 * i : 8 * i + 8]
+        strip[i // 8] = strip[i // 8] + (pltpu.roll(piece, 16 * (i % 8), 1) if i % 8 else piece)
+    fill = jnp.zeros((payload_rows(rows) - 3 * rows - 16, 128), F32)
+    parts = [grads[:, 128 * i : 128 * (i + 1)] for i in range(3)] + strip
+    if fill.shape[0]:
+        parts.append(fill)
+    o_ref[...] = encode(jnp.concatenate(parts, 0))
+
+
+def last_kernel(rows, per, samples, own_ref, other_ref, grad_ref, mix_ref):
+    total = decode(own_ref[...])
+    total = total + decode(other_ref[...])
+    lane = lax.broadcasted_iota(jnp.int32, (8, 128), 1)
+    strip = [total[3 * rows : 3 * rows + 8], total[3 * rows + 8 : 3 * rows + 16]]
+    tail = []
+    for i in range(rows // 8):
+        piece = pltpu.roll(strip[i // 8], 128 - 16 * (i % 8), 1) if i % 8 else strip[i // 8]
+        tail.append(jnp.where(lane < C * C - 384, piece, 0.0))
+    grads = jnp.concatenate([total[i * rows : (i + 1) * rows] for i in range(3)] + [jnp.concatenate(tail, 0)], 1)
+    grads = jnp.transpose(grads * (1.0 / math.sqrt(samples * PL)))[0 : C * C]
+    grad_ref[:, 0, :] = grads[:, 0:per]
+    grad_ref[:, 1, :] = grads[:, per : 2 * per]
+    mix = strip[1] * (1.0 / math.sqrt(samples * PL * NX * NY))
+    mix_ref[0:8, :] = pltpu.roll(mix, 64, 1)[:, 0:C]
+    mix_ref[8:16, :] = pltpu.roll(mix, 64 - C, 1)[:, 0:C]
+    mix_ref[16:C, :] = pltpu.roll(mix, 64 - 2 * C, 1)[0 : C - 16, 0:C]
 
 
 def sum_over_dp(coded, samples):
-    if samples & (samples - 1):
-        parts = lax.all_gather(coded, "dp", axis=0)
-        return jnp.sum(decode(parts), axis=0)
+    if samples & (samples - 1) or samples == 1:
+        total = jnp.sum(decode(lax.all_gather(coded, "dp", axis=0)), axis=0)
+        return encode(total), jnp.zeros_like(coded)
     step = 1
     while True:
         other = lax.ppermute(coded, "dp", [(i, i ^ step) for i in range(samples)])
-        total = decode(coded) + decode(other)
         step *= 2
         if step >= samples:
-            return total
-        coded = encode(total)
+            return coded, other
+        coded = encode(decode(coded) + decode(other))
 
 
 def compiler_params(mib):
@@ -407,7 +441,7 @@
         out_specs=(hbm, vmem),
         out_shape=(
             jax.ShapeDtypeStruct((CP, cells), BF),
-            jax.ShapeDtypeStruct((groups, rows + 8, CP), BF),
+            jax.ShapeDtypeStruct((groups, rows * CP // 128 + 8, 128), BF),
         ),
         scratch_shapes=[
             pltpu.VMEM((high, cells), BF),
@@ -429,18 +463,19 @@
 
     coded = pl.pallas_call(
         functools.partial(grad_kernel, groups, rows),
-        out_shape=jax.ShapeDtypeStruct((rows + 8, 512), F32),
-        scratch_shapes=[pltpu.VMEM((CP, 128), F32), pltpu.VMEM((C * CR, 256), F32)],
+        out_shape=jax.ShapeDtypeStruct((payload_rows(rows), 128), BF),
+        scratch_shapes=[pltpu.VMEM((CR * PL, 128), F32), pltpu.VMEM((C * CR, 256), F32)],
         compiler_params=compiler_params(8),
         name="mode_grads",
     )(got, spec, spread, fold)
-    total = sum_over_dp(coded.astype(BF), samples)
-
-    grads = total[: 2 * per, : C * CR].reshape(2, per, C, CR)[..., :C]
-    spectral_grad = jnp.transpose(grads, (1, 0, 3, 2)) * (1.0 / math.sqrt(samples * PL))
-    extra = total[rows:, :384].reshape(8, 3, 128)[:, :, :C]
-    mixing = jnp.transpose(extra, (1, 0, 2)).reshape(24, C)[:C]
-    mixing_grad = mixing * (1.0 / math.sqrt(samples * PL * NX * NY))
+    own, other = sum_over_dp(coded, samples)
+    grads, mixing_grad = pl.pallas_call(
+        functools.partial(last_kernel, rows, per, samples),
+        out_shape=(jax.ShapeDtypeStruct((C * C, 2, per), F32), jax.ShapeDtypeStruct((C, C), F32)),
+        compiler_params=compiler_params(8),
+        name="gradients_out",
+    )(own, other)
+    spectral_grad = jnp.transpose(grads.reshape(C, C, 2, per), (3, 2, 0, 1))
     return (output.reshape(1, C, PL, cells), spectral_grad, mixing_grad)
 
 

time: 78 us -> 74.1 us (0.950)
  blocking collectives: 26 us -> 24.6 us
  local copies, waits for them, and re-layouts: 2.28 us -> 0.95 us
  other arithmetic: 1.05 us -> 0.1 us
    pallas_call x0 -> x1, Pallas kernels: none -> 1.49 us  [local(): pl.pallas_call(functools.partial(last_kernel, rows, per, samples), out_sh...]
    all_to_all x1, blocking collectives: 15.5 us -> 14.1 us  [local(): got = lax.all_to_all(sent, GROUP, 0, 0, tiled=True)]
    pallas_call x1, Pallas kernels: 4.01 us -> 2.84 us  [local(): pl.pallas_call(functools.partial(grad_kernel, groups, rows), out_shape=ja...]
    unnamed x13 -> x12, local copies, waits for them, and re-layouts: 0.93 us -> 0.03 us
    mul x2 -> x0, other arithmetic: 0.82 us -> none  [the longest x1 0.6 us: local(): mixing_grad = mixing * (1.0 / math.sqrt(samples * PL * NX * NY))]
where the time goes in v3:
time: 74.1 us; the launch traced here: 73.7 us
  Pallas kernels  29.5 us (40%)
  blocking collectives  24.6 us (33%)
  starting transfers between devices  9.48 us (13%)
  waiting for transfers between devices  8.4 us (11%)
  local copies, waits for them, and re-layouts  0.95 us (1%)
    all_to_all x1, blocking collectives, local(): got = lax.all_to_all(sent, GROUP, 0, 0, tiled=True)  14.1 us
    pallas_call x1, Pallas kernels, local(): pl.pallas_call(functools.partial(main_kernel, groups, rows, halves), in_s...  10.6 us
    all_gather x1, blocking collectives, local(): all_vals = lax.all_gather(vals, GROUP, axis=0, tiled=True)  10.5 us
    pallas_call x1, Pallas kernels, local(): pl.pallas_call(functools.partial(cell_mix_kernel, parts), in_specs=[hbm,...  6.92 us
    pallas_call x1, Pallas kernels, local(): pl.pallas_call(functools.partial(first_kernel, groups, rows, halves), in_...  5.23 us
    all_to_all x1, starting transfers between devices, local(): got = lax.all_to_all(sent, GROUP, 0, 0, tiled=True)  5.18 us
    ppermute x2, waiting for transfers between devices, sum_over_dp(): other = lax.ppermute(coded, 'dp', [(i, i ^ step) for i in range(samples)])  5.17 us
    ppermute x2, starting transfers between devices, sum_over_dp(): other = lax.ppermute(coded, 'dp', [(i, i ^ step) for i in range(samples)])  4.3 us
  transfers between devices with their start and end apart: 3, of which 3 were waited for; matrix products, arithmetic and copies ran while one was open for 1% of the time, Pallas kernels for 9%

profile of v3, /device:TPU:0, one launch (start us, length us, event | category | flops | bytes accessed | tf_op | source)
XLA Modules:
  0.0 73.7 jit_solution(10030321381811845628)
XLA Ops:
  0.6 0.0 copy-start.5
  0.6 5.2 %spectrum_parts.1 = bf16[8,72,640]{2,1,0:T(8,128)(2,1)} custom-call(s32[1]{0:T(128)} %bitcast.gid_ref, bf16[640,2048]{1,0:T(8,128)(2,1)} %bitcast.8, bf16[8,576,2048]{2,1,0:T(8,128)(2,1)} %constant.23.clone.t_hbm), custom_call_target="tpu_custom_call" | custom-call | tf_op jit(solution)/shard_map/spectrum_parts/pallas_call | solution.py:394
  5.9 5.2 %all-to-all-start = ((bf16[8,72,640]{2,1,0:T(8,128)(2,1)}), bf16[8,72,640]{2,1,0:T(8,128)(2,1)S(1)}, u32[]{:S(2)}, u32[]{:S(2)}) async-start(bf16[8,72,640]{2,1,0:T(8,128)(2,1)} %spectrum_parts.1), calls=%async_computation | async-start | bytes 1474560 | tf_op jit(solution)/shard_map/all_to_all | solution.py:410
  11.1 0.0 copy-done.5
  11.1 0.5 copy.15
  11.6 0.4 reshape.30.w_ref
  12.0 0.0 copy-start.1
  12.0 0.0 copy-start.3
  12.0 0.0 copy-start.4
  12.0 0.0 copy-start
  12.0 6.9 %cell_mixing.1.mixed_hbm = f32[20,2,16,2048]{3,2,1,0:T(8,128)} custom-call(bf16[640,2048]{1,0:T(8,128)(2,1)} %bitcast.9, bf16[20,20]{1,0:T(8,128)(2,1)} %mix_ref.1), custom_call_target="tpu_custom_call" | custom-call | flops 838860800 | bytes 8388608 | tf_op jit(solution)/shard_map/cell_mixing/pallas_call | solution.py:412
  19.0 3.2 %all-to-all-done.r_ref = bf16[8,72,640]{2,1,0:T(8,128)(2,1)S(1)} async-done(((bf16[8,72,640]{2,1,0:T(8,128)(2,1)}), bf16[8,72,640]{2,1,0:T(8,128)(2,1)S(1)}, u32[]{:S(2)}, u32[]{:S(2)}) %all-to-all-start) | async-done | bytes 737312 | tf_op jit(solution)/shard_map/all_to_all | solution.py:410
  22.2 0.0 copy-done.4
  22.2 2.4 %mode_mixing.1 = (bf16[72,640]{1,0:T(8,128)(2,1)S(1)}, f32[2,768,128]{2,1,0:T(8,128)S(1)}) custom-call(bf16[8,72,640]{2,1,0:T(8,128)(2,1)S(1)} %all-to-all-done.r_ref, bf16[36,800]{1,0:T(8,128)(2,1)S(1)} %reshape.30.w_ref, bf16[144,256]{1,0:T(8,128)(2,1)S(1)} %copy-done.1, bf16[36,128]{1,0:T(8,128)(2,1)S(1)} %copy-done.4, bf16[72,256]{1,0:T(8,128)(2,1)S(1)} %copy-done.3), custom_call_target="tpu_custom_call" | custom-call | tf_op jit(solution)/shard_map/mode_mixing/pallas_call | solution.py:429
  24.6 10.5 %all_gather.3.v_ref = bf16[576,640]{1,0:T(8,128)(2,1)S(1)} all-gather(bf16[72,640]{1,0:T(8,128)(2,1)S(1)} %get-tuple-element.9), channel_id=1, replica_groups=mesh['dp'=4,'gx'=2,'gy'=4] {'gx','gy'}, dimensions={0}, use_global_device_ids=true | all-gather | bytes 829440 | tf_op jit(solution)/shard_map/all_gather | solution.py:436
  35.1 10.6 %cells.1 = (bf16[640,2048]{1,0:T(8,128)(2,1)}, bf16[8,368,128]{2,1,0:T(8,128)(2,1)S(1)}) custom-call(s32[1]{0:T(128)} %bitcast.gid_ref, bf16[8,576,2048]{2,1,0:T(8,128)(2,1)} %constant.23.clone.t_hbm, f32[20,2,16,2048]{3,2,1,0:T(8,128)} %cell_mixing.1.mixed_hbm, bf16[640,2048]{1,0:T(8,128)(2,1)S(1)} %bitcast.7, bf16[640,2048]{1,0:T(8,128)(2,1)} %bitcast.10, ...), custom_call_target="tpu_custom_call" | custom-call | tf_op jit(solution)/shard_map/cells/pallas_call | solution.py:438
  45.7 14.1 %all_to_all.10.r_ref = bf16[8,368,128]{2,1,0:T(8,128)(2,1)S(1)} all-to-all(bf16[8,368,128]{2,1,0:T(8,128)(2,1)S(1)} %get-tuple-element.11), channel_id=1, replica_groups=mesh['dp'=4,'gx'=2,'gy'=4] {'gx','gy'}, dimensions={0} | all-to-all | bytes 1507328 | tf_op jit(solution)/shard_map/all_to_all | solution.py:462
  59.8 2.8 %mode_grads.1 = bf16[240,128]{1,0:T(8,128)(2,1)S(1)} custom-call(bf16[8,368,128]{2,1,0:T(8,128)(2,1)S(1)} %all_to_all.10.r_ref, f32[2,768,128]{2,1,0:T(8,128)S(1)} %get-tuple-element.12.s_ref, bf16[144,256]{1,0:T(8,128)(2,1)S(1)} %copy-done.1, bf16[72,512]{1,0:T(8,128)(2,1)S(1)} %copy-done.2), custom_call_target="tpu_custom_call" | custom-call | tf_op jit(solution)/shard_map/mode_grads/pallas_call | solution.py:464
  62.7 1.6 %collective-permute-start = (bf16[240,128]{1,0:T(8,128)(2,1)S(1)}, bf16[240,128]{1,0:T(8,128)(2,1)S(1)}, u32[]{:S(2)}, u32[]{:S(2)}) collective-permute-start(bf16[240,128]{1,0:T(8,128)(2,1)S(1)} %mode_grads.1), channel_id=1, source_target_pairs={{0,8},{8,0},{16,24},{24,16},{1,9},{9,1},{17,25},{25,17},{2,10},{10... | collective-permute-start | bytes 184328 | tf_op jit(solution)/shard_map/ppermute | solution.py:364
  64.3 2.6 %collective-permute-done = bf16[240,128]{1,0:T(8,128)(2,1)S(1)} collective-permute-done((bf16[240,128]{1,0:T(8,128)(2,1)S(1)}, bf16[240,128]{1,0:T(8,128)(2,1)S(1)}, u32[]{:S(2)}, u32[]{:S(2)}) %collective-permute-start) | collective-permute-done | bytes 61472 | tf_op jit(solution)/shard_map/ppermute | solution.py:364
  67.0 0.1 fusion.10.own_ref
  67.1 2.7 %collective-permute-start.1 = (bf16[240,128]{1,0:T(8,128)(2,1)S(1)}, bf16[240,128]{1,0:T(8,128)(2,1)S(1)}, u32[]{:S(2)}, u32[]{:S(2)}) collective-permute-start(bf16[240,128]{1,0:T(8,128)(2,1)S(1)} %fusion.10.own_ref), channel_id=1, source_target_pairs={{0,16},{8,24},{16,0},{24,8},{1,17},{9,25},{17,1},{25,9},{2,18},{10... | collective-permute-start | bytes 184328 | tf_op jit(solution)/shard_map/ppermute | solution.py:364
  69.7 2.5 %collective-permute-done.1.other_ref = bf16[240,128]{1,0:T(8,128)(2,1)S(1)} collective-permute-done((bf16[240,128]{1,0:T(8,128)(2,1)S(1)}, bf16[240,128]{1,0:T(8,128)(2,1)S(1)}, u32[]{:S(2)}, u32[]{:S(2)}) %collective-permute-start.1) | collective-permute-done | bytes 61472 | tf_op jit(solution)/shard_map/ppermute | solution.py:364
  72.2 1.5 %gradients_out.1 = (f32[400,2,36]{2,1,0:T(2,128)}, f32[20,20]{1,0:T(8,128)}) custom-call(bf16[240,128]{1,0:T(8,128)(2,1)S(1)} %fusion.10.own_ref, bf16[240,128]{1,0:T(8,128)(2,1)S(1)} %collective-permute-done.1.other_ref), custom_call_target="tpu_custom_call" | custom-call | tf_op jit(solution)/shard_map/gradients_out/pallas_call | solution.py:472
  (5 shorter events, 0.0 us)
Async XLA Ops:
  0.6 10.4 %copy-start.5 = (bf16[36,2,20,20]{0,1,3,2:T(2,128)(2,1)S(1)}, bf16[36,2,20,20]{0,1,3,2:T(2,128)(2,1)}, u32[]{:S(2)}) copy-start(bf16[36,2,20,20]{0,1,3,2:T(2,128)(2,1)} %param.12) | copy-start | bytes 172804
  5.9 16.3 %all-to-all-start = ((bf16[8,72,640]{2,1,0:T(8,128)(2,1)}), bf16[8,72,640]{2,1,0:T(8,128)(2,1)S(1)}, u32[]{:S(2)}, u32[]{:S(2)}) async-start(bf16[8,72,640]{2,1,0:T(8,128)(2,1)} %spectrum_parts.1), calls=%async_computation | async-start | bytes 1474560 | tf_op jit(solution)/shard_map/all_to_all | solution.py:410
  12.0 10.2 %copy-start.1 = (bf16[144,256]{1,0:T(8,128)(2,1)S(1)}, bf16[144,256]{1,0:T(8,128)(2,1)}, u32[]{:S(2)}) copy-start(bf16[144,256]{1,0:T(8,128)(2,1)} %constant.24.clone.spread_ref) | copy-start | bytes 221188
  12.0 10.2 %copy-start.3 = (bf16[72,256]{1,0:T(8,128)(2,1)S(1)}, bf16[72,256]{1,0:T(8,128)(2,1)}, u32[]{:S(2)}) copy-start(bf16[72,256]{1,0:T(8,128)(2,1)} %constant.26.clone.collect_ref) | copy-start | bytes 110596
  12.0 10.2 %copy-start.4 = (bf16[36,128]{1,0:T(8,128)(2,1)S(1)}, bf16[36,128]{1,0:T(8,128)(2,1)}, u32[]{:S(2)}) copy-start(bf16[36,128]{1,0:T(8,128)(2,1)} %constant.25.clone.wsel_ref) | copy-start | bytes 27652
  12.0 23.1 %copy-start = (bf16[1,20,32,2048]{3,2,1,0:T(8,128)(2,1)S(1)}, bf16[1,20,32,2048]{3,2,1,0:T(8,128)(2,1)}, u32[]{:S(2)}) copy-start(bf16[1,20,32,2048]{3,2,1,0:T(8,128)(2,1)} %param.10) | copy-start | bytes 7864324
  35.1 24.7 %copy-start.2 = (bf16[72,512]{1,0:T(8,128)(2,1)S(1)}, bf16[72,512]{1,0:T(8,128)(2,1)}, u32[]{:S(2)}) copy-start(bf16[72,512]{1,0:T(8,128)(2,1)} %constant.27.clone.fold_ref) | copy-start | bytes 221188
  62.7 4.3 %collective-permute-start = (bf16[240,128]{1,0:T(8,128)(2,1)S(1)}, bf16[240,128]{1,0:T(8,128)(2,1)S(1)}, u32[]{:S(2)}, u32[]{:S(2)}) collective-permute-start(bf16[240,128]{1,0:T(8,128)(2,1)S(1)} %mode_grads.1), channel_id=1, source_target_pairs={{0,8},{8,0},{16,24},{24,16},{1,9},{9,1},{17,25},{25,17},{2,10},{10... | collective-permute-start | bytes 184328 | tf_op jit(solution)/shard_map/ppermute | solution.py:364
  67.1 5.2 %collective-permute-start.1 = (bf16[240,128]{1,0:T(8,128)(2,1)S(1)}, bf16[240,128]{1,0:T(8,128)(2,1)S(1)}, u32[]{:S(2)}, u32[]{:S(2)}) collective-permute-start(bf16[240,128]{1,0:T(8,128)(2,1)S(1)} %fusion.10.own_ref), channel_id=1, source_target_pairs={{0,16},{8,24},{16,0},{24,8},{1,17},{9,25},{17,1},{25,9},{2,18},{10... | collective-permute-start | bytes 184328 | tf_op jit(solution)/shard_map/ppermute | solution.py:364

commit v4 on v3

--- a/solution.py
+++ b/solution.py
@@ -118,7 +118,7 @@
             copy.start()
 
 
-def first_kernel(groups, rows, parts, gid_ref, f_hbm, t_hbm, o_hbm, f_ref, t_ref, acc_ref, o_ref, sem, o_sem):
+def first_kernel(groups, rows, parts, gid_ref, f_hbm, t_hbm, o_ref, f_ref, t_ref, acc_ref, sem):
     gid = gid_ref[0]
     width = f_ref.shape[1] // parts
     copies = chunk_copies([(f_hbm, f_ref), (t_hbm.at[gid], t_ref)], parts, sem)
@@ -134,13 +134,8 @@
         elif j < parts - 1:
             acc_ref[...] += part
     sent = acc_ref[...] + part if parts > 1 else part
-    out = []
     for g in range(groups):
         o_ref[g] = encode(sent[g * rows : (g + 1) * rows, :])
-        out.append(pltpu.make_async_copy(o_ref.at[g], o_hbm.at[g], o_sem.at[g]))
-        out[g].start()
-    for copy in out:
-        copy.wait()
 
 
 def same_plane(n):
@@ -159,28 +154,12 @@
     return x.reshape(C, PL // HP, HP, x.shape[1])[:, h].reshape(HALF, x.shape[1])
 
 
-def cell_mix_kernel(parts, f_hbm, mix_ref, o_hbm, f_ref, o_ref, sem, o_sem):
-    width = f_ref.shape[1] // parts
-    copies = chunk_copies([(f_hbm, f_ref)], parts, sem)
-    start_chunk(copies, 0)
-    e = channel_of(C)
-    u = dot(e, mix_ref[...], 1, 1).astype(BF)
-    m = jnp.where(same_plane(HALF), dot(u, e, 1, 1), 0.0).astype(BF)
-    out = []
-    for j in range(parts):
-        at = slice(j * width, (j + 1) * width)
-        copies[j][0].wait()
-        start_chunk(copies, j + 1)
-        f = f_ref[:, at]
-        for h in range(PL // HP):
-            o_ref[:, h, :, at] = dot(m, half(f, h), 1, 0).reshape(C, HP, width)
-        out.append(pltpu.make_async_copy(o_ref.at[:, :, :, at], o_hbm.at[:, :, :, at], o_sem.at[j]))
-        out[j].start()
-    for copy in out:
-        copy.wait()
-
-
-def mix_kernel(groups, rows, r_ref, w_ref, spread_ref, wsel_ref, collect_ref, v_ref, s_ref, wa_ref, wb_ref, vals_ref):
+def mix_kernel(
+    groups, rows, cot_hbm, r_ref, w_ref, spread_ref, wsel_ref, collect_ref, v_ref, s_ref, cot_ref,
+    wa_ref, wb_ref, vals_ref, sem,
+):
+    cot_copy = pltpu.make_async_copy(cot_hbm, cot_ref, sem.at[0])
+    cot_copy.start()
     total = decode(r_ref[0])
     for g in range(1, groups):
         total = total + decode(r_ref[g])
@@ -190,9 +169,9 @@
     s_ref[0, 0:CP, :] = dot(both, spread_ref[:, 0:128], 0, 0)
     s_ref[1, 0:CP, :] = dot(both, spread_ref[:, 128:256], 0, 0)
     s_ref[:, CP:, :] = jnp.zeros((2, CR * PL - CP, 128), F32)
-    w = w_ref[...]
-    wa_ref[...] = dot(w[:, : C * C], wsel_ref[...], 0, 0)
-    wb_ref[...] = dot(w[:, C * C :], wsel_ref[...], 0, 0)
+    w = w_ref[...].astype(F32)
+    wa_ref[...] = dot(w[:, 0, :].astype(BF), wsel_ref[...], 1, 0)
+    wb_ref[...] = dot(w[:, 1, :].astype(BF), wsel_ref[...], 1, 0)
 
     def some(block, _):
         base = block * 4
@@ -212,6 +191,7 @@
     vals = vals_ref[...] * (1.0 / (SCALE * math.sqrt(MODES)))
     hi, lo = split(vals)
     v_ref[...] = dot(collect_ref[...], jnp.concatenate([hi, lo], 1), 1, 1).astype(BF)
+    cot_copy.wait()
 
 
 def gelu_both(h):
@@ -224,33 +204,28 @@
 
 
 def main_kernel(
-    groups, rows, parts, gid_ref, t_hbm, mixed_hbm, cot_hbm, f_hbm, v_ref, out_hbm, o_ref,
-    t_ref, mixed_ref, cot_ref, f_ref, out_ref, a_ref, acc_ref, product_ref, t_sem, sem, out_sem,
+    groups, rows, parts, t_ref, f_ref, cot_ref, v_ref, mix_ref, out_hbm, o_ref,
+    out_ref, a_ref, acc_ref, product_ref, out_sem,
 ):
-    gid = gid_ref[0]
     width = f_ref.shape[1] // parts
-    table_copy = pltpu.make_async_copy(t_hbm.at[gid], t_ref, t_sem.at[0])
-    table_copy.start()
-    copies = chunk_copies([(mixed_hbm, mixed_ref), (cot_hbm, cot_ref), (f_hbm, f_ref)], parts, sem)
-    for j in range(parts):
-        start_chunk(copies, j)
-    a_ref[...] = jnp.transpose(v_ref[...].astype(F32)).astype(BF)
-    table_copy.wait()
+    vals = jnp.transpose(v_ref[...].astype(F32))
+    e = channel_of(C)
+    m = jnp.where(same_plane(HALF), dot(dot(e, mix_ref[...], 1, 1).astype(BF), e, 1, 1), 0.0)
+    for h in range(PL // HP):
+        a_ref[h] = jnp.concatenate([half(vals, h), m], 1).astype(BF)
     out = []
     for j in range(parts):
         at = slice(j * width, (j + 1) * width)
         t = t_ref[:, at]
-        pre = dot(a_ref[...], t, 1, 0)
-        for copy in copies[j]:
-            copy.wait()
-        pre = pre + mixed_ref[:, :, :, at].reshape(CP, width)
+        f = f_ref[:, at]
+        pre = [dot(a_ref[h], jnp.concatenate([t, half(f, h)], 0), 1, 0) for h in range(PL // HP)]
+        pre = jnp.stack([x.reshape(C, HP, width) for x in pre], 1).reshape(CP, width)
         value, slope = gelu_both(pre)
         out_ref[:, at] = value.astype(BF)
         out.append(pltpu.make_async_copy(out_ref.at[:, at], out_hbm.at[:, at], out_sem.at[j]))
         out[j].start()
         back = (cot_ref[:, at].astype(F32) * slope).astype(BF)
         part = dot(t, back, 1, 1)
-        f = f_ref[:, at]
         product = dot(half(f, 0), half(back, 0), 1, 1)
         for h in range(1, PL // HP):
             product = product + dot(half(f, h), half(back, h), 1, 1)
@@ -382,83 +357,70 @@
     flat = fields.reshape(CP, cells)
     cot = cotangent.reshape(CP, cells)
     gid = (lax.axis_index("gx") * lax.axis_size("gy") + lax.axis_index("gy")).astype(jnp.int32).reshape(1)
-    parts = max(1, cells // 512)
     halves = max(1, cells // 1024)
     high = groups * rows
     vmem = pl.BlockSpec(memory_space=pltpu.VMEM)
     smem = pl.BlockSpec(memory_space=pltpu.SMEM)
 
     hbm = pl.BlockSpec(memory_space=pltpu.HBM)
-    mixed_shape = (C, PL // HP, HP, cells)
-
-    sent = pl.pallas_call(
+
+    sent, flat_in, table_in = pl.pallas_call(
         functools.partial(first_kernel, groups, rows, halves),
         in_specs=[smem, hbm, hbm],
-        out_specs=hbm,
-        out_shape=jax.ShapeDtypeStruct((groups, rows, CP), BF),
+        out_specs=(vmem, vmem, vmem),
+        out_shape=(
+            jax.ShapeDtypeStruct((groups, rows, CP), BF),
+            jax.ShapeDtypeStruct((CP, cells), BF),
+            jax.ShapeDtypeStruct((high, cells), BF),
+        ),
         scratch_shapes=[
-            pltpu.VMEM((CP, cells), BF),
-            pltpu.VMEM((high, cells), BF),
             pltpu.VMEM((high, CP), F32),
-            pltpu.VMEM((groups, rows, CP), BF),
             pltpu.SemaphoreType.DMA((2, halves)),
-            pltpu.SemaphoreType.DMA((groups,)),
         ],
-        compiler_params=compiler_params(60),
+        compiler_params=compiler_params(50),
         name="spectrum_parts",
     )(gid, flat, tables)
     got = lax.all_to_all(sent, GROUP, 0, 0, tiled=True)
 
-    mixed = pl.pallas_call(
-        functools.partial(cell_mix_kernel, parts),
-        in_specs=[hbm, vmem],
-        out_specs=hbm,
-        out_shape=jax.ShapeDtypeStruct(mixed_shape, F32),
+    weights = jnp.transpose(spectral_weight, (2, 3, 1, 0)).reshape(C * C, 2, per)
+    vals, spec, cot_in = pl.pallas_call(
+        functools.partial(mix_kernel, groups, rows),
+        in_specs=[hbm] + [vmem] * 5,
+        out_specs=[vmem] * 3,
+        out_shape=[
+            jax.ShapeDtypeStruct((rows, CP), BF),
+            jax.ShapeDtypeStruct((2, CR * PL, 128), F32),
+            jax.ShapeDtypeStruct((CP, cells), BF),
+        ],
         scratch_shapes=[
-            pltpu.VMEM((CP, cells), BF),
-            pltpu.VMEM(mixed_shape, F32),
-            pltpu.SemaphoreType.DMA((1, parts)),
-            pltpu.SemaphoreType.DMA((parts,)),
+            pltpu.VMEM((C * C, 128), F32),
+            pltpu.VMEM((C * C, 128), F32),
+            pltpu.VMEM((CP, 128), F32),
+            pltpu.SemaphoreType.DMA((1,)),
         ],
-        compiler_params=compiler_params(60),
-        cost_estimate=pl.CostEstimate(flops=2 * 2 * HALF * HALF * cells, bytes_accessed=8 * 2**20, transcendentals=0),
-        name="cell_mixing",
-    )(flat, mix_weight)
-
-    weights = spectral_weight.reshape(per, 2 * C * C)
-    vals, spec = pl.pallas_call(
-        functools.partial(mix_kernel, groups, rows),
-        out_shape=(jax.ShapeDtypeStruct((rows, CP), BF), jax.ShapeDtypeStruct((2, CR * PL, 128), F32)),
-        scratch_shapes=[pltpu.VMEM((C * C, 128), F32), pltpu.VMEM((C * C, 128), F32), pltpu.VMEM((CP, 128), F32)],
-        compiler_params=compiler_params(8),
+        compiler_params=compiler_params(48),
         name="mode_mixing",
-    )(got, weights, spread, wsel, collect)
+    )(cot, got, weights, spread, wsel, collect)
     all_vals = lax.all_gather(vals, GROUP, axis=0, tiled=True)
 
     output, sent = pl.pallas_call(
-        functools.partial(main_kernel, groups, rows, halves),
-        in_specs=[smem, hbm, hbm, hbm, hbm, vmem],
+        functools.partial(main_kernel, groups, rows, 1),
+        in_specs=[vmem] * 5,
         out_specs=(hbm, vmem),
         out_shape=(
             jax.ShapeDtypeStruct((CP, cells), BF),
             jax.ShapeDtypeStruct((groups, rows * CP // 128 + 8, 128), BF),
         ),
         scratch_shapes=[
-            pltpu.VMEM((high, cells), BF),
-            pltpu.VMEM(mixed_shape, F32),
             pltpu.VMEM((CP, cells), BF),
-            pltpu.VMEM((CP, cells), BF),
-            pltpu.VMEM((CP, cells), BF),
-            pltpu.VMEM((CP, high), BF),
+            pltpu.VMEM((PL // HP, HALF, high + HALF), BF),
             pltpu.VMEM((high, CP), F32),
             pltpu.VMEM((HALF, HALF), F32),
             pltpu.SemaphoreType.DMA((1,)),
-            pltpu.SemaphoreType.DMA((3, halves)),
-            pltpu.SemaphoreType.DMA((halves,)),
         ],
-        compiler_params=compiler_params(48),
+        compiler_params=compiler_params(40),
         name="cells",
-    )(gid, tables, mixed, cot, flat, all_vals)
+    )(table_in, flat_in, cot_in, all_vals, mix_weight)
     got = lax.all_to_all(sent, GROUP, 0, 0, tiled=True)
 
     coded = pl.pallas_call(

time: 74.1 us -> 69.8 us (0.942)
  blocking collectives: 24.6 us -> 40.6 us
  Pallas kernels: 29.5 us -> 18.7 us
  starting transfers between devices: 9.48 us -> 4.3 us
  waiting for transfers between devices: 8.4 us -> 5.17 us
  local copies, waits for them, and re-layouts: 0.95 us -> 0.04 us
    all_to_all x1 -> x2, blocking collectives: 14.1 us -> 30.5 us  [local(): got = lax.all_to_all(sent, GROUP, 0, 0, tiled=True)]
    pallas_call x3 -> x2, Pallas kernels: 20 us -> 9.62 us  [the longest x1 6.89 us: local(): pl.pallas_call(functools.partial(main_kernel, groups, rows, 1), in_specs=...]
    all_to_all x1 -> x0, starting transfers between devices: 5.18 us -> none  [local(): got = lax.all_to_all(sent, GROUP, 0, 0, tiled=True)]
    all_to_all x1 -> x0, waiting for transfers between devices: 3.23 us -> none  [local(): got = lax.all_to_all(sent, GROUP, 0, 0, tiled=True)]
    reshape x2 -> x0, local copies, waits for them, and re-layouts: 0.91 us -> none  [local(): weights = spectral_weight.reshape(per, 2 * C * C)]
  transfers between devices with their start and end apart: 3 -> 2, of which waited for: 3 -> 2; matrix products, arithmetic and copies ran while one was open for 1% -> 0% of each run, Pallas kernels for 9% -> 0%
where the time goes in v4:
time: 69.8 us; the launch traced here: 69.6 us
  blocking collectives  40.6 us (58%)
  Pallas kernels  18.7 us (27%)
  waiting for transfers between devices  5.17 us (7%)
  starting transfers between devices  4.3 us (6%)
  between operations  0.72 us (1%)
    all_to_all x2, blocking collectives, local(): got = lax.all_to_all(sent, GROUP, 0, 0, tiled=True)  30.5 us
    all_gather x1, blocking collectives, local(): all_vals = lax.all_gather(vals, GROUP, axis=0, tiled=True)  10.1 us
    pallas_call x1, Pallas kernels, local(): pl.pallas_call(functools.partial(main_kernel, groups, rows, 1), in_specs=...  6.89 us
    ppermute x2, waiting for transfers between devices, sum_over_dp(): other = lax.ppermute(coded, 'dp', [(i, i ^ step) for i in range(samples)])  5.17 us
    pallas_call x1, Pallas kernels, local(): pl.pallas_call(functools.partial(first_kernel, groups, rows, halves), in_...  4.55 us
    ppermute x2, starting transfers between devices, sum_over_dp(): other = lax.ppermute(coded, 'dp', [(i, i ^ step) for i in range(samples)])  4.3 us
    pallas_call x1, Pallas kernels, local(): pl.pallas_call(functools.partial(grad_kernel, groups, rows), out_shape=ja...  2.99 us
    pallas_call x1, Pallas kernels, local(): pl.pallas_call(functools.partial(mix_kernel, groups, rows), in_specs=[hbm...  2.73 us
  transfers between devices with their start and end apart: 2, of which 2 were waited for; matrix products, arithmetic and copies ran while one was open for 0% of the time, Pallas kernels for 0%

profile of v4, /device:TPU:0, one launch (start us, length us, event | category | flops | bytes accessed | tf_op | source)
XLA Modules:
  0.0 69.6 jit_solution(1784261010205907192)
XLA Ops:
  0.6 0.0 copy-start.1
  0.6 0.0 copy-start.2
  0.7 0.0 copy-start.4
  0.7 0.0 copy-start.5
  0.7 4.6 %spectrum_parts.1 = (bf16[8,72,640]{2,1,0:T(8,128)(2,1)S(1)}, bf16[640,2048]{1,0:T(8,128)(2,1)}, bf16[576,2048]{1,0:T(8,128)(2,1)S(1)}) custom-call(s32[1]{0:T(128)} %bitcast.gid_ref, bf16[640,2048]{1,0:T(8,128)(2,1)} %bitcast.11, bf16[8,576,2048]{2,1,0:T(8,128)(2,1)} %constant.23.clone.t_hbm), custom_call_target="tpu_custom_call" | custom-call | tf_op jit(solution)/shard_map/spectrum_parts/pallas_call | solution.py:367
  5.2 16.4 %all_to_all.10.r_ref = bf16[8,72,640]{2,1,0:T(8,128)(2,1)S(1)} all-to-all(bf16[8,72,640]{2,1,0:T(8,128)(2,1)S(1)} %get-tuple-element.15), channel_id=1, replica_groups=mesh['dp'=4,'gx'=2,'gy'=4] {'gx','gy'}, dimensions={0} | all-to-all | bytes 1474560 | tf_op jit(solution)/shard_map/all_to_all | solution.py:383
  21.7 0.0 copy-done.1
  21.7 0.0 copy-done.2
  21.7 0.0 copy-done.4
  21.7 0.0 copy-done.5
  21.7 2.7 %mode_mixing.1 = (bf16[72,640]{1,0:T(8,128)(2,1)S(1)}, f32[2,768,128]{2,1,0:T(8,128)S(1)}, bf16[640,2048]{1,0:T(8,128)(2,1)S(1)}) custom-call(bf16[640,2048]{1,0:T(8,128)(2,1)} %bitcast.12, bf16[8,72,640]{2,1,0:T(8,128)(2,1)S(1)} %all_to_all.10.r_ref, bf16[400,2,36]{2,1,0:T(2,128)(2,1)S(1)} %bitcast.10, bf16[144,256]{1,0:T(8,128)(2,1)S(1)} %copy-done.1, ...), custom_call_target="tpu_custom_call" | custom-call | tf_op jit(solution)/shard_map/mode_mixing/pallas_call | solution.py:386
  24.4 10.1 %all_gather.3.v_ref = bf16[576,640]{1,0:T(8,128)(2,1)S(1)} all-gather(bf16[72,640]{1,0:T(8,128)(2,1)S(1)} %get-tuple-element.17), channel_id=1, replica_groups=mesh['dp'=4,'gx'=2,'gy'=4] {'gx','gy'}, dimensions={0}, use_global_device_ids=true | all-gather | bytes 829440 | tf_op jit(solution)/shard_map/all_gather | solution.py:404
  34.5 0.0 copy-done
  34.5 0.0 copy-done.6
  34.5 6.9 %cells.1 = (bf16[640,2048]{1,0:T(8,128)(2,1)}, bf16[8,368,128]{2,1,0:T(8,128)(2,1)S(1)}) custom-call(bf16[576,2048]{1,0:T(8,128)(2,1)S(1)} %get-tuple-element.13.t_ref, bf16[640,2048]{1,0:T(8,128)(2,1)S(1)} %copy-done, bf16[640,2048]{1,0:T(8,128)(2,1)S(1)} %get-tuple-element.16.cot_ref, bf16[576,640]{1,0:T(8,128)(2,1)S(1)} %all_gather.3.v_ref, ...), custom_call_target="tpu_custom_call" | custom-call | tf_op jit(solution)/shard_map/cells/pallas_call | solution.py:406
  41.4 14.1 %all_to_all.11.r_ref = bf16[8,368,128]{2,1,0:T(8,128)(2,1)S(1)} all-to-all(bf16[8,368,128]{2,1,0:T(8,128)(2,1)S(1)} %get-tuple-element.19), channel_id=1, replica_groups=mesh['dp'=4,'gx'=2,'gy'=4] {'gx','gy'}, dimensions={0} | all-to-all | bytes 1507328 | tf_op jit(solution)/shard_map/all_to_all | solution.py:424
  55.5 0.0 copy-done.3
  55.5 3.0 %mode_grads.1 = bf16[240,128]{1,0:T(8,128)(2,1)S(1)} custom-call(bf16[8,368,128]{2,1,0:T(8,128)(2,1)S(1)} %all_to_all.11.r_ref, f32[2,768,128]{2,1,0:T(8,128)S(1)} %get-tuple-element.20.s_ref, bf16[144,256]{1,0:T(8,128)(2,1)S(1)} %copy-done.1, bf16[72,512]{1,0:T(8,128)(2,1)S(1)} %copy-done.3), custom_call_target="tpu_custom_call" | custom-call | tf_op jit(solution)/shard_map/mode_grads/pallas_call | solution.py:426
  58.5 1.6 %collective-permute-start = (bf16[240,128]{1,0:T(8,128)(2,1)S(1)}, bf16[240,128]{1,0:T(8,128)(2,1)S(1)}, u32[]{:S(2)}, u32[]{:S(2)}) collective-permute-start(bf16[240,128]{1,0:T(8,128)(2,1)S(1)} %mode_grads.1), channel_id=1, source_target_pairs={{0,8},{8,0},{16,24},{24,16},{1,9},{9,1},{17,25},{25,17},{2,10},{10... | collective-permute-start | bytes 184328 | tf_op jit(solution)/shard_map/ppermute | solution.py:339
  60.1 2.6 %collective-permute-done = bf16[240,128]{1,0:T(8,128)(2,1)S(1)} collective-permute-done((bf16[240,128]{1,0:T(8,128)(2,1)S(1)}, bf16[240,128]{1,0:T(8,128)(2,1)S(1)}, u32[]{:S(2)}, u32[]{:S(2)}) %collective-permute-start) | collective-permute-done | bytes 61472 | tf_op jit(solution)/shard_map/ppermute | solution.py:339
  62.8 0.1 fusion.10.own_ref
  62.9 2.7 %collective-permute-start.1 = (bf16[240,128]{1,0:T(8,128)(2,1)S(1)}, bf16[240,128]{1,0:T(8,128)(2,1)S(1)}, u32[]{:S(2)}, u32[]{:S(2)}) collective-permute-start(bf16[240,128]{1,0:T(8,128)(2,1)S(1)} %fusion.10.own_ref), channel_id=1, source_target_pairs={{0,16},{8,24},{16,0},{24,8},{1,17},{9,25},{17,1},{25,9},{2,18},{10... | collective-permute-start | bytes 184328 | tf_op jit(solution)/shard_map/ppermute | solution.py:339
  65.5 2.5 %collective-permute-done.1.other_ref = bf16[240,128]{1,0:T(8,128)(2,1)S(1)} collective-permute-done((bf16[240,128]{1,0:T(8,128)(2,1)S(1)}, bf16[240,128]{1,0:T(8,128)(2,1)S(1)}, u32[]{:S(2)}, u32[]{:S(2)}) %collective-permute-start.1) | collective-permute-done | bytes 61472 | tf_op jit(solution)/shard_map/ppermute | solution.py:339
  68.1 1.5 %gradients_out.1 = (f32[400,2,36]{2,1,0:T(2,128)}, f32[20,20]{1,0:T(8,128)}) custom-call(bf16[240,128]{1,0:T(8,128)(2,1)S(1)} %fusion.10.own_ref, bf16[240,128]{1,0:T(8,128)(2,1)S(1)} %collective-permute-done.1.other_ref), custom_call_target="tpu_custom_call" | custom-call | tf_op jit(solution)/shard_map/gradients_out/pallas_call | solution.py:434
  (3 shorter events, 0.0 us)
Async XLA Ops:
  0.6 21.0 %copy-start.1 = (bf16[144,256]{1,0:T(8,128)(2,1)S(1)}, bf16[144,256]{1,0:T(8,128)(2,1)}, u32[]{:S(2)}) copy-start(bf16[144,256]{1,0:T(8,128)(2,1)} %constant.24.clone.spread_ref) | copy-start | bytes 221188
  0.6 21.0 %copy-start.2 = (bf16[36,2,20,20]{0,1,3,2:T(2,128)(2,1)S(1)}, bf16[36,2,20,20]{0,1,3,2:T(2,128)(2,1)}, u32[]{:S(2)}) copy-start(bf16[36,2,20,20]{0,1,3,2:T(2,128)(2,1)} %param.12) | copy-start | bytes 172804
  0.7 21.0 %copy-start.4 = (bf16[72,256]{1,0:T(8,128)(2,1)S(1)}, bf16[72,256]{1,0:T(8,128)(2,1)}, u32[]{:S(2)}) copy-start(bf16[72,256]{1,0:T(8,128)(2,1)} %constant.26.clone.collect_ref) | copy-start | bytes 110596
  0.7 21.0 %copy-start.5 = (bf16[36,128]{1,0:T(8,128)(2,1)S(1)}, bf16[36,128]{1,0:T(8,128)(2,1)}, u32[]{:S(2)}) copy-start(bf16[36,128]{1,0:T(8,128)(2,1)} %constant.25.clone.wsel_ref) | copy-start | bytes 27652
  21.7 12.8 %copy-start = (bf16[640,2048]{1,0:T(8,128)(2,1)S(1)}, bf16[640,2048]{1,0:T(8,128)(2,1)}, u32[]{:S(2)}) copy-start(bf16[640,2048]{1,0:T(8,128)(2,1)} %get-tuple-element.14.f_ref) | copy-start | bytes 7864324
  21.7 12.8 %copy-start.6 = (bf16[20,20]{1,0:T(8,128)(2,1)S(1)}, bf16[20,20]{1,0:T(8,128)(2,1)}, u32[]{:S(2)}) copy-start(bf16[20,20]{1,0:T(8,128)(2,1)} %mix_ref.1) | copy-start | bytes 2404
  34.5 21.0 %copy-start.3 = (bf16[72,512]{1,0:T(8,128)(2,1)S(1)}, bf16[72,512]{1,0:T(8,128)(2,1)}, u32[]{:S(2)}) copy-start(bf16[72,512]{1,0:T(8,128)(2,1)} %constant.27.clone.fold_ref) | copy-start | bytes 221188
  58.5 4.3 %collective-permute-start = (bf16[240,128]{1,0:T(8,128)(2,1)S(1)}, bf16[240,128]{1,0:T(8,128)(2,1)S(1)}, u32[]{:S(2)}, u32[]{:S(2)}) collective-permute-start(bf16[240,128]{1,0:T(8,128)(2,1)S(1)} %mode_grads.1), channel_id=1, source_target_pairs={{0,8},{8,0},{16,24},{24,16},{1,9},{9,1},{17,25},{25,17},{2,10},{10... | collective-permute-start | bytes 184328 | tf_op jit(solution)/shard_map/ppermute | solution.py:339
  62.9 5.2 %collective-permute-start.1 = (bf16[240,128]{1,0:T(8,128)(2,1)S(1)}, bf16[240,128]{1,0:T(8,128)(2,1)S(1)}, u32[]{:S(2)}, u32[]{:S(2)}) collective-permute-start(bf16[240,128]{1,0:T(8,128)(2,1)S(1)} %fusion.10.own_ref), channel_id=1, source_target_pairs={{0,16},{8,24},{16,0},{24,8},{1,17},{9,25},{17,1},{25,9},{2,18},{10... | collective-permute-start | bytes 184328 | tf_op jit(solution)/shard_map/ppermute | solution.py:339

commit v5 on v4

--- a/solution.py
+++ b/solution.py
@@ -18,8 +18,9 @@
 C = 20
 PL = 32
 CP = C * PL
-HP = 16
-HALF = C * HP
+HP = 8
+PART = C * HP
+OUT_PARTS = 4
 CR = 24
 SCALE = 1.6656925
 GROUP = ("gx", "gy")
@@ -65,18 +66,24 @@
     collect = np.zeros((rows, 128), np.float32)
     collect[re, re] = 1
     collect[im, im] = 1
-    fold = np.zeros((rows, 256), np.float32)
-    fold[re, re] = 1
-    fold[re, im] = 1
-    fold[im, 128 + re] = 1
-    fold[im, 128 + im] = 1
+    fold = np.zeros((256, 256), np.float32)
+    for first in (0, 128):
+        fold[first + re, first + re] = 1
+        fold[first + im, first + re] = 1
     cast = lambda a: a.astype(ml_dtypes.bfloat16)
     return (
         cast(np.concatenate([spread, spread], 0)),
         cast(weights),
         cast(np.concatenate([collect, collect], 1)),
-        cast(np.concatenate([fold, fold], 1)),
+        cast(np.concatenate([fold, fold], 0)),
     )
+
+
+def plane_order():
+    order = np.zeros((PL, CR, C, PL), np.float32)
+    for d in range(C):
+        order[np.arange(PL), d, d, np.arange(PL)] = 1
+    return order.reshape(PL * CR, CP).astype(ml_dtypes.bfloat16)
 
 
 def dot(a, b, ca, cb):
@@ -145,13 +152,13 @@
 
 
 def channel_of(lanes):
-    i = lax.broadcasted_iota(jnp.int32, (HALF, lanes), 0)
-    j = lax.broadcasted_iota(jnp.int32, (HALF, lanes), 1)
+    i = lax.broadcasted_iota(jnp.int32, (PART, lanes), 0)
+    j = lax.broadcasted_iota(jnp.int32, (PART, lanes), 1)
     return jnp.where(lax.div(i, HP) == j, 1.0, 0.0).astype(BF)
 
 
-def half(x, h):
-    return x.reshape(C, PL // HP, HP, x.shape[1])[:, h].reshape(HALF, x.shape[1])
+def planes_of(x, h):
+    return x.reshape(C, PL // HP, HP, x.shape[1])[:, h].reshape(PART, x.shape[1])
 
 
 def mix_kernel(
@@ -210,25 +217,30 @@
     width = f_ref.shape[1] // parts
     vals = jnp.transpose(v_ref[...].astype(F32))
     e = channel_of(C)
-    m = jnp.where(same_plane(HALF), dot(dot(e, mix_ref[...], 1, 1).astype(BF), e, 1, 1), 0.0)
+    m = jnp.where(same_plane(PART), dot(dot(e, mix_ref[...], 1, 1).astype(BF), e, 1, 1), 0.0)
     for h in range(PL // HP):
-        a_ref[h] = jnp.concatenate([half(vals, h), m], 1).astype(BF)
+        a_ref[h] = jnp.concatenate([planes_of(vals, h), m], 1).astype(BF)
     out = []
     for j in range(parts):
         at = slice(j * width, (j + 1) * width)
         t = t_ref[:, at]
-        f = f_ref[:, at]
-        pre = [dot(a_ref[h], jnp.concatenate([t, half(f, h)], 0), 1, 0) for h in range(PL // HP)]
+        f = f_ref[:, at].astype(F32)
+        f = [planes_of(f, h).astype(BF) for h in range(PL // HP)]
+        pre = [dot(a_ref[h], jnp.concatenate([t, f[h]], 0), 1, 0) for h in range(PL // HP)]
         pre = jnp.stack([x.reshape(C, HP, width) for x in pre], 1).reshape(CP, width)
-        value, slope = gelu_both(pre)
-        out_ref[:, at] = value.astype(BF)
-        out.append(pltpu.make_async_copy(out_ref.at[:, at], out_hbm.at[:, at], out_sem.at[j]))
-        out[j].start()
-        back = (cot_ref[:, at].astype(F32) * slope).astype(BF)
-        part = dot(t, back, 1, 1)
-        product = dot(half(f, 0), half(back, 0), 1, 1)
+        back = []
+        for i in range(OUT_PARTS):
+            some = slice(i * CP // OUT_PARTS, (i + 1) * CP // OUT_PARTS)
+            value, slope = gelu_both(pre[some])
+            out_ref[some, at] = value.astype(BF)
+            out.append(pltpu.make_async_copy(out_ref.at[some, at], out_hbm.at[some, at], out_sem.at[j, i]))
+            out[-1].start()
+            back.append(cot_ref[some, at].astype(F32) * slope)
+        back = jnp.concatenate(back, 0)
+        part = dot(t, back.astype(BF), 1, 1)
+        product = dot(f[0], planes_of(back, 0).astype(BF), 1, 1)
         for h in range(1, PL // HP):
-            product = product + dot(half(f, h), half(back, h), 1, 1)
+            product = product + dot(f[h], planes_of(back, h).astype(BF), 1, 1)
         if j == 0:
             acc_ref[...] = part
             product_ref[...] = product
@@ -238,9 +250,9 @@
     spectrum = acc_ref[...]
     product = product_ref[...]
 
-    kept = jnp.where(same_plane(HALF), product, 0.0)
-    kept = jnp.sum(kept.reshape(C, HP, HALF), axis=1)
-    kept = jnp.concatenate([kept, jnp.zeros((CR - C, HALF), F32)], 0)
+    kept = jnp.where(same_plane(PART), product, 0.0)
+    kept = jnp.sum(kept.reshape(C, HP, PART), axis=1)
+    kept = jnp.concatenate([kept, jnp.zeros((CR - C, PART), F32)], 0)
     hi, lo = split(kept)
     e = channel_of(128)
     y = dot(hi, e, 1, 0) + dot(lo, e, 1, 0)
@@ -256,11 +268,7 @@
         copy.wait()
 
 
-def payload_rows(rows):
-    return round_up(3 * rows + 16, 16)
-
-
-def grad_kernel(groups, rows, r_ref, s_ref, spread_ref, fold_ref, o_ref, g_ref, p_ref):
+def grad_kernel(groups, rows, per, r_ref, s_ref, spread_ref, fold_ref, order_ref, o_ref, g_ref, p_ref):
     high = rows * CP // 128
     total = None
     extra = None
@@ -274,60 +282,51 @@
     total = jnp.concatenate([total[i * rows : (i + 1) * rows] for i in range(CP // 128)], 1)
     hi, lo = split(total)
     both = jnp.concatenate([hi.astype(F32), lo.astype(F32)], 0).astype(BF)
-    g_ref[0:CP, :] = dot(both, spread_ref[:, 0:128], 0, 0)
-    g_ref[CP:, :] = jnp.zeros((CR * PL - CP, 128), F32)
-
-    def some(block, _):
-        base = block * 5
-        one = [jnp.zeros((CR, 128), F32)] * 5
-        two = [jnp.zeros((CR, 128), F32)] * 5
+    hi, lo = split(dot(both, spread_ref[:, 0:128], 0, 0))
+    by_plane = dot(order_ref[...], jnp.concatenate([hi, lo], 1), 1, 0)
+    g_ref[...] = by_plane[:, 0:128] + by_plane[:, 128:256]
+
+    for base in range(0, C, 4):
+        one = [jnp.zeros((CR, 128), F32)] * 4
+        two = [jnp.zeros((CR, 128), F32)] * 4
         for p in range(PL):
-            g = g_ref[pl.ds(p, CR, stride=PL), :]
-            for k in range(5):
-                one[k] = one[k] + s_ref[0, pl.ds((base + k) * PL + p, 1), :] * g
-                two[k] = two[k] + s_ref[1, pl.ds((base + k) * PL + p, 1), :] * g
-        for k in range(5):
-            at = pl.multiple_of((base + k) * CR, CR)
-            p_ref[pl.ds(at, CR), 0:128] = one[k]
-            p_ref[pl.ds(at, CR), 128:256] = two[k]
-        return 0
-
-    lax.fori_loop(0, C // 5, some, 0)
+            g = g_ref[p * CR : (p + 1) * CR, :]
+            for k in range(4):
+                row = (base + k) * PL + p
+                one[k] = one[k] + s_ref[0, row : row + 1, :] * g
+                two[k] = two[k] + s_ref[1, row : row + 1, :] * g
+        for k in range(4):
+            at = (base + k) * CR
+            p_ref[at : at + CR, 0:128] = one[k]
+            p_ref[at : at + CR, 128:256] = two[k]
     products = jnp.concatenate([p_ref[c * CR : c * CR + C, :] for c in range(C)], 0)
     hi, lo = split(products)
-    grads = dot(fold_ref[...], jnp.concatenate([hi, lo], 1), 1, 1)
-    tail = jnp.concatenate([grads[:, 384:], jnp.zeros((rows, 512 - C * C), F32)], 1)
+    both = jnp.concatenate([hi, lo], 1)
+    slots = dot(both, fold_ref[...], 1, 0)
+    re, im = slots[:, 0:128], slots[:, 128:256]
+    middle = pltpu.roll(jnp.concatenate([re[272:], im[0:144]], 0), per, 1)
+    last = pltpu.roll(jnp.concatenate([im[144:], jnp.zeros((16, 128), F32)], 0), 2 * per, 1)
     lane = lax.broadcasted_iota(jnp.int32, (8, 128), 1)
     extra = extra + pltpu.roll(extra, 64, 1)
-    extra = jnp.where(lane < 3 * C, extra, 0.0)
-    strip = [jnp.zeros((8, 128), F32), pltpu.roll(extra, 64, 1)]
-    for i in range(rows // 8):
-        piece = tail[8 * i : 8 * i + 8]
-        strip[i // 8] = strip[i // 8] + (pltpu.roll(piece, 16 * (i % 8), 1) if i % 8 else piece)
-    fill = jnp.zeros((payload_rows(rows) - 3 * rows - 16, 128), F32)
-    parts = [grads[:, 128 * i : 128 * (i + 1)] for i in range(3)] + strip
-    if fill.shape[0]:
-        parts.append(fill)
-    o_ref[...] = encode(jnp.concatenate(parts, 0))
-
-
-def last_kernel(rows, per, samples, own_ref, other_ref, grad_ref, mix_ref):
-    total = decode(own_ref[...])
-    total = total + decode(other_ref[...])
-    lane = lax.broadcasted_iota(jnp.int32, (8, 128), 1)
-    strip = [total[3 * rows : 3 * rows + 8], total[3 * rows + 8 : 3 * rows + 16]]
-    tail = []
-    for i in range(rows // 8):
-        piece = pltpu.roll(strip[i // 8], 128 - 16 * (i % 8), 1) if i % 8 else strip[i // 8]
-        tail.append(jnp.where(lane < C * C - 384, piece, 0.0))
-    grads = jnp.concatenate([total[i * rows : (i + 1) * rows] for i in range(3)] + [jnp.concatenate(tail, 0)], 1)
-    grads = jnp.transpose(grads * (1.0 / math.sqrt(samples * PL)))[0 : C * C]
-    grad_ref[:, 0, :] = grads[:, 0:per]
-    grad_ref[:, 1, :] = grads[:, per : 2 * per]
-    mix = strip[1] * (1.0 / math.sqrt(samples * PL * NX * NY))
-    mix_ref[0:8, :] = pltpu.roll(mix, 64, 1)[:, 0:C]
-    mix_ref[8:16, :] = pltpu.roll(mix, 64 - C, 1)[:, 0:C]
-    mix_ref[16:C, :] = pltpu.roll(mix, 64 - 2 * C, 1)[0 : C - 16, 0:C]
+    pieces = []
+    for k in range(3):
+        piece = pltpu.roll(extra, (3 * per - k * C) % 128, 1)
+        pieces.append(jnp.where(jnp.logical_and(lane >= 3 * per, lane < 3 * per + C), piece, 0.0))
+    pieces.append(jnp.zeros((272 - 24, 128), F32))
+    o_ref[...] = encode(re[0:272] + middle + last + jnp.concatenate(pieces, 0))
+
+
+def last_kernel(per, samples, own_ref, other_ref, grad_ref, mix_ref):
+    total = decode(own_ref[...]) + decode(other_ref[...])
+    grads = total * (1.0 / math.sqrt(samples * PL))
+    one = pltpu.roll(grads, 128 - per, 1)
+    two = pltpu.roll(grads, 128 - 2 * per, 1)
+    grad_ref[0:272, 0, :] = grads[:, 0:per]
+    grad_ref[272:400, 0, :] = one[0:128, 0:per]
+    grad_ref[0:144, 1, :] = one[128:272, 0:per]
+    grad_ref[144:400, 1, :] = two[0:256, 0:per]
+    mix = pltpu.roll(total[0:24], 128 - 3 * per, 1) * (1.0 / math.sqrt(samples * PL * NX * NY))
+    mix_ref[...] = mix[0:C, 0:C]
 
 
 def sum_over_dp(coded, samples):
@@ -413,10 +412,10 @@
         ),
         scratch_shapes=[
             pltpu.VMEM((CP, cells), BF),
-            pltpu.VMEM((PL // HP, HALF, high + HALF), BF),
+            pltpu.VMEM((PL // HP, PART, high + PART), BF),
             pltpu.VMEM((high, CP), F32),
-            pltpu.VMEM((HALF, HALF), F32),
-            pltpu.SemaphoreType.DMA((1,)),
+            pltpu.VMEM((PART, PART), F32),
+            pltpu.SemaphoreType.DMA((1, OUT_PARTS)),
         ],
         compiler_params=compiler_params(40),
         name="cells",
@@ -424,15 +423,15 @@
     got = lax.all_to_all(sent, GROUP, 0, 0, tiled=True)
 
     coded = pl.pallas_call(
-        functools.partial(grad_kernel, groups, rows),
-        out_shape=jax.ShapeDtypeStruct((payload_rows(rows), 128), BF),
+        functools.partial(grad_kernel, groups, rows, per),
+        out_shape=jax.ShapeDtypeStruct((272, 128), BF),
         scratch_shapes=[pltpu.VMEM((CR * PL, 128), F32), pltpu.VMEM((C * CR, 256), F32)],
         compiler_params=compiler_params(8),
         name="mode_grads",
-    )(got, spec, spread, fold)
+    )(got, spec, spread, fold, plane_order())
     own, other = sum_over_dp(coded, samples)
     grads, mixing_grad = pl.pallas_call(
-        functools.partial(last_kernel, rows, per, samples),
+        functools.partial(last_kernel, per, samples),
         out_shape=(jax.ShapeDtypeStruct((C * C, 2, per), F32), jax.ShapeDtypeStruct((C, C), F32)),
         compiler_params=compiler_params(8),
         name="gradients_out",

time: 69.8 us -> 68.6 us (0.983)
  Pallas kernels: 18.7 us -> 17.3 us
    pallas_call x2, Pallas kernels: 4.48 us -> 3.76 us  [the longest x1 2.71 us: local(): pl.pallas_call(functools.partial(grad_kernel, groups, rows, per), out_sha...]
where the time goes in v5:
time: 68.6 us; the launch traced here: 68.4 us
  blocking collectives  40.6 us (59%)
  Pallas kernels  17.3 us (25%)
  waiting for transfers between devices  5.35 us (8%)
  starting transfers between devices  4.3 us (6%)
  between operations  0.73 us (1%)
    all_to_all x2, blocking collectives, local(): got = lax.all_to_all(sent, GROUP, 0, 0, tiled=True)  30.5 us
    all_gather x1, blocking collectives, local(): all_vals = lax.all_gather(vals, GROUP, axis=0, tiled=True)  10.1 us
    pallas_call x1, Pallas kernels, local(): pl.pallas_call(functools.partial(main_kernel, groups, rows, 1), in_specs=...  6.26 us
    ppermute x2, waiting for transfers between devices, sum_over_dp(): other = lax.ppermute(coded, 'dp', [(i, i ^ step) for i in range(samples)])  5.35 us
    pallas_call x1, Pallas kernels, local(): pl.pallas_call(functools.partial(first_kernel, groups, rows, halves), in_...  4.56 us
    ppermute x2, starting transfers between devices, sum_over_dp(): other = lax.ppermute(coded, 'dp', [(i, i ^ step) for i in range(samples)])  4.3 us
    pallas_call x1, Pallas kernels, local(): pl.pallas_call(functools.partial(mix_kernel, groups, rows), in_specs=[hbm...  2.73 us
    pallas_call x1, Pallas kernels, local(): pl.pallas_call(functools.partial(grad_kernel, groups, rows, per), out_sha...  2.71 us
  transfers between devices with their start and end apart: 2, of which 2 were waited for; matrix products, arithmetic and copies ran while one was open for 0% of the time, Pallas kernels for 0%

profile of v5, /device:TPU:0, one launch (start us, length us, event | category | flops | bytes accessed | tf_op | source)
XLA Modules:
  0.0 68.4 jit_solution(7766755561370459962)
XLA Ops:
  0.6 0.0 copy-start.2
  0.6 0.0 copy-start.4
  0.7 0.0 copy-start.5
  0.7 0.0 copy-start.6
  0.7 4.6 %spectrum_parts.1 = (bf16[8,72,640]{2,1,0:T(8,128)(2,1)S(1)}, bf16[640,2048]{1,0:T(8,128)(2,1)}, bf16[576,2048]{1,0:T(8,128)(2,1)S(1)}) custom-call(s32[1]{0:T(128)} %bitcast.gid_ref, bf16[640,2048]{1,0:T(8,128)(2,1)} %bitcast.11, bf16[8,576,2048]{2,1,0:T(8,128)(2,1)} %constant.25.clone.t_hbm), custom_call_target="tpu_custom_call" | custom-call | tf_op jit(solution)/shard_map/spectrum_parts/pallas_call | solution.py:366
  5.2 16.4 %all_to_all.10.r_ref = bf16[8,72,640]{2,1,0:T(8,128)(2,1)S(1)} all-to-all(bf16[8,72,640]{2,1,0:T(8,128)(2,1)S(1)} %get-tuple-element.15), channel_id=1, replica_groups=mesh['dp'=4,'gx'=2,'gy'=4] {'gx','gy'}, dimensions={0} | all-to-all | bytes 1474560 | tf_op jit(solution)/shard_map/all_to_all | solution.py:382
  21.7 0.0 copy-done.2
  21.7 0.0 copy-done.4
  21.7 0.0 copy-done.5
  21.7 0.0 copy-done.6
  21.7 2.7 %mode_mixing.1 = (bf16[72,640]{1,0:T(8,128)(2,1)S(1)}, f32[2,768,128]{2,1,0:T(8,128)S(1)}, bf16[640,2048]{1,0:T(8,128)(2,1)S(1)}) custom-call(bf16[640,2048]{1,0:T(8,128)(2,1)} %bitcast.12, bf16[8,72,640]{2,1,0:T(8,128)(2,1)S(1)} %all_to_all.10.r_ref, bf16[400,2,36]{2,1,0:T(2,128)(2,1)S(1)} %bitcast.10, bf16[144,256]{1,0:T(8,128)(2,1)S(1)} %copy-done.2, ...), custom_call_target="tpu_custom_call" | custom-call | tf_op jit(solution)/shard_map/mode_mixing/pallas_call | solution.py:385
  24.4 10.1 %all_gather.3.v_ref = bf16[576,640]{1,0:T(8,128)(2,1)S(1)} all-gather(bf16[72,640]{1,0:T(8,128)(2,1)S(1)} %get-tuple-element.17), channel_id=1, replica_groups=mesh['dp'=4,'gx'=2,'gy'=4] {'gx','gy'}, dimensions={0}, use_global_device_ids=true | all-gather | bytes 829440 | tf_op jit(solution)/shard_map/all_gather | solution.py:403
  34.5 0.0 copy-done
  34.5 0.0 copy-done.7
  34.5 6.3 %cells.1 = (bf16[640,2048]{1,0:T(8,128)(2,1)}, bf16[8,368,128]{2,1,0:T(8,128)(2,1)S(1)}) custom-call(bf16[576,2048]{1,0:T(8,128)(2,1)S(1)} %get-tuple-element.13.t_ref, bf16[640,2048]{1,0:T(8,128)(2,1)S(1)} %copy-done, bf16[640,2048]{1,0:T(8,128)(2,1)S(1)} %get-tuple-element.16.cot_ref, bf16[576,640]{1,0:T(8,128)(2,1)S(1)} %all_gather.3.v_ref, ...), custom_call_target="tpu_custom_call" | custom-call | tf_op jit(solution)/shard_map/cells/pallas_call | solution.py:405
  40.8 14.1 %all_to_all.11.r_ref = bf16[8,368,128]{2,1,0:T(8,128)(2,1)S(1)} all-to-all(bf16[8,368,128]{2,1,0:T(8,128)(2,1)S(1)} %get-tuple-element.19), channel_id=1, replica_groups=mesh['dp'=4,'gx'=2,'gy'=4] {'gx','gy'}, dimensions={0} | all-to-all | bytes 1507328 | tf_op jit(solution)/shard_map/all_to_all | solution.py:423
  54.9 0.0 copy-done.3
  54.9 2.7 %mode_grads.1 = bf16[272,128]{1,0:T(8,128)(2,1)S(1)} custom-call(bf16[8,368,128]{2,1,0:T(8,128)(2,1)S(1)} %all_to_all.11.r_ref, f32[2,768,128]{2,1,0:T(8,128)S(1)} %get-tuple-element.20.s_ref, bf16[144,256]{1,0:T(8,128)(2,1)S(1)} %copy-done.2, bf16[512,256]{1,0:T(8,128)(2,1)S(1)} %copy-done.3, bf16[768,640]{1,0:T(8,128)(2,1)S(1)} %copy-done.1), custom_call_target="tpu_custom_call" | custom-call | tf_op jit(solution)/shard_map/mode_grads/pallas_call | solution.py:425
  57.6 1.6 %collective-permute-start = (bf16[272,128]{1,0:T(8,128)(2,1)S(1)}, bf16[272,128]{1,0:T(8,128)(2,1)S(1)}, u32[]{:S(2)}, u32[]{:S(2)}) collective-permute-start(bf16[272,128]{1,0:T(8,128)(2,1)S(1)} %mode_grads.1), channel_id=1, source_target_pairs={{0,8},{8,0},{16,24},{24,16},{1,9},{9,1},{17,25},{25,17},{2,10},{10... | collective-permute-start | bytes 208904 | tf_op jit(solution)/shard_map/ppermute | solution.py:338
  59.2 2.7 %collective-permute-done = bf16[272,128]{1,0:T(8,128)(2,1)S(1)} collective-permute-done((bf16[272,128]{1,0:T(8,128)(2,1)S(1)}, bf16[272,128]{1,0:T(8,128)(2,1)S(1)}, u32[]{:S(2)}, u32[]{:S(2)}) %collective-permute-start) | collective-permute-done | bytes 69664 | tf_op jit(solution)/shard_map/ppermute | solution.py:338
  61.9 0.1 fusion.10.own_ref
  62.1 2.7 %collective-permute-start.1 = (bf16[272,128]{1,0:T(8,128)(2,1)S(1)}, bf16[272,128]{1,0:T(8,128)(2,1)S(1)}, u32[]{:S(2)}, u32[]{:S(2)}) collective-permute-start(bf16[272,128]{1,0:T(8,128)(2,1)S(1)} %fusion.10.own_ref), channel_id=1, source_target_pairs={{0,16},{8,24},{16,0},{24,8},{1,17},{9,25},{17,1},{25,9},{2,18},{10... | collective-permute-start | bytes 208904 | tf_op jit(solution)/shard_map/ppermute | solution.py:338
  64.7 2.6 %collective-permute-done.1.other_ref = bf16[272,128]{1,0:T(8,128)(2,1)S(1)} collective-permute-done((bf16[272,128]{1,0:T(8,128)(2,1)S(1)}, bf16[272,128]{1,0:T(8,128)(2,1)S(1)}, u32[]{:S(2)}, u32[]{:S(2)}) %collective-permute-start.1) | collective-permute-done | bytes 69664 | tf_op jit(solution)/shard_map/ppermute | solution.py:338
  67.3 1.1 %gradients_out.1 = (f32[400,2,36]{2,1,0:T(2,128)}, f32[20,20]{1,0:T(8,128)}) custom-call(bf16[272,128]{1,0:T(8,128)(2,1)S(1)} %fusion.10.own_ref, bf16[272,128]{1,0:T(8,128)(2,1)S(1)} %collective-permute-done.1.other_ref), custom_call_target="tpu_custom_call" | custom-call | tf_op jit(solution)/shard_map/gradients_out/pallas_call | solution.py:433
  (5 shorter events, 0.0 us)
Async XLA Ops:
  0.6 21.0 %copy-start.2 = (bf16[144,256]{1,0:T(8,128)(2,1)S(1)}, bf16[144,256]{1,0:T(8,128)(2,1)}, u32[]{:S(2)}) copy-start(bf16[144,256]{1,0:T(8,128)(2,1)} %constant.26.clone.spread_ref) | copy-start | bytes 221188
  0.6 21.0 %copy-start.4 = (bf16[36,2,20,20]{0,1,3,2:T(2,128)(2,1)S(1)}, bf16[36,2,20,20]{0,1,3,2:T(2,128)(2,1)}, u32[]{:S(2)}) copy-start(bf16[36,2,20,20]{0,1,3,2:T(2,128)(2,1)} %param.13) | copy-start | bytes 172804
  0.7 21.0 %copy-start.5 = (bf16[72,256]{1,0:T(8,128)(2,1)S(1)}, bf16[72,256]{1,0:T(8,128)(2,1)}, u32[]{:S(2)}) copy-start(bf16[72,256]{1,0:T(8,128)(2,1)} %constant.28.clone.collect_ref) | copy-start | bytes 110596
  0.7 21.0 %copy-start.6 = (bf16[36,128]{1,0:T(8,128)(2,1)S(1)}, bf16[36,128]{1,0:T(8,128)(2,1)}, u32[]{:S(2)}) copy-start(bf16[36,128]{1,0:T(8,128)(2,1)} %constant.27.clone.wsel_ref) | copy-start | bytes 27652
  21.7 12.8 %copy-start = (bf16[640,2048]{1,0:T(8,128)(2,1)S(1)}, bf16[640,2048]{1,0:T(8,128)(2,1)}, u32[]{:S(2)}) copy-start(bf16[640,2048]{1,0:T(8,128)(2,1)} %get-tuple-element.14.f_ref) | copy-start | bytes 7864324
  21.7 12.8 %copy-start.7 = (bf16[20,20]{1,0:T(8,128)(2,1)S(1)}, bf16[20,20]{1,0:T(8,128)(2,1)}, u32[]{:S(2)}) copy-start(bf16[20,20]{1,0:T(8,128)(2,1)} %mix_ref.1) | copy-start | bytes 2404
  34.5 20.4 %copy-start.1 = (bf16[768,640]{1,0:T(8,128)(2,1)S(1)}, bf16[768,640]{1,0:T(8,128)(2,1)}, u32[]{:S(2)}) copy-start(bf16[768,640]{1,0:T(8,128)(2,1)} %constant.30.clone.order_ref) | copy-start | bytes 2949124
  34.5 20.4 %copy-start.3 = (bf16[512,256]{1,0:T(8,128)(2,1)S(1)}, bf16[512,256]{1,0:T(8,128)(2,1)}, u32[]{:S(2)}) copy-start(bf16[512,256]{1,0:T(8,128)(2,1)} %constant.29.clone.fold_ref) | copy-start | bytes 786436
  57.6 4.4 %collective-permute-start = (bf16[272,128]{1,0:T(8,128)(2,1)S(1)}, bf16[272,128]{1,0:T(8,128)(2,1)S(1)}, u32[]{:S(2)}, u32[]{:S(2)}) collective-permute-start(bf16[272,128]{1,0:T(8,128)(2,1)S(1)} %mode_grads.1), channel_id=1, source_target_pairs={{0,8},{8,0},{16,24},{24,16},{1,9},{9,1},{17,25},{25,17},{2,10},{10... | collective-permute-start | bytes 208904 | tf_op jit(solution)/shard_map/ppermute | solution.py:338
  62.1 5.3 %collective-permute-start.1 = (bf16[272,128]{1,0:T(8,128)(2,1)S(1)}, bf16[272,128]{1,0:T(8,128)(2,1)S(1)}, u32[]{:S(2)}, u32[]{:S(2)}) collective-permute-start(bf16[272,128]{1,0:T(8,128)(2,1)S(1)} %fusion.10.own_ref), channel_id=1, source_target_pairs={{0,16},{8,24},{16,0},{24,8},{1,17},{9,25},{17,1},{25,9},{2,18},{10... | collective-permute-start | bytes 208904 | tf_op jit(solution)/shard_map/ppermute | solution.py:338

commit v6 on v5

--- a/solution.py
+++ b/solution.py
@@ -21,6 +21,7 @@
 HP = 8
 PART = C * HP
 OUT_PARTS = 4
+ROWS = 240
 CR = 24
 SCALE = 1.6656925
 GROUP = ("gx", "gy")
@@ -304,35 +305,42 @@
     both = jnp.concatenate([hi, lo], 1)
     slots = dot(both, fold_ref[...], 1, 0)
     re, im = slots[:, 0:128], slots[:, 128:256]
-    middle = pltpu.roll(jnp.concatenate([re[272:], im[0:144]], 0), per, 1)
-    last = pltpu.roll(jnp.concatenate([im[144:], jnp.zeros((16, 128), F32)], 0), 2 * per, 1)
     lane = lax.broadcasted_iota(jnp.int32, (8, 128), 1)
     extra = extra + pltpu.roll(extra, 64, 1)
-    pieces = []
-    for k in range(3):
-        piece = pltpu.roll(extra, (3 * per - k * C) % 128, 1)
-        pieces.append(jnp.where(jnp.logical_and(lane >= 3 * per, lane < 3 * per + C), piece, 0.0))
-    pieces.append(jnp.zeros((272 - 24, 128), F32))
-    o_ref[...] = encode(re[0:272] + middle + last + jnp.concatenate(pieces, 0))
-
-
-def last_kernel(per, samples, own_ref, other_ref, grad_ref, mix_ref):
-    total = decode(own_ref[...]) + decode(other_ref[...])
+    slot = [im[320:], pltpu.roll(im[320:], 128 - C, 1)]
+    slot += [extra if k == 0 else pltpu.roll(extra, 128 - k * C, 1) for k in range(3)]
+    slot = jnp.concatenate(slot + [jnp.zeros((ROWS - 184, 128), F32)], 0)
+    narrow = lax.broadcasted_iota(jnp.int32, (ROWS, 128), 1) < C
+    payload = re[0:ROWS] + pltpu.roll(jnp.concatenate([re[ROWS:], im[0:80]], 0), per, 1)
+    payload = payload + pltpu.roll(im[80:320], 2 * per, 1)
+    o_ref[...] = encode(payload + pltpu.roll(jnp.where(narrow, slot, 0.0), 3 * per, 1))
+
+
+def last_kernel(per, samples, *refs):
+    parts, (grad_ref, mix_ref) = [decode(ref[...]) for ref in refs[:-2]], refs[-2:]
+    total = parts[0] + parts[1]
+    if len(parts) == 4:
+        total = total + (parts[2] + parts[3])
     grads = total * (1.0 / math.sqrt(samples * PL))
     one = pltpu.roll(grads, 128 - per, 1)
     two = pltpu.roll(grads, 128 - 2 * per, 1)
-    grad_ref[0:272, 0, :] = grads[:, 0:per]
-    grad_ref[272:400, 0, :] = one[0:128, 0:per]
-    grad_ref[0:144, 1, :] = one[128:272, 0:per]
-    grad_ref[144:400, 1, :] = two[0:256, 0:per]
-    mix = pltpu.roll(total[0:24], 128 - 3 * per, 1) * (1.0 / math.sqrt(samples * PL * NX * NY))
-    mix_ref[...] = mix[0:C, 0:C]
+    slot = pltpu.roll(total, 128 - 3 * per, 1)
+    grad_ref[0:240, 0, :] = grads[:, 0:per]
+    grad_ref[240:400, 0, :] = one[0:160, 0:per]
+    grad_ref[0:80, 1, :] = one[160:240, 0:per]
+    grad_ref[80:320, 1, :] = two[:, 0:per]
+    narrow = lax.broadcasted_iota(jnp.int32, (80, 128), 1) < C
+    rest = jnp.where(narrow, slot[0:80], pltpu.roll(slot[80:160], C, 1)) * (1.0 / math.sqrt(samples * PL))
+    grad_ref[320:400, 1, :] = rest[:, 0:per]
+    mix_ref[...] = slot[160 : 160 + C, 0:C] * (1.0 / math.sqrt(samples * PL * NX * NY))
 
 
 def sum_over_dp(coded, samples):
     if samples & (samples - 1) or samples == 1:
         total = jnp.sum(decode(lax.all_gather(coded, "dp", axis=0)), axis=0)
         return encode(total), jnp.zeros_like(coded)
+    if samples == 4:
+        return [coded] + [lax.ppermute(coded, "dp", [(i, i ^ k) for i in range(samples)]) for k in range(1, samples)]
     step = 1
     while True:
         other = lax.ppermute(coded, "dp", [(i, i ^ step) for i in range(samples)])
@@ -424,18 +432,18 @@
 
     coded = pl.pallas_call(
         functools.partial(grad_kernel, groups, rows, per),
-        out_shape=jax.ShapeDtypeStruct((272, 128), BF),
+        out_shape=jax.ShapeDtypeStruct((ROWS, 128), BF),
         scratch_shapes=[pltpu.VMEM((CR * PL, 128), F32), pltpu.VMEM((C * CR, 256), F32)],
         compiler_params=compiler_params(8),
         name="mode_grads",
     )(got, spec, spread, fold, plane_order())
-    own, other = sum_over_dp(coded, samples)
+    summands = sum_over_dp(coded, samples)
     grads, mixing_grad = pl.pallas_call(
         functools.partial(last_kernel, per, samples),
         out_shape=(jax.ShapeDtypeStruct((C * C, 2, per), F32), jax.ShapeDtypeStruct((C, C), F32)),
         compiler_params=compiler_params(8),
         name="gradients_out",
-    )(own, other)
+    )(*summands)
     spectral_grad = jnp.transpose(grads.reshape(C, C, 2, per), (3, 2, 0, 1))
     return (output.reshape(1, C, PL, cells), spectral_grad, mixing_grad)
 

time: 68.6 us -> 67.9 us (0.990)
  waiting for transfers between devices: 5.35 us -> 4.46 us
    ppermute x2 -> x3, waiting for transfers between devices: 5.35 us -> 4.46 us  [sum_over_dp(): lax.ppermute(coded, 'dp', [(i, i ^ k) for i in range(samples)])]
    ppermute x2 -> x3, starting transfers between devices: 4.3 us -> 4.45 us  [sum_over_dp(): lax.ppermute(coded, 'dp', [(i, i ^ k) for i in range(samples)])]
  transfers between devices with their start and end apart: 2 -> 3, of which waited for: 2 -> 3; matrix products, arithmetic and copies ran while one was open for 0% -> 0% of each run, Pallas kernels for 0% -> 0%
where the time goes in v6:
time: 67.9 us; the launch traced here: 67.7 us
  blocking collectives  40.6 us (60%)
  Pallas kernels  17.4 us (26%)
  waiting for transfers between devices  4.46 us (7%)
  starting transfers between devices  4.45 us (7%)
  between operations  0.73 us (1%)
    all_to_all x2, blocking collectives, local(): got = lax.all_to_all(sent, GROUP, 0, 0, tiled=True)  30.5 us
    all_gather x1, blocking collectives, local(): all_vals = lax.all_gather(vals, GROUP, axis=0, tiled=True)  10.1 us
    pallas_call x1, Pallas kernels, local(): pl.pallas_call(functools.partial(main_kernel, groups, rows, 1), in_specs=...  6.26 us
    pallas_call x1, Pallas kernels, local(): pl.pallas_call(functools.partial(first_kernel, groups, rows, halves), in_...  4.56 us
    ppermute x3, waiting for transfers between devices, sum_over_dp(): lax.ppermute(coded, 'dp', [(i, i ^ k) for i in range(samples)])  4.46 us
    ppermute x3, starting transfers between devices, sum_over_dp(): lax.ppermute(coded, 'dp', [(i, i ^ k) for i in range(samples)])  4.45 us
    pallas_call x1, Pallas kernels, local(): pl.pallas_call(functools.partial(grad_kernel, groups, rows, per), out_sha...  2.77 us
    pallas_call x1, Pallas kernels, local(): pl.pallas_call(functools.partial(mix_kernel, groups, rows), in_specs=[hbm...  2.73 us
  transfers between devices with their start and end apart: 3, of which 3 were waited for; matrix products, arithmetic and copies ran while one was open for 0% of the time, Pallas kernels for 0%

profile of v6, /device:TPU:0, one launch (start us, length us, event | category | flops | bytes accessed | tf_op | source)
XLA Modules:
  0.0 67.7 jit_solution(16284600356994123546)
XLA Ops:
  0.6 0.0 copy-start.2
  0.6 0.0 copy-start.4
  0.7 0.0 copy-start.5
  0.7 0.0 copy-start.6
  0.7 4.6 %spectrum_parts.1 = (bf16[8,72,640]{2,1,0:T(8,128)(2,1)S(1)}, bf16[640,2048]{1,0:T(8,128)(2,1)}, bf16[576,2048]{1,0:T(8,128)(2,1)S(1)}) custom-call(s32[1]{0:T(128)} %bitcast.gid_ref, bf16[640,2048]{1,0:T(8,128)(2,1)} %bitcast.11, bf16[8,576,2048]{2,1,0:T(8,128)(2,1)} %constant.23.clone.t_hbm), custom_call_target="tpu_custom_call" | custom-call | tf_op jit(solution)/shard_map/spectrum_parts/pallas_call | solution.py:374
  5.2 16.4 %all_to_all.10.r_ref = bf16[8,72,640]{2,1,0:T(8,128)(2,1)S(1)} all-to-all(bf16[8,72,640]{2,1,0:T(8,128)(2,1)S(1)} %get-tuple-element.15), channel_id=1, replica_groups=mesh['dp'=4,'gx'=2,'gy'=4] {'gx','gy'}, dimensions={0} | all-to-all | bytes 1474560 | tf_op jit(solution)/shard_map/all_to_all | solution.py:390
  21.7 0.0 copy-done.2
  21.7 0.0 copy-done.4
  21.7 0.0 copy-done.5
  21.7 0.0 copy-done.6
  21.7 2.7 %mode_mixing.1 = (bf16[72,640]{1,0:T(8,128)(2,1)S(1)}, f32[2,768,128]{2,1,0:T(8,128)S(1)}, bf16[640,2048]{1,0:T(8,128)(2,1)S(1)}) custom-call(bf16[640,2048]{1,0:T(8,128)(2,1)} %bitcast.12, bf16[8,72,640]{2,1,0:T(8,128)(2,1)S(1)} %all_to_all.10.r_ref, bf16[400,2,36]{2,1,0:T(2,128)(2,1)S(1)} %bitcast.10, bf16[144,256]{1,0:T(8,128)(2,1)S(1)} %copy-done.2, ...), custom_call_target="tpu_custom_call" | custom-call | tf_op jit(solution)/shard_map/mode_mixing/pallas_call | solution.py:393
  24.4 10.1 %all_gather.3.v_ref = bf16[576,640]{1,0:T(8,128)(2,1)S(1)} all-gather(bf16[72,640]{1,0:T(8,128)(2,1)S(1)} %get-tuple-element.17), channel_id=1, replica_groups=mesh['dp'=4,'gx'=2,'gy'=4] {'gx','gy'}, dimensions={0}, use_global_device_ids=true | all-gather | bytes 829440 | tf_op jit(solution)/shard_map/all_gather | solution.py:411
  34.5 0.0 copy-done
  34.5 0.0 copy-done.7
  34.5 6.3 %cells.1 = (bf16[640,2048]{1,0:T(8,128)(2,1)}, bf16[8,368,128]{2,1,0:T(8,128)(2,1)S(1)}) custom-call(bf16[576,2048]{1,0:T(8,128)(2,1)S(1)} %get-tuple-element.13.t_ref, bf16[640,2048]{1,0:T(8,128)(2,1)S(1)} %copy-done, bf16[640,2048]{1,0:T(8,128)(2,1)S(1)} %get-tuple-element.16.cot_ref, bf16[576,640]{1,0:T(8,128)(2,1)S(1)} %all_gather.3.v_ref, ...), custom_call_target="tpu_custom_call" | custom-call | tf_op jit(solution)/shard_map/cells/pallas_call | solution.py:413
  40.8 14.1 %all_to_all.11.r_ref = bf16[8,368,128]{2,1,0:T(8,128)(2,1)S(1)} all-to-all(bf16[8,368,128]{2,1,0:T(8,128)(2,1)S(1)} %get-tuple-element.19), channel_id=1, replica_groups=mesh['dp'=4,'gx'=2,'gy'=4] {'gx','gy'}, dimensions={0} | all-to-all | bytes 1507328 | tf_op jit(solution)/shard_map/all_to_all | solution.py:431
  54.9 2.8 %mode_grads.1.refs_0_ = bf16[240,128]{1,0:T(8,128)(2,1)S(1)} custom-call(bf16[8,368,128]{2,1,0:T(8,128)(2,1)S(1)} %all_to_all.11.r_ref, f32[2,768,128]{2,1,0:T(8,128)S(1)} %get-tuple-element.20.s_ref, bf16[144,256]{1,0:T(8,128)(2,1)S(1)} %copy-done.2, bf16[512,256]{1,0:T(8,128)(2,1)S(1)} %copy-done.3, bf16[768,640]{1,0:T(8,128)(2,1)S(1)} %copy-done.1), custom_call_target="tpu_custom_call" | custom-call | tf_op jit(solution)/shard_map/mode_grads/pallas_call | solution.py:433
  57.6 3.7 %collective-permute-start.2 = (bf16[240,128]{1,0:T(8,128)(2,1)S(1)}, bf16[240,128]{1,0:T(8,128)(2,1)S(1)}, u32[]{:S(2)}, u32[]{:S(2)}) collective-permute-start(bf16[240,128]{1,0:T(8,128)(2,1)S(1)} %mode_grads.1.refs_0_), channel_id=1, source_target_pairs={{0,24},{8,16},{16,8},{24,0},{1,25},{9,17},{17,9},{25,1},{2,26},{10... | collective-permute-start | bytes 184328 | tf_op jit(solution)/shard_map/ppermute | solution.py:343
  61.3 0.0 collective-permute-start.1
  61.3 0.8 %collective-permute-start = (bf16[240,128]{1,0:T(8,128)(2,1)S(1)}, bf16[240,128]{1,0:T(8,128)(2,1)S(1)}, u32[]{:S(2)}, u32[]{:S(2)}) collective-permute-start(bf16[240,128]{1,0:T(8,128)(2,1)S(1)} %mode_grads.1.refs_0_), channel_id=1, source_target_pairs={{0,8},{8,0},{16,24},{24,16},{1,9},{9,1},{17,25},{25,17},{2,10},{10... | collective-permute-start | bytes 184328 | tf_op jit(solution)/shard_map/ppermute | solution.py:343
  62.1 2.3 %collective-permute-done.2.refs_3_ = bf16[240,128]{1,0:T(8,128)(2,1)S(1)} collective-permute-done((bf16[240,128]{1,0:T(8,128)(2,1)S(1)}, bf16[240,128]{1,0:T(8,128)(2,1)S(1)}, u32[]{:S(2)}, u32[]{:S(2)}) %collective-permute-start.2) | collective-permute-done | bytes 61472 | tf_op jit(solution)/shard_map/ppermute | solution.py:343
  64.4 2.1 %collective-permute-done.1.refs_2_ = bf16[240,128]{1,0:T(8,128)(2,1)S(1)} collective-permute-done((bf16[240,128]{1,0:T(8,128)(2,1)S(1)}, bf16[240,128]{1,0:T(8,128)(2,1)S(1)}, u32[]{:S(2)}, u32[]{:S(2)}) %collective-permute-start.1) | collective-permute-done | bytes 61472 | tf_op jit(solution)/shard_map/ppermute | solution.py:343
  66.5 0.1 collective-permute-done.refs_1_
  66.6 1.1 %gradients_out.1 = (f32[400,2,36]{2,1,0:T(2,128)}, f32[20,20]{1,0:T(8,128)}) custom-call(bf16[240,128]{1,0:T(8,128)(2,1)S(1)} %mode_grads.1.refs_0_, bf16[240,128]{1,0:T(8,128)(2,1)S(1)} %collective-permute-done.refs_1_, bf16[240,128]{1,0:T(8,128)(2,1)S(1)} %collective-permute-done.1.refs_2_, bf16[240,128]{1,0:T(8,128)(2,1)S(1)} %collective-permute-done.2.refs_3_), custom_call_target="tpu_custom_call" | custom-call | tf_op jit(solution)/shard_map/gradients_out/pallas_call | solution.py:441
  (6 shorter events, 0.0 us)
Async XLA Ops:
  0.6 21.0 %copy-start.2 = (bf16[144,256]{1,0:T(8,128)(2,1)S(1)}, bf16[144,256]{1,0:T(8,128)(2,1)}, u32[]{:S(2)}) copy-start(bf16[144,256]{1,0:T(8,128)(2,1)} %constant.24.clone.spread_ref) | copy-start | bytes 221188
  0.6 21.0 %copy-start.4 = (bf16[36,2,20,20]{0,1,3,2:T(2,128)(2,1)S(1)}, bf16[36,2,20,20]{0,1,3,2:T(2,128)(2,1)}, u32[]{:S(2)}) copy-start(bf16[36,2,20,20]{0,1,3,2:T(2,128)(2,1)} %param.13) | copy-start | bytes 172804
  0.7 21.0 %copy-start.5 = (bf16[72,256]{1,0:T(8,128)(2,1)S(1)}, bf16[72,256]{1,0:T(8,128)(2,1)}, u32[]{:S(2)}) copy-start(bf16[72,256]{1,0:T(8,128)(2,1)} %constant.26.clone.collect_ref) | copy-start | bytes 110596
  0.7 21.0 %copy-start.6 = (bf16[36,128]{1,0:T(8,128)(2,1)S(1)}, bf16[36,128]{1,0:T(8,128)(2,1)}, u32[]{:S(2)}) copy-start(bf16[36,128]{1,0:T(8,128)(2,1)} %constant.25.clone.wsel_ref) | copy-start | bytes 27652
  21.7 12.8 %copy-start = (bf16[640,2048]{1,0:T(8,128)(2,1)S(1)}, bf16[640,2048]{1,0:T(8,128)(2,1)}, u32[]{:S(2)}) copy-start(bf16[640,2048]{1,0:T(8,128)(2,1)} %get-tuple-element.14.f_ref) | copy-start | bytes 7864324
  21.7 12.8 %copy-start.7 = (bf16[20,20]{1,0:T(8,128)(2,1)S(1)}, bf16[20,20]{1,0:T(8,128)(2,1)}, u32[]{:S(2)}) copy-start(bf16[20,20]{1,0:T(8,128)(2,1)} %mix_ref.1) | copy-start | bytes 2404
  34.5 20.4 %copy-start.1 = (bf16[768,640]{1,0:T(8,128)(2,1)S(1)}, bf16[768,640]{1,0:T(8,128)(2,1)}, u32[]{:S(2)}) copy-start(bf16[768,640]{1,0:T(8,128)(2,1)} %constant.28.clone.order_ref) | copy-start | bytes 2949124
  34.5 20.4 %copy-start.3 = (bf16[512,256]{1,0:T(8,128)(2,1)S(1)}, bf16[512,256]{1,0:T(8,128)(2,1)}, u32[]{:S(2)}) copy-start(bf16[512,256]{1,0:T(8,128)(2,1)} %constant.27.clone.fold_ref) | copy-start | bytes 786436
  57.6 6.8 %collective-permute-start.2 = (bf16[240,128]{1,0:T(8,128)(2,1)S(1)}, bf16[240,128]{1,0:T(8,128)(2,1)S(1)}, u32[]{:S(2)}, u32[]{:S(2)}) collective-permute-start(bf16[240,128]{1,0:T(8,128)(2,1)S(1)} %mode_grads.1.refs_0_), channel_id=1, source_target_pairs={{0,24},{8,16},{16,8},{24,0},{1,25},{9,17},{17,9},{25,1},{2,26},{10... | collective-permute-start | bytes 184328 | tf_op jit(solution)/shard_map/ppermute | solution.py:343
  61.3 5.2 %collective-permute-start.1 = (bf16[240,128]{1,0:T(8,128)(2,1)S(1)}, bf16[240,128]{1,0:T(8,128)(2,1)S(1)}, u32[]{:S(2)}, u32[]{:S(2)}) collective-permute-start(bf16[240,128]{1,0:T(8,128)(2,1)S(1)} %mode_grads.1.refs_0_), channel_id=1, source_target_pairs={{0,16},{8,24},{16,0},{24,8},{1,17},{9,25},{17,1},{25,9},{2,18},{10... | collective-permute-start | bytes 184328 | tf_op jit(solution)/shard_map/ppermute | solution.py:343
  61.3 5.2 %collective-permute-start = (bf16[240,128]{1,0:T(8,128)(2,1)S(1)}, bf16[240,128]{1,0:T(8,128)(2,1)S(1)}, u32[]{:S(2)}, u32[]{:S(2)}) collective-permute-start(bf16[240,128]{1,0:T(8,128)(2,1)S(1)} %mode_grads.1.refs_0_), channel_id=1, source_target_pairs={{0,8},{8,0},{16,24},{24,16},{1,9},{9,1},{17,25},{25,17},{2,10},{10... | collective-permute-start | bytes 184328 | tf_op jit(solution)/shard_map/ppermute | solution.py:343

commit v7 on v6

--- a/solution.py
+++ b/solution.py
@@ -21,6 +21,7 @@
 HP = 8
 PART = C * HP
 OUT_PARTS = 4
+MAIN = 32
 ROWS = 240
 CR = 24
 SCALE = 1.6656925
@@ -56,27 +57,26 @@
     per = MODES // groups
     rows = round_up(2 * per, 8)
     re, im = np.arange(per), per + np.arange(per)
-    spread = np.zeros((rows, 256), np.float32)
-    spread[re, re] = 1
-    spread[im, im] = 1
-    spread[im, 128 + re] = -1
-    spread[re, 128 + im] = 1
-    weights = np.zeros((per, 128), np.float32)
-    weights[re, re] = 1
-    weights[re, im] = 1
-    collect = np.zeros((rows, 128), np.float32)
-    collect[re, re] = 1
-    collect[im, im] = 1
+    main = min(per, MAIN)
+    pairs = np.zeros((rows, 512), np.float32)
+    weights = np.zeros((2, per, 256), np.float32)
+    collect = np.zeros((rows, 256), np.float32)
     fold = np.zeros((256, 256), np.float32)
-    for first in (0, 128):
-        fold[first + re, first + re] = 1
-        fold[first + im, first + re] = 1
+    for k, (s_row, s_sign, g_row) in enumerate(((re, 1, re), (im, 1, im), (im, -1, re), (re, 1, im))):
+        for m in range(per):
+            places = [k * MAIN + m] if m < main else [128 + 16 * j + 4 * k + m - main for j in range(8)]
+            for at in places:
+                pairs[s_row[m], at] = s_sign
+                pairs[g_row[m], 256 + at] = 1
+                fold[at, 128 * (k // 2) + m] = 1
+                weights[k // 2, m, at] = 1
+                collect[(re, im)[k % 2][m], at] = 1
     cast = lambda a: a.astype(ml_dtypes.bfloat16)
     return (
-        cast(np.concatenate([spread, spread], 0)),
         cast(weights),
         cast(np.concatenate([collect, collect], 1)),
         cast(np.concatenate([fold, fold], 0)),
+        cast(np.concatenate([pairs, pairs], 0)),
     )
 
 
@@ -162,9 +162,25 @@
     return x.reshape(C, PL // HP, HP, x.shape[1])[:, h].reshape(PART, x.shape[1])
 
 
+def own_group():
+    shape = (PL // 8, 8, 128)
+    group = 2 * lax.broadcasted_iota(jnp.int32, shape, 0) + lax.div(lax.broadcasted_iota(jnp.int32, shape, 1), 4)
+    return group == lax.div(lax.broadcasted_iota(jnp.int32, shape, 2), 16)
+
+
+def across_lanes(x):
+    x = jnp.where(own_group()[None], x.reshape(C, PL // 8, 8, 128), 0.0)
+    x = jnp.sum(x, axis=1)
+    return (x + jnp.concatenate([x[:, 4:], x[:, :4]], 1)).reshape(C * 8, 128)
+
+
+def along_planes(x):
+    return jnp.where(own_group()[None], x.reshape(C, 1, 8, 128), 0.0).reshape(CP, 128)
+
+
 def mix_kernel(
-    groups, rows, cot_hbm, r_ref, w_ref, spread_ref, wsel_ref, collect_ref, v_ref, s_ref, cot_ref,
-    wa_ref, wb_ref, vals_ref, sem,
+    groups, rows, per, cot_hbm, r_ref, w_ref, wsel_ref, collect_ref, pairs_ref,
+    v_ref, spec_ref, spec_rest_ref, cot_ref, weights_ref, vals_ref, rest_ref, sem,
 ):
     cot_copy = pltpu.make_async_copy(cot_hbm, cot_ref, sem.at[0])
     cot_copy.start()
@@ -174,30 +190,29 @@
     total = total * (1.0 / (SCALE * math.sqrt(NX * NY)))
     hi, lo = split(total)
     both = jnp.concatenate([hi.astype(F32), lo.astype(F32)], 0).astype(BF)
-    s_ref[0, 0:CP, :] = dot(both, spread_ref[:, 0:128], 0, 0)
-    s_ref[1, 0:CP, :] = dot(both, spread_ref[:, 128:256], 0, 0)
-    s_ref[:, CP:, :] = jnp.zeros((2, CR * PL - CP, 128), F32)
+    spec_ref[...] = dot(both, pairs_ref[:, 0:128], 0, 0)
+    spec_rest_ref[...] = across_lanes(dot(both, pairs_ref[:, 128:256], 0, 0))
     w = w_ref[...].astype(F32)
-    wa_ref[...] = dot(w[:, 0, :].astype(BF), wsel_ref[...], 1, 0)
-    wb_ref[...] = dot(w[:, 1, :].astype(BF), wsel_ref[...], 1, 0)
-
-    def some(block, _):
-        base = block * 4
-        acc = [None] * 4
+    weights_ref[...] = dot(w[:, 0, :].astype(BF), wsel_ref[0], 1, 0) + dot(w[:, 1, :].astype(BF), wsel_ref[1], 1, 0)
+
+    for base in range(0, C, 4):
+        main = [None] * 4
+        rest = [None] * 4
         for c in range(C):
-            s = s_ref[0, c * PL : (c + 1) * PL, :]
-            t = s_ref[1, c * PL : (c + 1) * PL, :]
+            s = spec_ref[c * PL : (c + 1) * PL, :]
+            t = spec_rest_ref[c * 8 : (c + 1) * 8, :]
             for k in range(4):
                 row = c * C + base + k
-                term = s * wa_ref[pl.ds(row, 1), :] + t * wb_ref[pl.ds(row, 1), :]
-                acc[k] = term if acc[k] is None else acc[k] + term
+                one = s * weights_ref[row : row + 1, 0:128]
+                main[k] = one if main[k] is None else main[k] + one
+                two = t * weights_ref[row : row + 1, 128:256]
+                rest[k] = two if rest[k] is None else rest[k] + two
         for k in range(4):
-            vals_ref[pl.ds(pl.multiple_of((base + k) * PL, PL), PL), :] = acc[k]
-        return 0
-
-    lax.fori_loop(0, C // 4, some, 0)
-    vals = vals_ref[...] * (1.0 / (SCALE * math.sqrt(MODES)))
-    hi, lo = split(vals)
+            d = base + k
+            vals_ref[d * PL : (d + 1) * PL, :] = main[k]
+            rest_ref[d * 8 : (d + 1) * 8, :] = rest[k]
+    vals = jnp.concatenate([vals_ref[...], along_planes(rest_ref[...])], 1)
+    hi, lo = split(vals * (1.0 / (SCALE * math.sqrt(MODES))))
     v_ref[...] = dot(collect_ref[...], jnp.concatenate([hi, lo], 1), 1, 1).astype(BF)
     cot_copy.wait()
 
@@ -269,7 +284,9 @@
         copy.wait()
 
 
-def grad_kernel(groups, rows, per, r_ref, s_ref, spread_ref, fold_ref, order_ref, o_ref, g_ref, p_ref):
+def grad_kernel(
+    groups, rows, per, r_ref, s_ref, s_rest_ref, pairs_ref, fold_ref, order_ref, o_ref, g_ref, p_ref, g_rest_ref
+):
     high = rows * CP // 128
     total = None
     extra = None
@@ -283,20 +300,28 @@
     total = jnp.concatenate([total[i * rows : (i + 1) * rows] for i in range(CP // 128)], 1)
     hi, lo = split(total)
     both = jnp.concatenate([hi.astype(F32), lo.astype(F32)], 0).astype(BF)
-    hi, lo = split(dot(both, spread_ref[:, 0:128], 0, 0))
+    hi, lo = split(dot(both, pairs_ref[:, 256:384], 0, 0))
     by_plane = dot(order_ref[...], jnp.concatenate([hi, lo], 1), 1, 0)
     g_ref[...] = by_plane[:, 0:128] + by_plane[:, 128:256]
 
-    for base in range(0, C, 4):
-        one = [jnp.zeros((CR, 128), F32)] * 4
-        two = [jnp.zeros((CR, 128), F32)] * 4
+    rest = per > MAIN
+    if rest:
+        g_rest_ref[0 : C * 8, :] = across_lanes(dot(both, pairs_ref[:, 384:512], 0, 0))
+        g_rest_ref[C * 8 :, :] = jnp.zeros(((CR + 1 - C) * 8, 128), F32)
+    for base in range(0, C, 5):
+        one = [jnp.zeros((CR, 128), F32)] * 5
+        two = [jnp.zeros((CR, 128), F32)] * 5
         for p in range(PL):
             g = g_ref[p * CR : (p + 1) * CR, :]
-            for k in range(4):
+            for k in range(5):
                 row = (base + k) * PL + p
-                one[k] = one[k] + s_ref[0, row : row + 1, :] * g
-                two[k] = two[k] + s_ref[1, row : row + 1, :] * g
-        for k in range(4):
+                one[k] = one[k] + s_ref[row : row + 1, :] * g
+        for p in range(4 if rest else 0):
+            g = g_rest_ref[pl.ds(p, CR, stride=8), :]
+            for k in range(5):
+                row = (base + k) * 8 + p
+                two[k] = two[k] + s_rest_ref[row : row + 1, :] * g
+        for k in range(5):
             at = (base + k) * CR
             p_ref[at : at + CR, 0:128] = one[k]
             p_ref[at : at + CR, 128:256] = two[k]
@@ -355,7 +380,7 @@
 
 
 def local(tables, consts, fields, cotangent, mix_weight, spectral_weight):
-    spread, wsel, collect, fold = consts
+    wsel, collect, fold, pairs = consts
     cells = fields.shape[3]
     groups = lax.axis_size("gx") * lax.axis_size("gy")
     samples = lax.axis_size("dp")
@@ -390,24 +415,25 @@
     got = lax.all_to_all(sent, GROUP, 0, 0, tiled=True)
 
     weights = jnp.transpose(spectral_weight, (2, 3, 1, 0)).reshape(C * C, 2, per)
-    vals, spec, cot_in = pl.pallas_call(
-        functools.partial(mix_kernel, groups, rows),
+    vals, spec, spec_rest, cot_in = pl.pallas_call(
+        functools.partial(mix_kernel, groups, rows, per),
         in_specs=[hbm] + [vmem] * 5,
-        out_specs=[vmem] * 3,
+        out_specs=[vmem] * 4,
         out_shape=[
             jax.ShapeDtypeStruct((rows, CP), BF),
-            jax.ShapeDtypeStruct((2, CR * PL, 128), F32),
+            jax.ShapeDtypeStruct((CP, 128), F32),
+            jax.ShapeDtypeStruct((C * 8, 128), F32),
             jax.ShapeDtypeStruct((CP, cells), BF),
         ],
         scratch_shapes=[
-            pltpu.VMEM((C * C, 128), F32),
-            pltpu.VMEM((C * C, 128), F32),
+            pltpu.VMEM((C * C, 256), F32),
             pltpu.VMEM((CP, 128), F32),
+            pltpu.VMEM((C * 8, 128), F32),
             pltpu.SemaphoreType.DMA((1,)),
         ],
         compiler_params=compiler_params(48),
         name="mode_mixing",
-    )(cot, got, weights, spread, wsel, collect)
+    )(cot, got, weights, wsel, collect, pairs)
     all_vals = lax.all_gather(vals, GROUP, axis=0, tiled=True)
 
     output, sent = pl.pallas_call(
@@ -433,10 +459,10 @@
     coded = pl.pallas_call(
         functools.partial(grad_kernel, groups, rows, per),
         out_shape=jax.ShapeDtypeStruct((ROWS, 128), BF),
-        scratch_shapes=[pltpu.VMEM((CR * PL, 128), F32), pltpu.VMEM((C * CR, 256), F32)],
+        scratch_shapes=[pltpu.VMEM((CR * PL, 128), F32), pltpu.VMEM((C * CR, 256), F32), pltpu.VMEM(((CR + 1) * 8, 128), F32)],
         compiler_params=compiler_params(8),
         name="mode_grads",
-    )(got, spec, spread, fold, plane_order())
+    )(got, spec, spec_rest, pairs, fold, plane_order())
     summands = sum_over_dp(coded, samples)
     grads, mixing_grad = pl.pallas_call(
         functools.partial(last_kernel, per, samples),

time: 67.9 us -> 66.6 us (0.981)
  Pallas kernels: 17.4 us -> 16.1 us
    pallas_call x1, Pallas kernels: 2.73 us -> 1.94 us  [local(): pl.pallas_call(functools.partial(mix_kernel, groups, rows, per), in_specs...]
where the time goes in v7:
time: 66.6 us; the launch traced here: 66.3 us
  blocking collectives  40.6 us (61%)
  Pallas kernels  16.1 us (24%)
  starting transfers between devices  4.45 us (7%)
  waiting for transfers between devices  4.45 us (7%)
  between operations  0.73 us (1%)
    all_to_all x2, blocking collectives, local(): got = lax.all_to_all(sent, GROUP, 0, 0, tiled=True)  30.5 us
    all_gather x1, blocking collectives, local(): all_vals = lax.all_gather(vals, GROUP, axis=0, tiled=True)  10.1 us
    pallas_call x1, Pallas kernels, local(): pl.pallas_call(functools.partial(main_kernel, groups, rows, 1), in_specs=...  6.29 us
    pallas_call x1, Pallas kernels, local(): pl.pallas_call(functools.partial(first_kernel, groups, rows, halves), in_...  4.56 us
    ppermute x3, starting transfers between devices, sum_over_dp(): lax.ppermute(coded, 'dp', [(i, i ^ k) for i in range(samples)])  4.45 us
    ppermute x3, waiting for transfers between devices, sum_over_dp(): lax.ppermute(coded, 'dp', [(i, i ^ k) for i in range(samples)])  4.45 us
    pallas_call x1, Pallas kernels, local(): pl.pallas_call(functools.partial(grad_kernel, groups, rows, per), out_sha...  2.16 us
    pallas_call x1, Pallas kernels, local(): pl.pallas_call(functools.partial(mix_kernel, groups, rows, per), in_specs...  1.94 us
  transfers between devices with their start and end apart: 3, of which 3 were waited for; matrix products, arithmetic and copies ran while one was open for 0% of the time, Pallas kernels for 0%

profile of v7, /device:TPU:0, one launch (start us, length us, event | category | flops | bytes accessed | tf_op | source)
XLA Modules:
  0.0 66.3 jit_solution(11461662586674959469)
XLA Ops:
  0.6 0.0 copy-start.2
  0.6 0.0 copy-start.4
  0.7 0.0 copy-start.5
  0.7 0.0 copy-start.6
  0.7 4.6 %spectrum_parts.1 = (bf16[8,72,640]{2,1,0:T(8,128)(2,1)S(1)}, bf16[640,2048]{1,0:T(8,128)(2,1)}, bf16[576,2048]{1,0:T(8,128)(2,1)S(1)}) custom-call(s32[1]{0:T(128)} %bitcast.gid_ref, bf16[640,2048]{1,0:T(8,128)(2,1)} %bitcast.11, bf16[8,576,2048]{2,1,0:T(8,128)(2,1)} %constant.23.clone.t_hbm), custom_call_target="tpu_custom_call" | custom-call | tf_op jit(solution)/shard_map/spectrum_parts/pallas_call | solution.py:399
  5.3 16.4 %all_to_all.10.r_ref = bf16[8,72,640]{2,1,0:T(8,128)(2,1)S(1)} all-to-all(bf16[8,72,640]{2,1,0:T(8,128)(2,1)S(1)} %get-tuple-element.16), channel_id=1, replica_groups=mesh['dp'=4,'gx'=2,'gy'=4] {'gx','gy'}, dimensions={0} | all-to-all | bytes 1474560 | tf_op jit(solution)/shard_map/all_to_all | solution.py:415
  21.7 0.0 copy-done.2
  21.7 0.0 copy-done.4
  21.7 0.0 copy-done.5
  21.7 0.0 copy-done.6
  21.7 1.9 %mode_mixing.1 = (bf16[72,640]{1,0:T(8,128)(2,1)S(1)}, f32[640,128]{1,0:T(8,128)S(1)}, f32[160,128]{1,0:T(8,128)S(1)}, bf16[640,2048]{1,0:T(8,128)(2,1)S(1)}) custom-call(bf16[640,2048]{1,0:T(8,128)(2,1)} %bitcast.12, bf16[8,72,640]{2,1,0:T(8,128)(2,1)S(1)} %all_to_all.10.r_ref, bf16[400,2,36]{2,1,0:T(2,128)(2,1)S(1)} %bitcast.10, ...), custom_call_target="tpu_custom_call" | custom-call | tf_op jit(solution)/shard_map/mode_mixing/pallas_call | solution.py:418
  23.6 10.1 %all_gather.3.v_ref = bf16[576,640]{1,0:T(8,128)(2,1)S(1)} all-gather(bf16[72,640]{1,0:T(8,128)(2,1)S(1)} %get-tuple-element.18), channel_id=1, replica_groups=mesh['dp'=4,'gx'=2,'gy'=4] {'gx','gy'}, dimensions={0}, use_global_device_ids=true | all-gather | bytes 829440 | tf_op jit(solution)/shard_map/all_gather | solution.py:437
  33.7 0.0 copy-done
  33.7 0.0 copy-done.7
  33.7 6.3 %cells.1 = (bf16[640,2048]{1,0:T(8,128)(2,1)}, bf16[8,368,128]{2,1,0:T(8,128)(2,1)S(1)}) custom-call(bf16[576,2048]{1,0:T(8,128)(2,1)S(1)} %get-tuple-element.14.t_ref, bf16[640,2048]{1,0:T(8,128)(2,1)S(1)} %copy-done, bf16[640,2048]{1,0:T(8,128)(2,1)S(1)} %get-tuple-element.17.cot_ref, bf16[576,640]{1,0:T(8,128)(2,1)S(1)} %all_gather.3.v_ref, ...), custom_call_target="tpu_custom_call" | custom-call | tf_op jit(solution)/shard_map/cells/pallas_call | solution.py:439
  40.0 14.1 %all_to_all.11.r_ref = bf16[8,368,128]{2,1,0:T(8,128)(2,1)S(1)} all-to-all(bf16[8,368,128]{2,1,0:T(8,128)(2,1)S(1)} %get-tuple-element.20), channel_id=1, replica_groups=mesh['dp'=4,'gx'=2,'gy'=4] {'gx','gy'}, dimensions={0} | all-to-all | bytes 1507328 | tf_op jit(solution)/shard_map/all_to_all | solution.py:457
  54.1 2.2 %mode_grads.1.refs_0_ = bf16[240,128]{1,0:T(8,128)(2,1)S(1)} custom-call(bf16[8,368,128]{2,1,0:T(8,128)(2,1)S(1)} %all_to_all.11.r_ref, f32[640,128]{1,0:T(8,128)S(1)} %get-tuple-element.21.s_ref, f32[160,128]{1,0:T(8,128)S(1)} %get-tuple-element.22.s_rest_ref, bf16[144,512]{1,0:T(8,128)(2,1)S(1)} %copy-done.2, bf16[512,256]{1,0:T(8,128)(2,1)S(1)} %copy-done.3, ...), custom_call_target="tpu_custom_call" | custom-call | tf_op jit(solution)/shard_map/mode_grads/pallas_call | solution.py:459
  56.3 3.7 %collective-permute-start.2 = (bf16[240,128]{1,0:T(8,128)(2,1)S(1)}, bf16[240,128]{1,0:T(8,128)(2,1)S(1)}, u32[]{:S(2)}, u32[]{:S(2)}) collective-permute-start(bf16[240,128]{1,0:T(8,128)(2,1)S(1)} %mode_grads.1.refs_0_), channel_id=1, source_target_pairs={{0,24},{8,16},{16,8},{24,0},{1,25},{9,17},{17,9},{25,1},{2,26},{10... | collective-permute-start | bytes 184328 | tf_op jit(solution)/shard_map/ppermute | solution.py:368
  59.9 0.0 collective-permute-start.1
  59.9 0.8 %collective-permute-start = (bf16[240,128]{1,0:T(8,128)(2,1)S(1)}, bf16[240,128]{1,0:T(8,128)(2,1)S(1)}, u32[]{:S(2)}, u32[]{:S(2)}) collective-permute-start(bf16[240,128]{1,0:T(8,128)(2,1)S(1)} %mode_grads.1.refs_0_), channel_id=1, source_target_pairs={{0,8},{8,0},{16,24},{24,16},{1,9},{9,1},{17,25},{25,17},{2,10},{10... | collective-permute-start | bytes 184328 | tf_op jit(solution)/shard_map/ppermute | solution.py:368
  60.7 2.3 %collective-permute-done.2.refs_3_ = bf16[240,128]{1,0:T(8,128)(2,1)S(1)} collective-permute-done((bf16[240,128]{1,0:T(8,128)(2,1)S(1)}, bf16[240,128]{1,0:T(8,128)(2,1)S(1)}, u32[]{:S(2)}, u32[]{:S(2)}) %collective-permute-start.2) | collective-permute-done | bytes 61472 | tf_op jit(solution)/shard_map/ppermute | solution.py:368
  63.0 2.1 %collective-permute-done.1.refs_2_ = bf16[240,128]{1,0:T(8,128)(2,1)S(1)} collective-permute-done((bf16[240,128]{1,0:T(8,128)(2,1)S(1)}, bf16[240,128]{1,0:T(8,128)(2,1)S(1)}, u32[]{:S(2)}, u32[]{:S(2)}) %collective-permute-start.1) | collective-permute-done | bytes 61472 | tf_op jit(solution)/shard_map/ppermute | solution.py:368
  65.1 0.1 collective-permute-done.refs_1_
  65.2 1.1 %gradients_out.1 = (f32[400,2,36]{2,1,0:T(2,128)}, f32[20,20]{1,0:T(8,128)}) custom-call(bf16[240,128]{1,0:T(8,128)(2,1)S(1)} %mode_grads.1.refs_0_, bf16[240,128]{1,0:T(8,128)(2,1)S(1)} %collective-permute-done.refs_1_, bf16[240,128]{1,0:T(8,128)(2,1)S(1)} %collective-permute-done.1.refs_2_, bf16[240,128]{1,0:T(8,128)(2,1)S(1)} %collective-permute-done.2.refs_3_), custom_call_target="tpu_custom_call" | custom-call | tf_op jit(solution)/shard_map/gradients_out/pallas_call | solution.py:467
  (6 shorter events, 0.0 us)
Async XLA Ops:
  0.6 21.0 %copy-start.2 = (bf16[144,512]{1,0:T(8,128)(2,1)S(1)}, bf16[144,512]{1,0:T(8,128)(2,1)}, u32[]{:S(2)}) copy-start(bf16[144,512]{1,0:T(8,128)(2,1)} %constant.26.clone.pairs_ref) | copy-start | bytes 442372
  0.6 21.0 %copy-start.4 = (bf16[36,2,20,20]{0,1,3,2:T(2,128)(2,1)S(1)}, bf16[36,2,20,20]{0,1,3,2:T(2,128)(2,1)}, u32[]{:S(2)}) copy-start(bf16[36,2,20,20]{0,1,3,2:T(2,128)(2,1)} %param.13) | copy-start | bytes 172804
  0.7 21.0 %copy-start.5 = (bf16[72,512]{1,0:T(8,128)(2,1)S(1)}, bf16[72,512]{1,0:T(8,128)(2,1)}, u32[]{:S(2)}) copy-start(bf16[72,512]{1,0:T(8,128)(2,1)} %constant.25.clone.collect_ref) | copy-start | bytes 221188
  0.7 21.0 %copy-start.6 = (bf16[2,36,256]{2,1,0:T(8,128)(2,1)S(1)}, bf16[2,36,256]{2,1,0:T(8,128)(2,1)}, u32[]{:S(2)}) copy-start(bf16[2,36,256]{2,1,0:T(8,128)(2,1)} %constant.24.clone.wsel_ref) | copy-start | bytes 110596
  21.7 12.0 %copy-start = (bf16[640,2048]{1,0:T(8,128)(2,1)S(1)}, bf16[640,2048]{1,0:T(8,128)(2,1)}, u32[]{:S(2)}) copy-start(bf16[640,2048]{1,0:T(8,128)(2,1)} %get-tuple-element.15.f_ref) | copy-start | bytes 7864324
  21.7 12.0 %copy-start.7 = (bf16[20,20]{1,0:T(8,128)(2,1)S(1)}, bf16[20,20]{1,0:T(8,128)(2,1)}, u32[]{:S(2)}) copy-start(bf16[20,20]{1,0:T(8,128)(2,1)} %mix_ref.1) | copy-start | bytes 2404
  33.7 20.4 %copy-start.1 = (bf16[768,640]{1,0:T(8,128)(2,1)S(1)}, bf16[768,640]{1,0:T(8,128)(2,1)}, u32[]{:S(2)}) copy-start(bf16[768,640]{1,0:T(8,128)(2,1)} %constant.28.clone.order_ref) | copy-start | bytes 2949124
  33.7 20.4 %copy-start.3 = (bf16[512,256]{1,0:T(8,128)(2,1)S(1)}, bf16[512,256]{1,0:T(8,128)(2,1)}, u32[]{:S(2)}) copy-start(bf16[512,256]{1,0:T(8,128)(2,1)} %constant.27.clone.fold_ref) | copy-start | bytes 786436
  56.3 6.8 %collective-permute-start.2 = (bf16[240,128]{1,0:T(8,128)(2,1)S(1)}, bf16[240,128]{1,0:T(8,128)(2,1)S(1)}, u32[]{:S(2)}, u32[]{:S(2)}) collective-permute-start(bf16[240,128]{1,0:T(8,128)(2,1)S(1)} %mode_grads.1.refs_0_), channel_id=1, source_target_pairs={{0,24},{8,16},{16,8},{24,0},{1,25},{9,17},{17,9},{25,1},{2,26},{10... | collective-permute-start | bytes 184328 | tf_op jit(solution)/shard_map/ppermute | solution.py:368
  59.9 5.2 %collective-permute-start.1 = (bf16[240,128]{1,0:T(8,128)(2,1)S(1)}, bf16[240,128]{1,0:T(8,128)(2,1)S(1)}, u32[]{:S(2)}, u32[]{:S(2)}) collective-permute-start(bf16[240,128]{1,0:T(8,128)(2,1)S(1)} %mode_grads.1.refs_0_), channel_id=1, source_target_pairs={{0,16},{8,24},{16,0},{24,8},{1,17},{9,25},{17,1},{25,9},{2,18},{10... | collective-permute-start | bytes 184328 | tf_op jit(solution)/shard_map/ppermute | solution.py:368
  59.9 5.2 %collective-permute-start = (bf16[240,128]{1,0:T(8,128)(2,1)S(1)}, bf16[240,128]{1,0:T(8,128)(2,1)S(1)}, u32[]{:S(2)}, u32[]{:S(2)}) collective-permute-start(bf16[240,128]{1,0:T(8,128)(2,1)S(1)} %mode_grads.1.refs_0_), channel_id=1, source_target_pairs={{0,8},{8,0},{16,24},{24,16},{1,9},{9,1},{17,25},{25,17},{2,10},{10... | collective-permute-start | bytes 184328 | tf_op jit(solution)/shard_map/ppermute | solution.py:368

commit v8 on v7

--- a/solution.py
+++ b/solution.py
@@ -91,6 +91,15 @@
     return lax.dot_general(a, b, (((ca,), (cb,)), ((), ())), preferred_element_type=F32)
 
 
+def squared(v):
+    return v * jnp.abs(v)
+
+
+def square_root(y):
+    y = y.astype(F32)
+    return y * lax.rsqrt(jnp.maximum(jnp.abs(y), 1e-36))
+
+
 def encode(v):
     return ((v * jnp.abs(v)) * (v * v)).astype(BF)
 
@@ -143,7 +152,7 @@
             acc_ref[...] += part
     sent = acc_ref[...] + part if parts > 1 else part
     for g in range(groups):
-        o_ref[g] = encode(sent[g * rows : (g + 1) * rows, :])
+        o_ref[g] = squared(sent[g * rows : (g + 1) * rows, :]).astype(BF)
 
 
 def same_plane(n):
@@ -184,9 +193,9 @@
 ):
     cot_copy = pltpu.make_async_copy(cot_hbm, cot_ref, sem.at[0])
     cot_copy.start()
-    total = decode(r_ref[0])
+    total = square_root(r_ref[0])
     for g in range(1, groups):
-        total = total + decode(r_ref[g])
+        total = total + square_root(r_ref[g])
     total = total * (1.0 / (SCALE * math.sqrt(NX * NY)))
     hi, lo = split(total)
     both = jnp.concatenate([hi.astype(F32), lo.astype(F32)], 0).astype(BF)
@@ -277,7 +286,7 @@
     extra = y[0:8] + pltpu.roll(y[8:16], C, 1) + pltpu.roll(y[16:24], 2 * C, 1)
     for g in range(groups):
         v = spectrum[g * rows : (g + 1) * rows, :]
-        coded = (v * jnp.abs(v)) * (v * v)
+        coded = squared(v)
         tiles = [coded[:, 128 * i : 128 * (i + 1)] for i in range(CP // 128)]
         o_ref[g] = jnp.concatenate(tiles + [extra], 0).astype(BF)
     for copy in out:
@@ -292,7 +301,7 @@
     extra = None
     for g in range(groups):
         block = r_ref[g].astype(F32)
-        y = root(block[0:high])
+        y = square_root(block[0:high])
         total = y if total is None else total + y
         x = block[high : high + 8]
         extra = x if extra is None else extra + x

time: 66.6 us -> 66.3 us (level)
  no operation moved by 1% of the time
where the time goes in v8:
time: 66.3 us; the launch traced here: 66.1 us
  blocking collectives  40.5 us (61%)
  Pallas kernels  15.8 us (24%)
  waiting for transfers between devices  4.47 us (7%)
  starting transfers between devices  4.45 us (7%)
  between operations  0.73 us (1%)
    all_to_all x2, blocking collectives, local(): got = lax.all_to_all(sent, GROUP, 0, 0, tiled=True)  30.5 us
    all_gather x1, blocking collectives, local(): all_vals = lax.all_gather(vals, GROUP, axis=0, tiled=True)  10.1 us
    pallas_call x1, Pallas kernels, local(): pl.pallas_call(functools.partial(main_kernel, groups, rows, 1), in_specs=...  6.22 us
    pallas_call x1, Pallas kernels, local(): pl.pallas_call(functools.partial(first_kernel, groups, rows, halves), in_...  4.56 us
    ppermute x3, waiting for transfers between devices, sum_over_dp(): lax.ppermute(coded, 'dp', [(i, i ^ k) for i in range(samples)])  4.47 us
    ppermute x3, starting transfers between devices, sum_over_dp(): lax.ppermute(coded, 'dp', [(i, i ^ k) for i in range(samples)])  4.45 us
    pallas_call x1, Pallas kernels, local(): pl.pallas_call(functools.partial(grad_kernel, groups, rows, per), out_sha...  2.02 us
    pallas_call x1, Pallas kernels, local(): pl.pallas_call(functools.partial(mix_kernel, groups, rows, per), in_specs...  1.9 us
  transfers between devices with their start and end apart: 3, of which 3 were waited for; matrix products, arithmetic and copies ran while one was open for 0% of the time, Pallas kernels for 0%

profile of v8, /device:TPU:0, one launch (start us, length us, event | category | flops | bytes accessed | tf_op | source)
XLA Modules:
  0.0 66.1 jit_solution(17629152087957603626)
XLA Ops:
  0.6 0.0 copy-start.2
  0.6 0.0 copy-start.4
  0.7 0.0 copy-start.5
  0.7 0.0 copy-start.6
  0.7 4.6 %spectrum_parts.1 = (bf16[8,72,640]{2,1,0:T(8,128)(2,1)S(1)}, bf16[640,2048]{1,0:T(8,128)(2,1)}, bf16[576,2048]{1,0:T(8,128)(2,1)S(1)}) custom-call(s32[1]{0:T(128)} %bitcast.gid_ref, bf16[640,2048]{1,0:T(8,128)(2,1)} %bitcast.11, bf16[8,576,2048]{2,1,0:T(8,128)(2,1)} %constant.23.clone.t_hbm), custom_call_target="tpu_custom_call" | custom-call | tf_op jit(solution)/shard_map/spectrum_parts/pallas_call | solution.py:408
  5.3 16.4 %all_to_all.10.r_ref = bf16[8,72,640]{2,1,0:T(8,128)(2,1)S(1)} all-to-all(bf16[8,72,640]{2,1,0:T(8,128)(2,1)S(1)} %get-tuple-element.16), channel_id=1, replica_groups=mesh['dp'=4,'gx'=2,'gy'=4] {'gx','gy'}, dimensions={0} | all-to-all | bytes 1474560 | tf_op jit(solution)/shard_map/all_to_all | solution.py:424
  21.7 0.0 copy-done.2
  21.7 0.0 copy-done.4
  21.7 0.0 copy-done.5
  21.7 0.0 copy-done.6
  21.7 1.9 %mode_mixing.1 = (bf16[72,640]{1,0:T(8,128)(2,1)S(1)}, f32[640,128]{1,0:T(8,128)S(1)}, f32[160,128]{1,0:T(8,128)S(1)}, bf16[640,2048]{1,0:T(8,128)(2,1)S(1)}) custom-call(bf16[640,2048]{1,0:T(8,128)(2,1)} %bitcast.12, bf16[8,72,640]{2,1,0:T(8,128)(2,1)S(1)} %all_to_all.10.r_ref, bf16[400,2,36]{2,1,0:T(2,128)(2,1)S(1)} %bitcast.10, ...), custom_call_target="tpu_custom_call" | custom-call | tf_op jit(solution)/shard_map/mode_mixing/pallas_call | solution.py:427
  23.6 10.1 %all_gather.3.v_ref = bf16[576,640]{1,0:T(8,128)(2,1)S(1)} all-gather(bf16[72,640]{1,0:T(8,128)(2,1)S(1)} %get-tuple-element.18), channel_id=1, replica_groups=mesh['dp'=4,'gx'=2,'gy'=4] {'gx','gy'}, dimensions={0}, use_global_device_ids=true | all-gather | bytes 829440 | tf_op jit(solution)/shard_map/all_gather | solution.py:446
  33.7 0.0 copy-done
  33.7 0.0 copy-done.7
  33.7 6.2 %cells.1 = (bf16[640,2048]{1,0:T(8,128)(2,1)}, bf16[8,368,128]{2,1,0:T(8,128)(2,1)S(1)}) custom-call(bf16[576,2048]{1,0:T(8,128)(2,1)S(1)} %get-tuple-element.14.t_ref, bf16[640,2048]{1,0:T(8,128)(2,1)S(1)} %copy-done, bf16[640,2048]{1,0:T(8,128)(2,1)S(1)} %get-tuple-element.17.cot_ref, bf16[576,640]{1,0:T(8,128)(2,1)S(1)} %all_gather.3.v_ref, ...), custom_call_target="tpu_custom_call" | custom-call | tf_op jit(solution)/shard_map/cells/pallas_call | solution.py:448
  39.9 14.1 %all_to_all.11.r_ref = bf16[8,368,128]{2,1,0:T(8,128)(2,1)S(1)} all-to-all(bf16[8,368,128]{2,1,0:T(8,128)(2,1)S(1)} %get-tuple-element.20), channel_id=1, replica_groups=mesh['dp'=4,'gx'=2,'gy'=4] {'gx','gy'}, dimensions={0} | all-to-all | bytes 1507328 | tf_op jit(solution)/shard_map/all_to_all | solution.py:466
  54.0 2.0 %mode_grads.1.refs_0_ = bf16[240,128]{1,0:T(8,128)(2,1)S(1)} custom-call(bf16[8,368,128]{2,1,0:T(8,128)(2,1)S(1)} %all_to_all.11.r_ref, f32[640,128]{1,0:T(8,128)S(1)} %get-tuple-element.21.s_ref, f32[160,128]{1,0:T(8,128)S(1)} %get-tuple-element.22.s_rest_ref, bf16[144,512]{1,0:T(8,128)(2,1)S(1)} %copy-done.2, bf16[512,256]{1,0:T(8,128)(2,1)S(1)} %copy-done.3, ...), custom_call_target="tpu_custom_call" | custom-call | tf_op jit(solution)/shard_map/mode_grads/pallas_call | solution.py:468
  56.0 3.7 %collective-permute-start.2 = (bf16[240,128]{1,0:T(8,128)(2,1)S(1)}, bf16[240,128]{1,0:T(8,128)(2,1)S(1)}, u32[]{:S(2)}, u32[]{:S(2)}) collective-permute-start(bf16[240,128]{1,0:T(8,128)(2,1)S(1)} %mode_grads.1.refs_0_), channel_id=1, source_target_pairs={{0,24},{8,16},{16,8},{24,0},{1,25},{9,17},{17,9},{25,1},{2,26},{10... | collective-permute-start | bytes 184328 | tf_op jit(solution)/shard_map/ppermute | solution.py:377
  59.7 0.0 collective-permute-start.1
  59.7 0.8 %collective-permute-start = (bf16[240,128]{1,0:T(8,128)(2,1)S(1)}, bf16[240,128]{1,0:T(8,128)(2,1)S(1)}, u32[]{:S(2)}, u32[]{:S(2)}) collective-permute-start(bf16[240,128]{1,0:T(8,128)(2,1)S(1)} %mode_grads.1.refs_0_), channel_id=1, source_target_pairs={{0,8},{8,0},{16,24},{24,16},{1,9},{9,1},{17,25},{25,17},{2,10},{10... | collective-permute-start | bytes 184328 | tf_op jit(solution)/shard_map/ppermute | solution.py:377
  60.5 2.3 %collective-permute-done.2.refs_3_ = bf16[240,128]{1,0:T(8,128)(2,1)S(1)} collective-permute-done((bf16[240,128]{1,0:T(8,128)(2,1)S(1)}, bf16[240,128]{1,0:T(8,128)(2,1)S(1)}, u32[]{:S(2)}, u32[]{:S(2)}) %collective-permute-start.2) | collective-permute-done | bytes 61472 | tf_op jit(solution)/shard_map/ppermute | solution.py:377
  62.8 2.1 %collective-permute-done.1.refs_2_ = bf16[240,128]{1,0:T(8,128)(2,1)S(1)} collective-permute-done((bf16[240,128]{1,0:T(8,128)(2,1)S(1)}, bf16[240,128]{1,0:T(8,128)(2,1)S(1)}, u32[]{:S(2)}, u32[]{:S(2)}) %collective-permute-start.1) | collective-permute-done | bytes 61472 | tf_op jit(solution)/shard_map/ppermute | solution.py:377
  64.9 0.1 collective-permute-done.refs_1_
  64.9 1.1 %gradients_out.1 = (f32[400,2,36]{2,1,0:T(2,128)}, f32[20,20]{1,0:T(8,128)}) custom-call(bf16[240,128]{1,0:T(8,128)(2,1)S(1)} %mode_grads.1.refs_0_, bf16[240,128]{1,0:T(8,128)(2,1)S(1)} %collective-permute-done.refs_1_, bf16[240,128]{1,0:T(8,128)(2,1)S(1)} %collective-permute-done.1.refs_2_, bf16[240,128]{1,0:T(8,128)(2,1)S(1)} %collective-permute-done.2.refs_3_), custom_call_target="tpu_custom_call" | custom-call | tf_op jit(solution)/shard_map/gradients_out/pallas_call | solution.py:476
  (6 shorter events, 0.0 us)
Async XLA Ops:
  0.6 21.0 %copy-start.2 = (bf16[144,512]{1,0:T(8,128)(2,1)S(1)}, bf16[144,512]{1,0:T(8,128)(2,1)}, u32[]{:S(2)}) copy-start(bf16[144,512]{1,0:T(8,128)(2,1)} %constant.26.clone.pairs_ref) | copy-start | bytes 442372
  0.6 21.0 %copy-start.4 = (bf16[36,2,20,20]{0,1,3,2:T(2,128)(2,1)S(1)}, bf16[36,2,20,20]{0,1,3,2:T(2,128)(2,1)}, u32[]{:S(2)}) copy-start(bf16[36,2,20,20]{0,1,3,2:T(2,128)(2,1)} %param.13) | copy-start | bytes 172804
  0.7 21.0 %copy-start.5 = (bf16[72,512]{1,0:T(8,128)(2,1)S(1)}, bf16[72,512]{1,0:T(8,128)(2,1)}, u32[]{:S(2)}) copy-start(bf16[72,512]{1,0:T(8,128)(2,1)} %constant.25.clone.collect_ref) | copy-start | bytes 221188
  0.7 21.0 %copy-start.6 = (bf16[2,36,256]{2,1,0:T(8,128)(2,1)S(1)}, bf16[2,36,256]{2,1,0:T(8,128)(2,1)}, u32[]{:S(2)}) copy-start(bf16[2,36,256]{2,1,0:T(8,128)(2,1)} %constant.24.clone.wsel_ref) | copy-start | bytes 110596
  21.7 12.0 %copy-start = (bf16[640,2048]{1,0:T(8,128)(2,1)S(1)}, bf16[640,2048]{1,0:T(8,128)(2,1)}, u32[]{:S(2)}) copy-start(bf16[640,2048]{1,0:T(8,128)(2,1)} %get-tuple-element.15.f_ref) | copy-start | bytes 7864324
  21.7 12.0 %copy-start.7 = (bf16[20,20]{1,0:T(8,128)(2,1)S(1)}, bf16[20,20]{1,0:T(8,128)(2,1)}, u32[]{:S(2)}) copy-start(bf16[20,20]{1,0:T(8,128)(2,1)} %mix_ref.1) | copy-start | bytes 2404
  33.7 20.3 %copy-start.1 = (bf16[768,640]{1,0:T(8,128)(2,1)S(1)}, bf16[768,640]{1,0:T(8,128)(2,1)}, u32[]{:S(2)}) copy-start(bf16[768,640]{1,0:T(8,128)(2,1)} %constant.28.clone.order_ref) | copy-start | bytes 2949124
  33.7 20.3 %copy-start.3 = (bf16[512,256]{1,0:T(8,128)(2,1)S(1)}, bf16[512,256]{1,0:T(8,128)(2,1)}, u32[]{:S(2)}) copy-start(bf16[512,256]{1,0:T(8,128)(2,1)} %constant.27.clone.fold_ref) | copy-start | bytes 786436
  56.0 6.8 %collective-permute-start.2 = (bf16[240,128]{1,0:T(8,128)(2,1)S(1)}, bf16[240,128]{1,0:T(8,128)(2,1)S(1)}, u32[]{:S(2)}, u32[]{:S(2)}) collective-permute-start(bf16[240,128]{1,0:T(8,128)(2,1)S(1)} %mode_grads.1.refs_0_), channel_id=1, source_target_pairs={{0,24},{8,16},{16,8},{24,0},{1,25},{9,17},{17,9},{25,1},{2,26},{10... | collective-permute-start | bytes 184328 | tf_op jit(solution)/shard_map/ppermute | solution.py:377
  59.7 5.2 %collective-permute-start.1 = (bf16[240,128]{1,0:T(8,128)(2,1)S(1)}, bf16[240,128]{1,0:T(8,128)(2,1)S(1)}, u32[]{:S(2)}, u32[]{:S(2)}) collective-permute-start(bf16[240,128]{1,0:T(8,128)(2,1)S(1)} %mode_grads.1.refs_0_), channel_id=1, source_target_pairs={{0,16},{8,24},{16,0},{24,8},{1,17},{9,25},{17,1},{25,9},{2,18},{10... | collective-permute-start | bytes 184328 | tf_op jit(solution)/shard_map/ppermute | solution.py:377
  59.7 5.2 %collective-permute-start = (bf16[240,128]{1,0:T(8,128)(2,1)S(1)}, bf16[240,128]{1,0:T(8,128)(2,1)S(1)}, u32[]{:S(2)}, u32[]{:S(2)}) collective-permute-start(bf16[240,128]{1,0:T(8,128)(2,1)S(1)} %mode_grads.1.refs_0_), channel_id=1, source_target_pairs={{0,8},{8,0},{16,24},{24,16},{1,9},{9,1},{17,25},{25,17},{2,10},{10... | collective-permute-start | bytes 184328 | tf_op jit(solution)/shard_map/ppermute | solution.py:377
